TPU v7x, 32 devices: a whole 2x2x4 slice. The times are simulated.
32 devices in a mesh: group: 2 (over y), inner: 4 (over z), outer: 2 (over x), cuts: 2 (over core).
Axes of the slice: x: 2, y: 2, z: 4, core: 2. Of those that a mesh axis runs over, the one named last changes fastest.
Arguments:
- volume: bfloat16 [96, 128, 256], P(('group', 'inner', 'outer'), None, 'cuts'), parts along dimension 0, may hold values from -6 to 6
- projector: bfloat16 [256, 4, 128, 128], P(('inner', 'outer')), may hold values from 0.19921875 to 1
- slot_ray: int32 [256], P(('inner', 'outer')), may hold values from 0 to 63, as said below
- slot_pixel: int32 [256, 4], P(('inner', 'outer')), may hold values from 0 to 5, as said below
- sinogram: bfloat16 [128, 128, 256], P(('group', 'inner', 'outer'), None, 'cuts'), parts along dimension 0, may hold values from -240 to 240
- weight_index: int32 [128, 128], P(('group', 'inner', 'outer')), parts along dimension 0, may hold values from 0 to 15
- weight_table: bfloat16 [16], replicated, may hold values from 0.099609375 to 1
Outputs:
- updated: float32 [96, 128, 256], P(('group', 'inner', 'outer'), None, 'cuts'), parts along dimension 0
There are 2 independent parts, one for each index of `group`. A program takes and returns all parts, laid end to end along the dimension named above; an argument that names none is the same for every part. Nothing has to cross between parts.
Inputs may be any that keep to these rules, and one draw needn't show every extreme that they name: `slot_ray`: each patch lists 32 ray tiles, possibly some more than once. At most 16 of one patch's slots name ray tiles of one band k * 16 to (k + 1) * 16 - 1, and in every draw some band receives exactly 16 slots from every patch. `slot_pixel`: the 4 entries of a slot are different pixel tiles of its own patch; every pixel tile of a patch is named by some slot of that patch.
All inputs are finite; a program needn't handle non-finite values.
Results may differ from a plain program's by a relative error of at most 0.0003.
Values may be sent and summed in bfloat16 or wider, within the bound.
No kernel may reach another device: no remote copies, remote signals or barrier semaphores. Data moves between devices by JAX's collectives and lax.ppermute only.
A program may use at most 64 MiB of HBM per device.

v0:
```python
import jax
import jax.numpy as jnp
from jax import lax
from jax.sharding import PartitionSpec as P


def on_device(volume, projector, slot_ray, slot_pixel, sinogram, weight_index, weight_table):
    inners = lax.axis_size("inner")
    outers = lax.axis_size("outer")
    slot_count = projector.shape[0]
    per_slot = projector.shape[1]
    tile_rows = projector.shape[2]
    tile_cols = projector.shape[3]
    patch_tiles = volume.shape[0]
    slice_count = volume.shape[2]
    owned_rows = sinogram.shape[0]
    band_rows = owned_rows * outers
    capacity = 2 * slot_count // inners
    cell_count = inners * capacity
    target = slot_ray // band_rows
    offset = slot_ray % band_rows
    same_target = target[:, None] == target[None, :]
    earlier = jnp.arange(slot_count)[:, None] > jnp.arange(slot_count)[None, :]
    slot_rank = jnp.sum(jnp.logical_and(same_target, earlier), axis=1)
    position = target * capacity + slot_rank
    partial_value = jnp.zeros((slot_count, tile_rows, slice_count), jnp.float32)
    for column in range(per_slot):
        pixels = volume[slot_pixel[:, column]]
        partial_value = partial_value + jnp.einsum(
            "srp,spc->src", projector[:, column], pixels, preferred_element_type=jnp.float32
        )
    outgoing = (
        jnp.zeros((cell_count, tile_rows, slice_count), jnp.float32).at[position].set(partial_value)
    )
    labels = jnp.full((cell_count,), -1.0, jnp.float32).at[position].set(offset.astype(jnp.float32))
    arrived, arrived_rows = (
        lax.all_to_all(
            outgoing.reshape(inners, capacity, tile_rows, slice_count),
            "inner",
            split_axis=0,
            concat_axis=0,
            tiled=True,
        ),
        lax.all_to_all(
            labels.reshape(inners, capacity), "inner", split_axis=0, concat_axis=0, tiled=True
        ),
    )
    selector = (
        jnp.arange(band_rows, dtype=jnp.float32)[:, None] == arrived_rows.reshape(1, cell_count)
    ).astype(jnp.float32)
    block_sums = jnp.dot(
        selector,
        arrived.reshape(cell_count, tile_rows * slice_count),
        precision=lax.Precision.HIGHEST,
    ).reshape(band_rows, tile_rows, slice_count)
    classes = weight_table.shape[0]
    lookup = weight_index[:, :, None] == jnp.arange(classes)[None, None, :]
    weights = jnp.sum(
        jnp.where(lookup, weight_table[None, None, :], jnp.zeros((), weight_table.dtype)), axis=2
    )
    own_sums = lax.psum_scatter(block_sums, "outer", scatter_dimension=0, tiled=True)
    own_residual = (
        weights.astype(jnp.float32)[:, :, None] * (sinogram.astype(jnp.float32) - own_sums)
    ).astype(jnp.bfloat16)
    residual = lax.all_gather(own_residual, "outer", axis=0, tiled=True)
    picked = jnp.dot(
        selector.T.astype(jnp.bfloat16),
        residual.reshape(band_rows, tile_rows * slice_count),
        preferred_element_type=jnp.float32,
    ).astype(jnp.bfloat16)
    returned = lax.all_to_all(
        picked.reshape(inners, capacity, tile_rows, slice_count),
        "inner",
        split_axis=0,
        concat_axis=0,
        tiled=True,
    )
    slot_residual = returned.reshape(cell_count, tile_rows, slice_count)[position]
    owners = jnp.arange(patch_tiles)
    backward = jnp.zeros((patch_tiles, tile_cols, slice_count), jnp.float32)
    column_sum = jnp.zeros((patch_tiles, tile_cols), jnp.float32)
    for column in range(per_slot):
        member = (owners[:, None] == slot_pixel[None, :, column]).astype(jnp.float32)
        spread = jnp.einsum(
            "srp,src->spc", projector[:, column], slot_residual, preferred_element_type=jnp.float32
        )
        backward = backward + jnp.einsum(
            "ts,spc->tpc", member, spread, precision=lax.Precision.HIGHEST
        )
        column_sum = column_sum + jnp.dot(
            member,
            jnp.sum(projector[:, column], axis=1, dtype=jnp.float32),
            precision=lax.Precision.HIGHEST,
        )
    return volume.astype(jnp.float32) + backward / column_sum[:, :, None]


def solution(mesh):
    in_specs = (
        P(("group", "inner", "outer"), None, "cuts"),
        P(("inner", "outer"), None, None, None),
        P(("inner", "outer")),
        P(("inner", "outer"), None),
        P(("group", "inner", "outer"), None, "cuts"),
        P(("group", "inner", "outer"), None),
        P(),
    )
    out_specs = P(("group", "inner", "outer"), None, "cuts")
    return jax.shard_map(
        on_device, mesh=mesh, in_specs=in_specs, out_specs=out_specs, check_vma=False
    )
```

profile of v0, /device:TPU:0, one launch (start us, length us, event | category | flops | bytes accessed | tf_op | source)
XLA Modules:
  0.0 267.7 jit_solution(11891685682074695904)
XLA Ops:
  6.5 0.7 fusion.52
  7.2 0.2 convert_reduce_fusion.4
  7.4 0.7 scatter_custom_fusion
  8.1 0.7 all_to_all.12
  8.8 6.3 %all-to-all-start = ((f32[4,1,16]{2,1,0:T(1,128)}), f32[4,1,16]{2,1,0:T(1,128)S(1)}, u32[]{:S(2)}, u32[]{:S(2)}) async-start(f32[4,1,16]{2,1,0:T(1,128)} %bitcast.2), calls=%async_computation | async-start | bytes 4096 | tf_op jit(solution)/shard_map/all_to_all | solution.py:44
  15.1 0.8 slice_bitcast_fusion
  15.9 1.7 gather_fusion.1
  17.6 0.0 copy-done
  17.6 1.7 gather_fusion
  19.3 2.2 fusion.12
  21.5 0.0 copy-done.3
  21.5 3.4 %fusion.15 = f32[32,128,128]{2,1,0:T(8,128)} fusion(bf16[32,128,128]{2,1,0:T(8,128)(2,1)S(1)} %copy-done.3, bf16[32,4,128,128]{3,2,1,0:T(8,128)(2,1)} %param.8), kind=kOutput, calls=%fused_computation.39 | convolution fusion | flops 134217728 | bytes 4194304 | tf_op jit(solution)/shard_map/srp,spc->src/dot_general | solution.py:29
  24.9 0.7 gather_fusion.2
  25.7 3.5 %fusion.9 = f32[32,128,128]{2,1,0:T(8,128)} fusion(bf16[32,128,128]{2,1,0:T(8,128)(2,1)S(1)} %gather_fusion.2, bf16[32,4,128,128]{3,2,1,0:T(8,128)(2,1)} %param.8), kind=kOutput, calls=%fused_computation.33 | convolution fusion | flops 134217728 | bytes 4194304 | tf_op jit(solution)/shard_map/srp,spc->src/dot_general | solution.py:29
  29.1 0.7 gather_fusion.3
  29.9 4.8 %add_bitcast_fusion = f32[32,128,128]{1,2,0:T(8,128)} fusion(f32[32,128,128]{2,1,0:T(8,128)} %fusion.9, f32[32,128,128]{2,1,0:T(8,128)} %fusion.15, f32[32,128,128]{2,1,0:T(8,128)S(1)} %fusion.12, bf16[32,128,128]{2,1,0:T(8,128)(2,1)S(1)} %gather_fusion.3, bf16[32,4,128,128]{3,2,1,0:T(8,128)(2,1)} %param.8), kind=kOutput, calls=%fused_computation.16 | convolution fusion | flops 135790592 | bytes 10485760 | tf_op jit(solution)/shard_map/srp,spc->src/dot_general | solution.py:29
  34.7 1.9 copy.92
  36.6 2.4 broadcast_in_dim.18
  39.1 5.4 %scatter_fusion = f32[64,128,128]{2,1,0:T(8,128)} fusion(f32[64,128,128]{2,1,0:T(8,128)} %broadcast_in_dim.18, s32[32]{0:T(128)S(1)} %compare_select_fusion.4, f32[32,128,128]{2,1,0:T(8,128)S(1)} %copy.92), kind=kCustom, calls=%fused_computation.6 | custom fusion | bytes 6291584 | tf_op jit(solution)/shard_map/scatter | solution.py:33
  44.5 0.0 all-to-all-done
  44.5 5.1 %all-to-all-start.1 = ((f32[4,16,128,128]{3,2,1,0:T(8,128)}), f32[4,16,128,128]{3,2,1,0:T(8,128)}, u32[]{:S(2)}, u32[]{:S(2)}) async-start(f32[4,16,128,128]{3,2,1,0:T(8,128)} %bitcast.117), calls=%async_computation.1 | async-start | bytes 8388608 | tf_op jit(solution)/shard_map/all_to_all | solution.py:37
  49.6 0.0 reduce-scatter.2.cloned.1.call-start
  49.6 0.5 broadcast.77
  50.1 0.7 reduce.4
  50.8 0.1 eq.118
  50.8 91.7 %all-to-all-done.1 = f32[4,16,128,128]{3,2,1,0:T(8,128)} async-done(((f32[4,16,128,128]{3,2,1,0:T(8,128)}), f32[4,16,128,128]{3,2,1,0:T(8,128)}, u32[]{:S(2)}, u32[]{:S(2)}) %all-to-all-start.1) | async-done | bytes 4194336 | tf_op jit(solution)/shard_map/all_to_all | solution.py:37
  142.6 6.8 %fusion = f32[16,128,128]{2,0,1:T(8,128)} fusion(f32[64]{0:T(128)S(1)} %eq.118, f32[8,8,128,128]{3,2,1,0:T(8,128)} %bitcast.39), kind=kOutput, calls=%fused_computation.9 | convolution fusion | flops 201327616 | bytes 5243136 | tf_op jit(solution)/shard_map/dot_general | solution.py:51
  149.4 0.0 reduce-scatter.2.cloned.1.call-update
  149.4 0.0 copy-done.6
  149.4 0.0 copy-done.7
  149.4 0.1 fusion.28
  149.5 0.1 copy.82
  149.6 19.3 %reduce-scatter.2.cloned.1.call-done = f32[8,128,128]{2,0,1:T(8,128)} async-done(((f32[16,128,128]{2,0,1:T(8,128)}), f32[8,128,128]{2,0,1:T(8,128)}) %reduce-scatter.2.cloned.1.call-update) | async-done | bytes 524304 | tf_op jit(solution)/shard_map/reduce_scatter | solution.py:61
  169.0 0.0 copy-done.5
  169.0 1.3 multiply_convert_fusion
  170.3 8.7 %all_gather.3 = bf16[16,128,128]{2,0,1:T(8,128)(2,1)S(1)} all-gather(bf16[8,128,128]{2,0,1:T(8,128)(2,1)S(1)} %multiply_convert_fusion), channel_id=1, replica_groups=mesh['group'=2,'inner'=4,'outer'=2,'cuts'=2] {'outer'}, dimensions={0}, use_global_device_ids=true | all-gather | bytes 786432 | tf_op jit(solution)/shard_map/all_gather | solution.py:65
  179.0 0.7 fusion.3
  179.7 1.9 copy.120
  181.7 4.6 %all-to-all-start.2 = ((bf16[4,16,128,128]{3,2,1,0:T(8,128)(2,1)}), bf16[4,16,128,128]{3,2,1,0:T(8,128)(2,1)S(1)}, u32[]{:S(2)}, u32[]{:S(2)}) async-start(bf16[4,16,128,128]{3,2,1,0:T(8,128)(2,1)} %bitcast.43), calls=%async_computation.3 | async-start | bytes 4194304 | tf_op jit(solution)/shard_map/all_to_all | solution.py:71
  186.3 3.4 %convert_reduce_fusion = (f32[32,128]{1,0:T(8,128)S(1)}, f32[32,128]{1,0:T(8,128)S(1)}, f32[32,128]{1,0:T(8,128)S(1)}, f32[32,128]{1,0:T(8,128)S(1)}) fusion(bf16[32,4,128,128]{3,2,1,0:T(8,128)(2,1)} %param.8), kind=kLoop, calls=%fused_computation.12 | loop fusion | flops 4177920 | bytes 4259840 | tf_op jit(solution)/shard_map/reduce_sum | solution.py:92
  189.6 0.1 fusion.37
  189.7 0.1 convolution_add_fusion.5
  189.9 0.1 convolution_add_fusion.4
  190.0 0.1 convolution_add_fusion.3
  190.1 0.1 copy.103
  190.3 43.4 %all-to-all-done.2 = bf16[4,16,128,128]{3,2,1,0:T(8,128)(2,1)S(1)} async-done(((bf16[4,16,128,128]{3,2,1,0:T(8,128)(2,1)}), bf16[4,16,128,128]{3,2,1,0:T(8,128)(2,1)S(1)}, u32[]{:S(2)}, u32[]{:S(2)}) %all-to-all-start.2) | async-done | bytes 2097184 | tf_op jit(solution)/shard_map/all_to_all | solution.py:71
  233.7 0.7 gather_fusion.4
  234.4 0.0 copy-start.1
  234.5 3.2 %convolution_bitcast_fusion.3 = f32[32,128,128]{1,2,0:T(8,128)} fusion(bf16[32,128,128]{2,1,0:T(8,128)(2,1)S(1)} %gather_fusion.4, bf16[32,4,128,128]{3,2,1,0:T(8,128)(2,1)} %param.8), kind=kOutput, calls=%fused_computation.20 | convolution fusion | flops 134217728 | bytes 4194304 | tf_op jit(solution)/shard_map/srp,src->spc/dot_general | solution.py:84
  237.7 0.0 copy-done.1
  237.7 1.8 convolution_bitcast_fusion.2
  239.5 0.5 convolution_bitcast_fusion.1
  240.1 1.9 convolution_bitcast_fusion
  241.9 3.1 %copy.96 = f32[32,128,128]{2,0,1:T(8,128)} copy(f32[32,128,128]{1,2,0:T(8,128)} %convolution_bitcast_fusion.3) | data formatting | bytes 4194304 | tf_op jit(solution)/shard_map/srp,src->spc/dot_general | solution.py:84
  245.0 3.1 %fusion.39 = f32[6,128,128]{2,0,1:T(8,128)} fusion(f32[32,128,128]{2,0,1:T(8,128)} %copy.96, s32[32]{0:T(128)S(1)} %get-tuple-element.15), kind=kOutput, calls=%fused_computation.78 | convolution fusion | flops 37748928 | bytes 2490496 | tf_op jit(solution)/shard_map/ts,spc->tpc/dot_general | solution.py:87
  248.2 3.1 %copy.98 = f32[32,128,128]{2,0,1:T(8,128)} copy(f32[32,128,128]{1,2,0:T(8,128)} %convolution_bitcast_fusion.2) | data formatting | bytes 4194304 | tf_op jit(solution)/shard_map/srp,src->spc/dot_general | solution.py:84
  251.3 2.0 copy.100
  253.3 2.4 copy.102
  255.8 0.0 copy-done.4
  255.8 0.0 copy-start.2
  255.8 2.5 convolution_add_fusion.2
  258.3 0.8 convolution_add_fusion.1
  259.1 0.9 fusion.5
  260.0 0.8 copy.104
  (11 shorter events, 0.0 us)
Async XLA Ops:
  6.5 11.1 %copy-start = (bf16[6,128,128]{2,1,0:T(8,128)(2,1)S(1)}, bf16[6,128,128]{2,1,0:T(8,128)(2,1)}, u32[]{:S(2)}) copy-start(bf16[6,128,128]{2,1,0:T(8,128)(2,1)} %param.7) | copy-start | bytes 589828
  8.8 35.7 %all-to-all-start = ((f32[4,1,16]{2,1,0:T(1,128)}), f32[4,1,16]{2,1,0:T(1,128)S(1)}, u32[]{:S(2)}, u32[]{:S(2)}) async-start(f32[4,1,16]{2,1,0:T(1,128)} %bitcast.2), calls=%async_computation | async-start | bytes 4096 | tf_op jit(solution)/shard_map/all_to_all | solution.py:44
  19.3 2.2 copy-start.3
  44.5 98.1 %all-to-all-start.1 = ((f32[4,16,128,128]{3,2,1,0:T(8,128)}), f32[4,16,128,128]{3,2,1,0:T(8,128)}, u32[]{:S(2)}, u32[]{:S(2)}) async-start(f32[4,16,128,128]{3,2,1,0:T(8,128)} %bitcast.117), calls=%async_computation.1 | async-start | bytes 8388608 | tf_op jit(solution)/shard_map/all_to_all | solution.py:37
  49.6 119.4 %reduce-scatter.2.cloned.1.call-start = ((), (), s32[]{:S(2)}) async-start(), calls=%async_computation.4 | async-start | bytes 1572864 | tf_op jit(solution)/shard_map/reduce_scatter | solution.py:61
  142.6 6.9 %copy-start.6 = (s32[8,128]{1,0:T(8,128)S(1)}, s32[8,128]{1,0:T(8,128)}, u32[]{:S(2)}) copy-start(s32[8,128]{1,0:T(8,128)} %param.12) | copy-start | bytes 12292
  142.6 6.9 %copy-start.7 = (bf16[16]{0:T(256)(128)(2,1)S(1)}, bf16[16]{0:T(256)(128)(2,1)}, u32[]{:S(2)}) copy-start(bf16[16]{0:T(256)(128)(2,1)} %param.13) | copy-start | bytes 100
  142.6 26.4 %copy-start.5 = (bf16[8,128,128]{2,1,0:T(8,128)(2,1)S(1)}, bf16[8,128,128]{2,1,0:T(8,128)(2,1)}, u32[]{:S(2)}) copy-start(bf16[8,128,128]{2,1,0:T(8,128)(2,1)} %param.11) | copy-start | bytes 786436
  181.7 52.0 %all-to-all-start.2 = ((bf16[4,16,128,128]{3,2,1,0:T(8,128)(2,1)}), bf16[4,16,128,128]{3,2,1,0:T(8,128)(2,1)S(1)}, u32[]{:S(2)}, u32[]{:S(2)}) async-start(bf16[4,16,128,128]{3,2,1,0:T(8,128)(2,1)} %bitcast.43), calls=%async_computation.3 | async-start | bytes 4194304 | tf_op jit(solution)/shard_map/all_to_all | solution.py:71
  234.4 3.2 %copy-start.1 = (bf16[32,4,128,128]{3,2,1,0:T(8,128)(2,1)S(1)}, bf16[32,4,128,128]{3,2,1,0:T(8,128)(2,1)}, u32[]{:S(2)}) copy-start(bf16[32,4,128,128]{3,2,1,0:T(8,128)(2,1)} %param.8) | copy-start | bytes 12582916
  253.3 2.4 copy-start.4
  255.8 2.5 copy-start.2
Sparse Core Ops, SparseCore 0:
  149.5 19.3 reduce-scatter.1
where the time goes:
time: 269 us; the launch traced here: 268 us
  waiting for transfers between devices  154 us (57%)
  matrix products  36.8 us (14%)
  local copies, waits for them, and re-layouts  31 us (12%)
  starting transfers between devices  16 us (6%)
  between operations  13.6 us (5%)
  blocking collectives  8.74 us (3%)
  other arithmetic  7.14 us (3%)
    all_to_all x1, waiting for transfers between devices, on_device(): lax.all_to_all(outgoing.reshape(inners, capacity, tile_rows, slice_count)...  91.7 us
    all_to_all x1, waiting for transfers between devices, on_device(): lax.all_to_all(picked.reshape(inners, capacity, tile_rows, slice_count),...  43.4 us
    reduce_scatter x1, waiting for transfers between devices, on_device(): lax.psum_scatter(block_sums, 'outer', scatter_dimension=0, tiled=True)  19.3 us
    dot_general x4, matrix products, on_device(): jnp.einsum('srp,spc->src', projector[:, column], pixels, preferred_elemen...  13.9 us
    dot_general x4, local copies, waits for them, and re-layouts, on_device(): jnp.einsum('srp,src->spc', projector[:, column], slot_residual, preferred...  10.7 us
    all_gather x1, blocking collectives, on_device(): residual = lax.all_gather(own_residual, 'outer', axis=0, tiled=True)  8.74 us
    dot_general x4, matrix products, on_device(): jnp.einsum('srp,src->spc', projector[:, column], slot_residual, preferred...  7.47 us
    dot_general x4, matrix products, on_device(): jnp.einsum('ts,spc->tpc', member, spread, precision=lax.Precision.HIGHEST)  7.36 us
  transfers between devices with their start and end apart: 4, of which 3 were waited for; matrix products, arithmetic and copies ran while one was open for 13% of the time, Pallas kernels for 0%

commit v1 on v0

--- a/solution.py
+++ b/solution.py
@@ -1,10 +1,330 @@
+import functools
+import math
+
 import jax
 import jax.numpy as jnp
 from jax import lax
+from jax.experimental import pallas as pl
+from jax.experimental.pallas import tpu as pltpu
 from jax.sharding import PartitionSpec as P
 
-
-def on_device(volume, projector, slot_ray, slot_pixel, sinogram, weight_index, weight_table):
+FULL = 32700.0
+VMEM = pl.BlockSpec(memory_space=pltpu.VMEM)
+SMEM = pl.BlockSpec(memory_space=pltpu.SMEM)
+LIMIT = 40 * 2**20
+
+
+def round_up(value, step):
+    return -(-value // step) * step
+
+
+def swap(value, axis, bits):
+    size = lax.axis_size(axis)
+    return lax.ppermute(value, axis, [(i, i ^ bits) for i in range(size)])
+
+
+def pack(tile, out_ref, levels_ref, t):
+    rows = tile.shape[0]
+    top = jnp.maximum(jnp.max(jnp.abs(tile), axis=0, keepdims=True), 1e-30)
+    level = jnp.ceil(jnp.log2(top))
+    out_ref[pl.ds(pl.multiple_of(t * rows, rows), rows), :] = (
+        jnp.round(tile * (FULL * jnp.exp2(-level))).astype(jnp.int32).astype(jnp.int16)
+    )
+    levels_ref[pl.ds(t, 1), :] = level
+
+
+def unpack(ref, scale_ref, t, rows):
+    block = ref[pl.ds(pl.multiple_of(t * rows, rows), rows), :]
+    return block.astype(jnp.int32).astype(jnp.float32) * scale_ref[pl.ds(t, 1), :]
+
+
+def cell_of(ray, zi, xi, tiles, outers, inners):
+    owner = ray // tiles
+    return ((owner % outers) ^ xi) * (inners * tiles) + ((owner // outers) ^ zi) * tiles + ray % tiles
+
+
+def forward_kernel(
+    outers, inners, tiles, pos_ref, ray_ref, pixel_ref, projector_ref, volume_ref, own_ref, *rest
+):
+    sends, (total, levels) = rest[:-2], rest[-2:]
+    block, per_slot, rows, cols = projector_ref.shape
+    step = pl.program_id(0)
+    zi, xi = pos_ref[0], pos_ref[1]
+    cells = outers * inners * tiles
+
+    @pl.when(step == 0)
+    def _():
+        total[...] = jnp.zeros_like(total)
+
+    @pl.loop(0, block)
+    def _(i):
+        s = step * block + i
+        cell = cell_of(ray_ref[s], zi, xi, tiles, outers, inners)
+        left = jnp.concatenate([projector_ref[i, g] for g in range(per_slot)], axis=1)
+        right = jnp.concatenate([volume_ref[pixel_ref[s, g]] for g in range(per_slot)], axis=0)
+        total[cell] += jnp.dot(left, right, preferred_element_type=jnp.float32)
+
+    @pl.when(step == pl.num_programs(0) - 1)
+    def _():
+        own_ref[...] = total[: inners * tiles].reshape(own_ref.shape)
+        levels[...] = jnp.zeros_like(levels)
+        for c, send in enumerate(sends):
+            base = (inners + c) * tiles
+
+            @pl.loop(0, tiles)
+            def _(t):
+                pack(total[base + t], send, levels, t)
+
+            send[tiles * rows :, :] = levels[...].astype(jnp.int32).astype(jnp.int16)
+
+
+def forward(pos, slot_ray, slot_pixel, projector, volume, outers, inners, tiles):
+    slots, per_slot, rows, cols = projector.shape
+    slices = volume.shape[2]
+    block = math.gcd(slots, 8)
+    extra = round_up(tiles, 16)
+    payload = jax.ShapeDtypeStruct((tiles * rows + extra, slices), jnp.int16)
+    whole = lambda shape: pl.BlockSpec(shape, lambda i: (0,) * len(shape))
+    count = (outers - 1) * inners
+    return pl.pallas_call(
+        functools.partial(forward_kernel, outers, inners, tiles),
+        grid=(slots // block,),
+        in_specs=[
+            SMEM,
+            SMEM,
+            SMEM,
+            pl.BlockSpec((block, per_slot, rows, cols), lambda i: (i, 0, 0, 0)),
+            whole(volume.shape),
+        ],
+        out_specs=[whole((inners, tiles, rows, slices))] + [whole(payload.shape)] * count,
+        out_shape=[jax.ShapeDtypeStruct((inners, tiles, rows, slices), jnp.float32)]
+        + [payload] * count,
+        scratch_shapes=[
+            pltpu.VMEM((outers * inners * tiles, rows, slices), jnp.float32),
+            pltpu.VMEM((extra, slices), jnp.float32),
+        ],
+        compiler_params=pltpu.CompilerParams(vmem_limit_bytes=LIMIT),
+        cost_estimate=pl.CostEstimate(
+            flops=2 * slots * per_slot * rows * cols * slices,
+            bytes_accessed=projector.size * 2,
+            transcendentals=0,
+        ),
+    )(pos, slot_ray, slot_pixel, projector, volume)
+
+
+def scales(ref, tiles, rows):
+    raw = ref[tiles * rows :, :].astype(jnp.int32).astype(jnp.float32)
+    return jnp.exp2(raw) * (1.0 / FULL)
+
+
+def combine_kernel(count, own_ref, *rest):
+    arrived, out_ref, scale_refs, levels = (
+        rest[:count],
+        rest[count],
+        rest[count + 1 : 2 * count + 1],
+        rest[-1],
+    )
+    _, tiles, rows, _ = own_ref.shape
+    levels[...] = jnp.zeros_like(levels)
+    for ref, scale_ref in zip(arrived, scale_refs):
+        scale_ref[...] = scales(ref, tiles, rows)
+
+    @pl.loop(0, tiles)
+    def _(t):
+        tile = own_ref[0, t]
+        for ref, scale_ref in zip(arrived, scale_refs):
+            tile = tile + unpack(ref, scale_ref, t, rows)
+        pack(tile, out_ref, levels, t)
+
+    out_ref[tiles * rows :, :] = levels[...].astype(jnp.int32).astype(jnp.int16)
+
+
+def combine(own, k, arrived):
+    _, tiles, rows, slices = own.shape
+    extra = round_up(tiles, 16)
+    count = len(arrived)
+    return pl.pallas_call(
+        functools.partial(combine_kernel, count),
+        grid=(1,),
+        in_specs=[pl.BlockSpec((1, tiles, rows, slices), lambda i: (k, 0, 0, 0))] + [VMEM] * count,
+        out_specs=VMEM,
+        out_shape=jax.ShapeDtypeStruct((tiles * rows + extra, slices), jnp.int16),
+        scratch_shapes=[pltpu.VMEM((extra, slices), jnp.float32)] * (count + 1),
+        compiler_params=pltpu.CompilerParams(vmem_limit_bytes=LIMIT),
+    )(own, *arrived)
+
+
+def residual_kernel(count, table_ref, own_ref, sinogram_ref, index_ref, *rest):
+    arrived, out_ref, scale_refs, weight = (
+        rest[:count],
+        rest[count],
+        rest[count + 1 : 2 * count + 1],
+        rest[-1],
+    )
+    _, tiles, rows, _ = own_ref.shape
+    for ref, scale_ref in zip(arrived, scale_refs):
+        scale_ref[...] = scales(ref, tiles, rows)
+    looked = jnp.zeros(weight.shape, jnp.float32)
+    for c in range(table_ref.shape[0]):
+        looked = jnp.where(index_ref[...] == c, table_ref[c], looked)
+    weight[...] = looked
+
+    @pl.loop(0, tiles)
+    def _(t):
+        tile = own_ref[0, t]
+        for ref, scale_ref in zip(arrived, scale_refs):
+            tile = tile + unpack(ref, scale_ref, t, rows)
+        gap = (sinogram_ref[t].astype(jnp.float32) - tile).T
+        out_ref[t] = (weight[pl.ds(t, 1), :] * gap).astype(jnp.bfloat16)
+
+
+def residual_of(table, own, sinogram, index, arrived):
+    _, tiles, rows, slices = own.shape
+    extra = round_up(tiles, 16)
+    count = len(arrived)
+    return pl.pallas_call(
+        functools.partial(residual_kernel, count),
+        grid=(1,),
+        in_specs=[SMEM, pl.BlockSpec((1, tiles, rows, slices), lambda i: (0, 0, 0, 0)), VMEM, VMEM]
+        + [VMEM] * count,
+        out_specs=VMEM,
+        out_shape=jax.ShapeDtypeStruct((tiles, slices, rows), jnp.bfloat16),
+        scratch_shapes=[pltpu.VMEM((extra, slices), jnp.float32)] * count
+        + [pltpu.VMEM((tiles, rows), jnp.float32)],
+        compiler_params=pltpu.CompilerParams(vmem_limit_bytes=LIMIT),
+    )(table, own, sinogram, index, *arrived)
+
+
+def column_kernel(pixel_ref, projector_ref, out_ref):
+    block, per_slot, rows, cols = projector_ref.shape
+    step = pl.program_id(0)
+
+    @pl.when(step == 0)
+    def _():
+        out_ref[...] = jnp.zeros_like(out_ref)
+
+    @pl.loop(0, block)
+    def _(i):
+        for g in range(per_slot):
+            column = jnp.sum(projector_ref[i, g].astype(jnp.float32), axis=0, keepdims=True)
+            out_ref[pixel_ref[step * block + i, g]] += column
+
+
+def column_sums(slot_pixel, projector, patch_tiles):
+    slots, per_slot, rows, cols = projector.shape
+    block = math.gcd(slots, 8)
+    return pl.pallas_call(
+        column_kernel,
+        grid=(slots // block,),
+        in_specs=[SMEM, pl.BlockSpec((block, per_slot, rows, cols), lambda i: (i, 0, 0, 0))],
+        out_specs=pl.BlockSpec((patch_tiles, 1, cols), lambda i: (0, 0, 0)),
+        out_shape=jax.ShapeDtypeStruct((patch_tiles, 1, cols), jnp.float32),
+        compiler_params=pltpu.CompilerParams(vmem_limit_bytes=LIMIT),
+        cost_estimate=pl.CostEstimate(
+            flops=2 * projector.size, bytes_accessed=projector.size * 2, transcendentals=0
+        ),
+    )(slot_pixel, projector)
+
+
+def backward_kernel(
+    outers, inners, pos_ref, ray_ref, pixel_ref, projector_ref, volume_ref, column_ref, *rest
+):
+    chunks, (out_ref, held, total) = rest[:-3], rest[-3:]
+    block, per_slot, rows, cols = projector_ref.shape
+    tiles = chunks[0].shape[0]
+    step = pl.program_id(0)
+    zi, xi = pos_ref[0], pos_ref[1]
+
+    @pl.when(step == 0)
+    def _():
+        total[...] = jnp.zeros_like(total)
+        for c, chunk in enumerate(chunks):
+            held[c * tiles : (c + 1) * tiles] = chunk[...]
+
+    @pl.loop(0, block)
+    def _(i):
+        s = step * block + i
+        cell = cell_of(ray_ref[s], zi, xi, tiles, outers, inners)
+        right = jnp.concatenate([projector_ref[i, g] for g in range(per_slot)], axis=1)
+        spread = jnp.dot(held[cell], right, preferred_element_type=jnp.float32)
+        for g in range(per_slot):
+            total[pixel_ref[s, g]] += spread[:, g * cols : (g + 1) * cols]
+
+    @pl.when(step == pl.num_programs(0) - 1)
+    def _():
+        @pl.loop(0, total.shape[0])
+        def _(q):
+            out_ref[q] = volume_ref[q].astype(jnp.float32) + (total[q] / column_ref[q]).T
+
+
+def backward(pos, slot_ray, slot_pixel, projector, volume, columns, chunks, outers, inners):
+    slots, per_slot, rows, cols = projector.shape
+    tiles = chunks[0].shape[0]
+    patch_tiles, _, slices = volume.shape
+    block = math.gcd(slots, 8)
+    whole = lambda shape: pl.BlockSpec(shape, lambda i: (0,) * len(shape))
+    return pl.pallas_call(
+        functools.partial(backward_kernel, outers, inners),
+        grid=(slots // block,),
+        in_specs=[
+            SMEM,
+            SMEM,
+            SMEM,
+            pl.BlockSpec((block, per_slot, rows, cols), lambda i: (i, 0, 0, 0)),
+            whole(volume.shape),
+            whole(columns.shape),
+        ]
+        + [whole(chunks[0].shape)] * len(chunks),
+        out_specs=whole(volume.shape),
+        out_shape=jax.ShapeDtypeStruct(volume.shape, jnp.float32),
+        scratch_shapes=[
+            pltpu.VMEM((len(chunks) * tiles, slices, rows), jnp.bfloat16),
+            pltpu.VMEM((patch_tiles, slices, cols), jnp.float32),
+        ],
+        compiler_params=pltpu.CompilerParams(vmem_limit_bytes=LIMIT),
+        cost_estimate=pl.CostEstimate(
+            flops=2 * slots * per_slot * rows * cols * slices,
+            bytes_accessed=projector.size * 2,
+            transcendentals=0,
+        ),
+    )(pos, slot_ray, slot_pixel, projector, volume, columns, *chunks)
+
+
+def dense_plan(volume, projector, slot_ray, slot_pixel, sinogram, weight_index, weight_table):
+    inners = lax.axis_size("inner")
+    outers = lax.axis_size("outer")
+    tiles = sinogram.shape[0]
+    pos = jnp.stack([lax.axis_index("inner"), lax.axis_index("outer")]).astype(jnp.int32)
+    own, *sends = forward(pos, slot_ray, slot_pixel, projector, volume, outers, inners, tiles)
+    arrived = {k: [] for k in range(inners)}
+    for k in reversed(range(inners)):
+        for j in range(1, outers):
+            arrived[k].append(swap(sends[(j - 1) * inners + k], "outer", j))
+    columns = column_sums(slot_pixel, projector, volume.shape[0])
+    live = list(range(inners))
+    bit = 1
+    while bit < inners:
+        for k in reversed([k for k in live if k & bit]):
+            arrived[k ^ bit].append(swap(combine(own, k, arrived[k]), "inner", bit))
+        live = [k for k in live if not k & bit]
+        bit *= 2
+    residual = residual_of(
+        weight_table.astype(jnp.float32), own, sinogram, weight_index, arrived[0]
+    )
+    held = {0: residual}
+    while bit > 1:
+        bit //= 2
+        for k in sorted(held):
+            held[k ^ bit] = swap(held[k], "inner", bit)
+    chunks = [held[k] for k in range(inners)]
+    for j in range(1, outers):
+        chunks += [swap(held[k], "outer", j) for k in range(inners)]
+    return backward(
+        pos, slot_ray, slot_pixel, projector, volume, columns, chunks, outers, inners
+    )
+
+
+def slot_plan(volume, projector, slot_ray, slot_pixel, sinogram, weight_index, weight_table):
     inners = lax.axis_size("inner")
     outers = lax.axis_size("outer")
     slot_count = projector.shape[0]
@@ -77,14 +397,14 @@
     )
     slot_residual = returned.reshape(cell_count, tile_rows, slice_count)[position]
     owners = jnp.arange(patch_tiles)
-    backward = jnp.zeros((patch_tiles, tile_cols, slice_count), jnp.float32)
+    backward_sum = jnp.zeros((patch_tiles, tile_cols, slice_count), jnp.float32)
     column_sum = jnp.zeros((patch_tiles, tile_cols), jnp.float32)
     for column in range(per_slot):
         member = (owners[:, None] == slot_pixel[None, :, column]).astype(jnp.float32)
         spread = jnp.einsum(
             "srp,src->spc", projector[:, column], slot_residual, preferred_element_type=jnp.float32
         )
-        backward = backward + jnp.einsum(
+        backward_sum = backward_sum + jnp.einsum(
             "ts,spc->tpc", member, spread, precision=lax.Precision.HIGHEST
         )
         column_sum = column_sum + jnp.dot(
@@ -92,7 +412,16 @@
             jnp.sum(projector[:, column], axis=1, dtype=jnp.float32),
             precision=lax.Precision.HIGHEST,
         )
-    return volume.astype(jnp.float32) + backward / column_sum[:, :, None]
+    return volume.astype(jnp.float32) + backward_sum / column_sum[:, :, None]
+
+
+def on_device(volume, projector, slot_ray, slot_pixel, sinogram, weight_index, weight_table):
+    inners = lax.axis_size("inner")
+    outers = lax.axis_size("outer")
+    capacity = 2 * slot_ray.shape[0] // inners
+    powers = inners & (inners - 1) == 0 and outers & (outers - 1) == 0
+    plan = dense_plan if powers and sinogram.shape[0] * outers <= capacity else slot_plan
+    return plan(volume, projector, slot_ray, slot_pixel, sinogram, weight_index, weight_table)
 
 
 def solution(mesh):

time: 269 us -> 90.8 us (0.34)
  waiting for transfers between devices: 154 us -> 39.1 us
  matrix products: 36.8 us -> 0 us
  local copies, waits for them, and re-layouts: 31 us -> 4.57 us
  Pallas kernels: 0 us -> 21.7 us
  between operations: 13.6 us -> 0.13 us
  blocking collectives: 8.74 us -> 0 us
  starting transfers between devices: 16 us -> 23.9 us
  other arithmetic: 7.14 us -> 0.08 us
    all_to_all x3 -> x0, waiting for transfers between devices: 135 us -> none  [the longest x1 91.7 us: on_device(): lax.all_to_all(outgoing.reshape(inners, capacity, tile_rows, slice_count)...]
    ppermute x0 -> x14, waiting for transfers between devices: none -> 39.1 us  [swap(): return lax.ppermute(value, axis, [(i, i ^ bits) for i in range(size)])]
    dot_general x18 -> x0, matrix products: 36.8 us -> none  [the longest x4 13.9 us: on_device(): jnp.einsum('srp,spc->src', projector[:, column], pixels, preferred_elemen...]
    ppermute x0 -> x14, starting transfers between devices: none -> 23.9 us  [swap(): return lax.ppermute(value, axis, [(i, i ^ bits) for i in range(size)])]
    pallas_call x0 -> x7, Pallas kernels: none -> 21.7 us  [the longest x1 8.66 us: backward(): pl.pallas_call(functools.partial(backward_kernel, outers, inners), grid=(...]
    reduce_scatter x1 -> x0, waiting for transfers between devices: 19.3 us -> none  [on_device(): lax.psum_scatter(block_sums, 'outer', scatter_dimension=0, tiled=True)]
    all_to_all x3 -> x0, starting transfers between devices: 16 us -> none  [the longest x1 6.32 us: on_device(): lax.all_to_all(labels.reshape(inners, capacity), 'inner', split_axis=0, c...]
    dot_general x4 -> x0, local copies, waits for them, and re-layouts: 10.7 us -> none  [on_device(): jnp.einsum('srp,src->spc', projector[:, column], slot_residual, preferred...]
  transfers between devices with their start and end apart: 4 -> 14, of which waited for: 3 -> 9; matrix products, arithmetic and copies ran while one was open for 13% -> 0% of each run, Pallas kernels for 0% -> 4%
where the time goes in v1:
time: 90.8 us; the launch traced here: 89.5 us
  waiting for transfers between devices  39.1 us (43%)
  starting transfers between devices  23.9 us (26%)
  Pallas kernels  21.7 us (24%)
  local copies, waits for them, and re-layouts  4.57 us (5%)
    ppermute x14, waiting for transfers between devices, swap(): return lax.ppermute(value, axis, [(i, i ^ bits) for i in range(size)])  39.1 us
    ppermute x14, starting transfers between devices, swap(): return lax.ppermute(value, axis, [(i, i ^ bits) for i in range(size)])  23.9 us
    pallas_call x1, Pallas kernels, backward(): pl.pallas_call(functools.partial(backward_kernel, outers, inners), grid=(...  8.66 us
    pallas_call x1, Pallas kernels, forward(): pl.pallas_call(functools.partial(forward_kernel, outers, inners, tiles),...  8.35 us
    unnamed x19, local copies, waits for them, and re-layouts  4.57 us
    pallas_call x1, Pallas kernels, column_sums(): pl.pallas_call(column_kernel, grid=(slots // block,), in_specs=[SMEM, pl....  1.99 us
  transfers between devices with their start and end apart: 14, of which 9 were waited for; matrix products, arithmetic and copies ran while one was open for 0% of the time, Pallas kernels for 4%

profile of v1, /device:TPU:0, one launch (start us, length us, event | category | flops | bytes accessed | tf_op | source)
XLA Modules:
  0.0 89.5 jit_solution(16917193986348013907)
XLA Ops:
  0.0 0.8 copy.10.pixel_ref
  0.8 0.1 pad_add_fusion.pos_ref
  0.8 0.0 copy-start
  0.8 2.2 %copy-done = bf16[32,4,128,128]{3,2,1,0:T(8,128)(2,1)S(1)} copy-done((bf16[32,4,128,128]{3,2,1,0:T(8,128)(2,1)S(1)}, bf16[32,4,128,128]{3,2,1,0:T(8,128)(2,1)}, u32[]{:S(2)}) %copy-start) | copy-done | bytes 4194328
  3.0 0.0 copy-start.2
  3.0 0.9 %copy-done.2 = bf16[6,128,128]{2,1,0:T(8,128)(2,1)S(1)} copy-done((bf16[6,128,128]{2,1,0:T(8,128)(2,1)S(1)}, bf16[6,128,128]{2,1,0:T(8,128)(2,1)}, u32[]{:S(2)}) %copy-start.2) | copy-done | bytes 196632
  4.0 0.0 copy-start.6
  4.0 0.7 copy-done.6
  4.6 8.3 %shard_map.74 = (f32[4,8,128,128]{3,2,1,0:T(8,128)S(1)}, s16[1040,128]{1,0:T(8,128)(2,1)S(1)}, s16[1040,128]{1,0:T(8,128)(2,1)S(1)}, s16[1040,128]{1,0:T(8,128)(2,1)S(1)}, s16[1040,128]{1,0:T(8,128)(2,1)S(1)}) custom-call(s32[2]{0:T(128)S(1)} %pad_add_fusion.pos_ref, s32[32]{0:T(128)S(1)} %copy-done.6, s32[32,4]{1,0:T(8,128)S(1)} %copy.10.pixel_ref, ...), custom_call_target="tpu_custom_call" | custom-call | flops 536870912 | bytes 4194304 | tf_op jit(solution)/shard_map/pallas_call | solution.py:89
  13.0 0.0 copy-start.8
  13.0 0.0 copy-start.4
  13.0 0.0 copy-start.5
  13.0 3.0 %collective-permute-start.4 = (s16[1040,128]{1,0:T(8,128)(2,1)S(1)}, s16[1040,128]{1,0:T(8,128)(2,1)S(1)}, u32[]{:S(2)}, u32[]{:S(2)}) collective-permute-start(s16[1040,128]{1,0:T(8,128)(2,1)S(1)} %get-tuple-element.14), channel_id=1, source_target_pairs={{0,2},{2,0},{1,3},{3,1},{4,6},{6,4},{5,7},{7,5},{8,10},{10,8},{9,1... | collective-permute-start | bytes 798728 | tf_op jit(solution)/shard_map/ppermute | solution.py:23
  16.0 0.1 collective-permute-start.3
  16.1 1.9 %collective-permute-start.1 = (s16[1040,128]{1,0:T(8,128)(2,1)S(1)}, s16[1040,128]{1,0:T(8,128)(2,1)S(1)}, u32[]{:S(2)}, u32[]{:S(2)}) collective-permute-start(s16[1040,128]{1,0:T(8,128)(2,1)S(1)} %get-tuple-element.12), channel_id=1, source_target_pairs={{0,2},{2,0},{1,3},{3,1},{4,6},{6,4},{5,7},{7,5},{8,10},{10,8},{9,1... | collective-permute-start | bytes 798728 | tf_op jit(solution)/shard_map/ppermute | solution.py:23
  18.0 5.2 %collective-permute-done.4.rest_0_ = s16[1040,128]{1,0:T(8,128)(2,1)S(1)} collective-permute-done((s16[1040,128]{1,0:T(8,128)(2,1)S(1)}, s16[1040,128]{1,0:T(8,128)(2,1)S(1)}, u32[]{:S(2)}, u32[]{:S(2)}) %collective-permute-start.4) | collective-permute-done | bytes 266272 | tf_op jit(solution)/shard_map/ppermute | solution.py:23
  23.2 0.4 shard_map.76
  23.6 2.2 %collective-permute-start.5 = (s16[1040,128]{1,0:T(8,128)(2,1)S(1)}, s16[1040,128]{1,0:T(8,128)(2,1)S(1)}, u32[]{:S(2)}, u32[]{:S(2)}) collective-permute-start(s16[1040,128]{1,0:T(8,128)(2,1)S(1)} %shard_map.76), channel_id=1, source_target_pairs={{0,4},{4,0},{8,12},{12,8},{1,5},{5,1},{9,13},{13,9},{2,6},{6,2},{1... | collective-permute-start | bytes 798728 | tf_op jit(solution)/shard_map/ppermute | solution.py:23
  25.8 0.0 copy-start.1
  25.8 1.5 %collective-permute-start = (s16[1040,128]{1,0:T(8,128)(2,1)S(1)}, s16[1040,128]{1,0:T(8,128)(2,1)S(1)}, u32[]{:S(2)}, u32[]{:S(2)}) collective-permute-start(s16[1040,128]{1,0:T(8,128)(2,1)S(1)} %get-tuple-element.11), channel_id=1, source_target_pairs={{0,2},{2,0},{1,3},{3,1},{4,6},{6,4},{5,7},{7,5},{8,10},{10,8},{9,1... | collective-permute-start | bytes 798728 | tf_op jit(solution)/shard_map/ppermute | solution.py:23
  27.3 7.3 %collective-permute-done.1.rest_0_ = s16[1040,128]{1,0:T(8,128)(2,1)S(1)} collective-permute-done((s16[1040,128]{1,0:T(8,128)(2,1)S(1)}, s16[1040,128]{1,0:T(8,128)(2,1)S(1)}, u32[]{:S(2)}, u32[]{:S(2)}) %collective-permute-start.1) | collective-permute-done | bytes 266272 | tf_op jit(solution)/shard_map/ppermute | solution.py:23
  34.6 0.4 shard_map.75
  35.0 2.2 %collective-permute-start.2 = (s16[1040,128]{1,0:T(8,128)(2,1)S(1)}, s16[1040,128]{1,0:T(8,128)(2,1)S(1)}, u32[]{:S(2)}, u32[]{:S(2)}) collective-permute-start(s16[1040,128]{1,0:T(8,128)(2,1)S(1)} %shard_map.75), channel_id=1, source_target_pairs={{0,4},{4,0},{8,12},{12,8},{1,5},{5,1},{9,13},{13,9},{2,6},{6,2},{1... | collective-permute-start | bytes 798728 | tf_op jit(solution)/shard_map/ppermute | solution.py:23
  37.2 0.0 collective-permute-done.3.rest_0_
  37.2 0.0 collective-permute-done.5.rest_1_
  37.3 0.5 shard_map.77
  37.7 0.0 copy-start.3
  37.7 0.0 copy-start.7
  37.7 2.7 %collective-permute-start.6 = (s16[1040,128]{1,0:T(8,128)(2,1)S(1)}, s16[1040,128]{1,0:T(8,128)(2,1)S(1)}, u32[]{:S(2)}, u32[]{:S(2)}) collective-permute-start(s16[1040,128]{1,0:T(8,128)(2,1)S(1)} %shard_map.77), channel_id=1, source_target_pairs={{0,8},{4,12},{8,0},{12,4},{1,9},{5,13},{9,1},{13,5},{2,10},{6,14},... | collective-permute-start | bytes 798728 | tf_op jit(solution)/shard_map/ppermute | solution.py:23
  40.4 0.0 copy-done.8
  40.4 0.0 collective-permute-done.rest_0_
  40.4 6.4 %collective-permute-done.2.rest_1_ = s16[1040,128]{1,0:T(8,128)(2,1)S(1)} collective-permute-done((s16[1040,128]{1,0:T(8,128)(2,1)S(1)}, s16[1040,128]{1,0:T(8,128)(2,1)S(1)}, u32[]{:S(2)}, u32[]{:S(2)}) %collective-permute-start.2) | collective-permute-done | bytes 266272 | tf_op jit(solution)/shard_map/ppermute | solution.py:23
  46.8 4.2 %collective-permute-done.6.rest_2_ = s16[1040,128]{1,0:T(8,128)(2,1)S(1)} collective-permute-done((s16[1040,128]{1,0:T(8,128)(2,1)S(1)}, s16[1040,128]{1,0:T(8,128)(2,1)S(1)}, u32[]{:S(2)}, u32[]{:S(2)}) %collective-permute-start.6) | collective-permute-done | bytes 266272 | tf_op jit(solution)/shard_map/ppermute | solution.py:23
  51.0 0.0 copy-done.4
  51.0 0.0 copy-done.5
  51.0 1.4 %shard_map.78.rest_0_ = bf16[8,128,128]{2,1,0:T(8,128)(2,1)S(1)} custom-call(f32[16]{0:T(128)S(1)} %convert_element_type.3.table_ref, f32[4,8,128,128]{3,2,1,0:T(8,128)S(1)} %get-tuple-element.10.own_ref, bf16[8,128,128]{2,1,0:T(8,128)(2,1)S(1)} %copy-done.4, s32[8,128]{1,0:T(8,128)S(1)} %copy-done.5, s16[1040,128]{1,0:T(8,128)(2,1)S(1)} %collective-permute-done.rest_0_, ...), custom_call_target="tpu_custom_call" | custom-call | tf_op jit(solution)/shard_map/pallas_call | solution.py:185
  52.5 0.1 collective-permute-start.8
  52.6 5.2 %collective-permute-start.7 = (bf16[8,128,128]{2,1,0:T(8,128)(2,1)S(1)}, bf16[8,128,128]{2,1,0:T(8,128)(2,1)S(1)}, u32[]{:S(2)}, u32[]{:S(2)}) collective-permute-start(bf16[8,128,128]{2,1,0:T(8,128)(2,1)S(1)} %shard_map.78.rest_0_), channel_id=1, source_target_pairs={{0,4},{4,0},{8,12},{12,8},{1,5},{5,1},{9,13},{13,9},{2,6},{6,2},{1... | collective-permute-start | bytes 786440 | tf_op jit(solution)/shard_map/ppermute | solution.py:23
  57.8 5.0 %collective-permute-done.8.rest_2_ = bf16[8,128,128]{2,1,0:T(8,128)(2,1)S(1)} collective-permute-done((bf16[8,128,128]{2,1,0:T(8,128)(2,1)S(1)}, bf16[8,128,128]{2,1,0:T(8,128)(2,1)S(1)}, u32[]{:S(2)}, u32[]{:S(2)}) %collective-permute-start.8) | collective-permute-done | bytes 262176 | tf_op jit(solution)/shard_map/ppermute | solution.py:23
  62.7 0.0 collective-permute-start.9
  62.7 1.5 %collective-permute-start.10 = (bf16[8,128,128]{2,1,0:T(8,128)(2,1)S(1)}, bf16[8,128,128]{2,1,0:T(8,128)(2,1)S(1)}, u32[]{:S(2)}, u32[]{:S(2)}) collective-permute-start(bf16[8,128,128]{2,1,0:T(8,128)(2,1)S(1)} %shard_map.78.rest_0_), channel_id=1, source_target_pairs={{0,2},{2,0},{1,3},{3,1},{4,6},{6,4},{5,7},{7,5},{8,10},{10,8},{9,1... | collective-permute-start | bytes 786440 | tf_op jit(solution)/shard_map/ppermute | solution.py:23
  64.2 0.5 collective-permute-start.12
  64.8 0.7 collective-permute-done.7.rest_1_
  65.4 1.5 %collective-permute-start.11 = (bf16[8,128,128]{2,1,0:T(8,128)(2,1)S(1)}, bf16[8,128,128]{2,1,0:T(8,128)(2,1)S(1)}, u32[]{:S(2)}, u32[]{:S(2)}) collective-permute-start(bf16[8,128,128]{2,1,0:T(8,128)(2,1)S(1)} %collective-permute-done.7.rest_1_), channel_id=1, source_target_pairs={{0,2},{2,0},{1,3},{3,1},{4,6},{6,4},{5,7},{7,5},{8,10},{10,8},{9,1... | collective-permute-start | bytes 786440 | tf_op jit(solution)/shard_map/ppermute | solution.py:23
  66.9 2.2 %collective-permute-done.9.rest_3_ = bf16[8,128,128]{2,1,0:T(8,128)(2,1)S(1)} collective-permute-done((bf16[8,128,128]{2,1,0:T(8,128)(2,1)S(1)}, bf16[8,128,128]{2,1,0:T(8,128)(2,1)S(1)}, u32[]{:S(2)}, u32[]{:S(2)}) %collective-permute-start.9) | collective-permute-done | bytes 262176 | tf_op jit(solution)/shard_map/ppermute | solution.py:23
  69.1 1.5 %collective-permute-start.13 = (bf16[8,128,128]{2,1,0:T(8,128)(2,1)S(1)}, bf16[8,128,128]{2,1,0:T(8,128)(2,1)S(1)}, u32[]{:S(2)}, u32[]{:S(2)}) collective-permute-start(bf16[8,128,128]{2,1,0:T(8,128)(2,1)S(1)} %collective-permute-done.9.rest_3_), channel_id=1, source_target_pairs={{0,2},{2,0},{1,3},{3,1},{4,6},{6,4},{5,7},{7,5},{8,10},{10,8},{9,1... | collective-permute-start | bytes 786440 | tf_op jit(solution)/shard_map/ppermute | solution.py:23
  70.6 0.0 copy-done.1
  70.6 2.0 %shard_map.73.column_ref = f32[6,1,128]{2,1,0:T(1,128)S(1)} custom-call(s32[32,4]{1,0:T(8,128)S(1)} %copy.10.pixel_ref, bf16[32,4,128,128]{3,2,1,0:T(8,128)(2,1)S(1)} %copy-done.1), custom_call_target="tpu_custom_call" | custom-call | flops 4194304 | bytes 4194304 | tf_op jit(solution)/shard_map/pallas_call | solution.py:216
  72.6 0.0 collective-permute-done.10.rest_4_
  72.6 5.4 %collective-permute-done.11.rest_5_ = bf16[8,128,128]{2,1,0:T(8,128)(2,1)S(1)} collective-permute-done((bf16[8,128,128]{2,1,0:T(8,128)(2,1)S(1)}, bf16[8,128,128]{2,1,0:T(8,128)(2,1)S(1)}, u32[]{:S(2)}, u32[]{:S(2)}) %collective-permute-start.11) | collective-permute-done | bytes 262176 | tf_op jit(solution)/shard_map/ppermute | solution.py:23
  78.0 0.0 collective-permute-done.12.rest_6_
  78.0 2.8 %collective-permute-done.13.rest_7_ = bf16[8,128,128]{2,1,0:T(8,128)(2,1)S(1)} collective-permute-done((bf16[8,128,128]{2,1,0:T(8,128)(2,1)S(1)}, bf16[8,128,128]{2,1,0:T(8,128)(2,1)S(1)}, u32[]{:S(2)}, u32[]{:S(2)}) %collective-permute-start.13) | collective-permute-done | bytes 262176 | tf_op jit(solution)/shard_map/ppermute | solution.py:23
  80.8 0.0 copy-done.3
  80.8 0.0 copy-done.7
  80.8 8.7 %shard_map.79 = f32[6,128,128]{2,1,0:T(8,128)} custom-call(s32[2]{0:T(128)S(1)} %pad_add_fusion.pos_ref, s32[32]{0:T(128)S(1)} %copy-done.7, s32[32,4]{1,0:T(8,128)S(1)} %copy.10.pixel_ref, bf16[32,4,128,128]{3,2,1,0:T(8,128)(2,1)S(1)} %copy-done.1, bf16[6,128,128]{2,1,0:T(8,128)(2,1)S(1)} %copy-done.3, f32[6,1,128]{2,1,0:T(1,128)S(1)} %shard_map.73.column_ref, ...), custom_call_target="tpu_custom_call" | custom-call | flops 536870912 | bytes 4194304 | tf_op jit(solution)/shard_map/pallas_call | solution.py:266
  (1 shorter events, 0.0 us)
Async XLA Ops:
  0.8 2.2 %copy-start = (bf16[32,4,128,128]{3,2,1,0:T(8,128)(2,1)S(1)}, bf16[32,4,128,128]{3,2,1,0:T(8,128)(2,1)}, u32[]{:S(2)}) copy-start(bf16[32,4,128,128]{3,2,1,0:T(8,128)(2,1)} %projector_ref.5) | copy-start | bytes 12582916
  3.0 0.9 %copy-start.2 = (bf16[6,128,128]{2,1,0:T(8,128)(2,1)S(1)}, bf16[6,128,128]{2,1,0:T(8,128)(2,1)}, u32[]{:S(2)}) copy-start(bf16[6,128,128]{2,1,0:T(8,128)(2,1)} %volume_ref.3) | copy-start | bytes 589828
  4.0 0.7 copy-start.6
  13.0 27.4 %copy-start.8 = (bf16[16]{0:T(256)(128)(2,1)S(1)}, bf16[16]{0:T(256)(128)(2,1)}, u32[]{:S(2)}) copy-start(bf16[16]{0:T(256)(128)(2,1)} %param.13) | copy-start | bytes 100
  13.0 38.1 %copy-start.4 = (bf16[8,128,128]{2,1,0:T(8,128)(2,1)S(1)}, bf16[8,128,128]{2,1,0:T(8,128)(2,1)}, u32[]{:S(2)}) copy-start(bf16[8,128,128]{2,1,0:T(8,128)(2,1)} %sinogram_ref.1) | copy-start | bytes 786436
  13.0 38.0 %copy-start.5 = (s32[8,128]{1,0:T(8,128)S(1)}, s32[8,128]{1,0:T(8,128)}, u32[]{:S(2)}) copy-start(s32[8,128]{1,0:T(8,128)} %index_ref.1) | copy-start | bytes 12292
  13.0 10.2 %collective-permute-start.4 = (s16[1040,128]{1,0:T(8,128)(2,1)S(1)}, s16[1040,128]{1,0:T(8,128)(2,1)S(1)}, u32[]{:S(2)}, u32[]{:S(2)}) collective-permute-start(s16[1040,128]{1,0:T(8,128)(2,1)S(1)} %get-tuple-element.14), channel_id=1, source_target_pairs={{0,2},{2,0},{1,3},{3,1},{4,6},{6,4},{5,7},{7,5},{8,10},{10,8},{9,1... | collective-permute-start | bytes 798728 | tf_op jit(solution)/shard_map/ppermute | solution.py:23
  16.0 21.2 %collective-permute-start.3 = (s16[1040,128]{1,0:T(8,128)(2,1)S(1)}, s16[1040,128]{1,0:T(8,128)(2,1)S(1)}, u32[]{:S(2)}, u32[]{:S(2)}) collective-permute-start(s16[1040,128]{1,0:T(8,128)(2,1)S(1)} %get-tuple-element.13), channel_id=1, source_target_pairs={{0,2},{2,0},{1,3},{3,1},{4,6},{6,4},{5,7},{7,5},{8,10},{10,8},{9,1... | collective-permute-start | bytes 798728 | tf_op jit(solution)/shard_map/ppermute | solution.py:23
  16.1 18.6 %collective-permute-start.1 = (s16[1040,128]{1,0:T(8,128)(2,1)S(1)}, s16[1040,128]{1,0:T(8,128)(2,1)S(1)}, u32[]{:S(2)}, u32[]{:S(2)}) collective-permute-start(s16[1040,128]{1,0:T(8,128)(2,1)S(1)} %get-tuple-element.12), channel_id=1, source_target_pairs={{0,2},{2,0},{1,3},{3,1},{4,6},{6,4},{5,7},{7,5},{8,10},{10,8},{9,1... | collective-permute-start | bytes 798728 | tf_op jit(solution)/shard_map/ppermute | solution.py:23
  23.6 13.6 %collective-permute-start.5 = (s16[1040,128]{1,0:T(8,128)(2,1)S(1)}, s16[1040,128]{1,0:T(8,128)(2,1)S(1)}, u32[]{:S(2)}, u32[]{:S(2)}) collective-permute-start(s16[1040,128]{1,0:T(8,128)(2,1)S(1)} %shard_map.76), channel_id=1, source_target_pairs={{0,4},{4,0},{8,12},{12,8},{1,5},{5,1},{9,13},{13,9},{2,6},{6,2},{1... | collective-permute-start | bytes 798728 | tf_op jit(solution)/shard_map/ppermute | solution.py:23
  25.8 44.8 %copy-start.1 = (bf16[32,4,128,128]{3,2,1,0:T(8,128)(2,1)S(1)}, bf16[32,4,128,128]{3,2,1,0:T(8,128)(2,1)}, u32[]{:S(2)}) copy-start(bf16[32,4,128,128]{3,2,1,0:T(8,128)(2,1)} %projector_ref.5) | copy-start | bytes 12582916
  25.8 14.6 %collective-permute-start = (s16[1040,128]{1,0:T(8,128)(2,1)S(1)}, s16[1040,128]{1,0:T(8,128)(2,1)S(1)}, u32[]{:S(2)}, u32[]{:S(2)}) collective-permute-start(s16[1040,128]{1,0:T(8,128)(2,1)S(1)} %get-tuple-element.11), channel_id=1, source_target_pairs={{0,2},{2,0},{1,3},{3,1},{4,6},{6,4},{5,7},{7,5},{8,10},{10,8},{9,1... | collective-permute-start | bytes 798728 | tf_op jit(solution)/shard_map/ppermute | solution.py:23
  35.0 11.7 %collective-permute-start.2 = (s16[1040,128]{1,0:T(8,128)(2,1)S(1)}, s16[1040,128]{1,0:T(8,128)(2,1)S(1)}, u32[]{:S(2)}, u32[]{:S(2)}) collective-permute-start(s16[1040,128]{1,0:T(8,128)(2,1)S(1)} %shard_map.75), channel_id=1, source_target_pairs={{0,4},{4,0},{8,12},{12,8},{1,5},{5,1},{9,13},{13,9},{2,6},{6,2},{1... | collective-permute-start | bytes 798728 | tf_op jit(solution)/shard_map/ppermute | solution.py:23
  37.7 43.1 %copy-start.3 = (bf16[6,128,128]{2,1,0:T(8,128)(2,1)S(1)}, bf16[6,128,128]{2,1,0:T(8,128)(2,1)}, u32[]{:S(2)}) copy-start(bf16[6,128,128]{2,1,0:T(8,128)(2,1)} %volume_ref.3) | copy-start | bytes 589828
  37.7 43.1 %copy-start.7 = (s32[32]{0:T(128)S(1)}, s32[32]{0:T(128)}, u32[]{:S(2)}) copy-start(s32[32]{0:T(128)} %ray_ref.3) | copy-start | bytes 388
  37.7 13.3 %collective-permute-start.6 = (s16[1040,128]{1,0:T(8,128)(2,1)S(1)}, s16[1040,128]{1,0:T(8,128)(2,1)S(1)}, u32[]{:S(2)}, u32[]{:S(2)}) collective-permute-start(s16[1040,128]{1,0:T(8,128)(2,1)S(1)} %shard_map.77), channel_id=1, source_target_pairs={{0,8},{4,12},{8,0},{12,4},{1,9},{5,13},{9,1},{13,5},{2,10},{6,14},... | collective-permute-start | bytes 798728 | tf_op jit(solution)/shard_map/ppermute | solution.py:23
  52.5 10.2 %collective-permute-start.8 = (bf16[8,128,128]{2,1,0:T(8,128)(2,1)S(1)}, bf16[8,128,128]{2,1,0:T(8,128)(2,1)S(1)}, u32[]{:S(2)}, u32[]{:S(2)}) collective-permute-start(bf16[8,128,128]{2,1,0:T(8,128)(2,1)S(1)} %shard_map.78.rest_0_), channel_id=1, source_target_pairs={{0,8},{4,12},{8,0},{12,4},{1,9},{5,13},{9,1},{13,5},{2,10},{6,14},... | collective-permute-start | bytes 786440 | tf_op jit(solution)/shard_map/ppermute | solution.py:23
  52.6 12.9 %collective-permute-start.7 = (bf16[8,128,128]{2,1,0:T(8,128)(2,1)S(1)}, bf16[8,128,128]{2,1,0:T(8,128)(2,1)S(1)}, u32[]{:S(2)}, u32[]{:S(2)}) collective-permute-start(bf16[8,128,128]{2,1,0:T(8,128)(2,1)S(1)} %shard_map.78.rest_0_), channel_id=1, source_target_pairs={{0,4},{4,0},{8,12},{12,8},{1,5},{5,1},{9,13},{13,9},{2,6},{6,2},{1... | collective-permute-start | bytes 786440 | tf_op jit(solution)/shard_map/ppermute | solution.py:23
  62.7 6.4 %collective-permute-start.9 = (bf16[8,128,128]{2,1,0:T(8,128)(2,1)S(1)}, bf16[8,128,128]{2,1,0:T(8,128)(2,1)S(1)}, u32[]{:S(2)}, u32[]{:S(2)}) collective-permute-start(bf16[8,128,128]{2,1,0:T(8,128)(2,1)S(1)} %collective-permute-done.8.rest_2_), channel_id=1, source_target_pairs={{0,4},{4,0},{8,12},{12,8},{1,5},{5,1},{9,13},{13,9},{2,6},{6,2},{1... | collective-permute-start | bytes 786440 | tf_op jit(solution)/shard_map/ppermute | solution.py:23
  62.7 9.9 %collective-permute-start.10 = (bf16[8,128,128]{2,1,0:T(8,128)(2,1)S(1)}, bf16[8,128,128]{2,1,0:T(8,128)(2,1)S(1)}, u32[]{:S(2)}, u32[]{:S(2)}) collective-permute-start(bf16[8,128,128]{2,1,0:T(8,128)(2,1)S(1)} %shard_map.78.rest_0_), channel_id=1, source_target_pairs={{0,2},{2,0},{1,3},{3,1},{4,6},{6,4},{5,7},{7,5},{8,10},{10,8},{9,1... | collective-permute-start | bytes 786440 | tf_op jit(solution)/shard_map/ppermute | solution.py:23
  64.2 13.7 %collective-permute-start.12 = (bf16[8,128,128]{2,1,0:T(8,128)(2,1)S(1)}, bf16[8,128,128]{2,1,0:T(8,128)(2,1)S(1)}, u32[]{:S(2)}, u32[]{:S(2)}) collective-permute-start(bf16[8,128,128]{2,1,0:T(8,128)(2,1)S(1)} %collective-permute-done.8.rest_2_), channel_id=1, source_target_pairs={{0,2},{2,0},{1,3},{3,1},{4,6},{6,4},{5,7},{7,5},{8,10},{10,8},{9,1... | collective-permute-start | bytes 786440 | tf_op jit(solution)/shard_map/ppermute | solution.py:23
  65.4 12.5 %collective-permute-start.11 = (bf16[8,128,128]{2,1,0:T(8,128)(2,1)S(1)}, bf16[8,128,128]{2,1,0:T(8,128)(2,1)S(1)}, u32[]{:S(2)}, u32[]{:S(2)}) collective-permute-start(bf16[8,128,128]{2,1,0:T(8,128)(2,1)S(1)} %collective-permute-done.7.rest_1_), channel_id=1, source_target_pairs={{0,2},{2,0},{1,3},{3,1},{4,6},{6,4},{5,7},{7,5},{8,10},{10,8},{9,1... | collective-permute-start | bytes 786440 | tf_op jit(solution)/shard_map/ppermute | solution.py:23
  69.1 11.7 %collective-permute-start.13 = (bf16[8,128,128]{2,1,0:T(8,128)(2,1)S(1)}, bf16[8,128,128]{2,1,0:T(8,128)(2,1)S(1)}, u32[]{:S(2)}, u32[]{:S(2)}) collective-permute-start(bf16[8,128,128]{2,1,0:T(8,128)(2,1)S(1)} %collective-permute-done.9.rest_3_), channel_id=1, source_target_pairs={{0,2},{2,0},{1,3},{3,1},{4,6},{6,4},{5,7},{7,5},{8,10},{10,8},{9,1... | collective-permute-start | bytes 786440 | tf_op jit(solution)/shard_map/ppermute | solution.py:23

commit v2 on v0

--- a/solution.py
+++ b/solution.py
@@ -1,10 +1,476 @@
+import functools
+import math
+
 import jax
 import jax.numpy as jnp
 from jax import lax
+from jax.experimental import pallas as pl
+from jax.experimental.pallas import tpu as pltpu
 from jax.sharding import PartitionSpec as P
 
-
-def on_device(volume, projector, slot_ray, slot_pixel, sinogram, weight_index, weight_table):
+FULL = 32700.0
+UNROLL = 4
+VMEM = pl.BlockSpec(memory_space=pltpu.VMEM)
+SMEM = pl.BlockSpec(memory_space=pltpu.SMEM)
+HBM = pl.BlockSpec(memory_space=pltpu.HBM)
+ANY = pl.BlockSpec(memory_space=pl.ANY)
+QUICK = pl.CostEstimate(flops=1, bytes_accessed=1, transcendentals=0)
+PARAMS = pltpu.CompilerParams(vmem_limit_bytes=24 * 2**20)
+
+
+def round_up(value, step):
+    return -(-value // step) * step
+
+
+def swap(value, axis, bits):
+    size = lax.axis_size(axis)
+    return lax.ppermute(value, axis, [(i, i ^ bits) for i in range(size)])
+
+
+def pack(tile, out_ref, levels_ref, t):
+    rows = tile.shape[0]
+    top = jnp.maximum(jnp.max(jnp.abs(tile), axis=0, keepdims=True), 1e-30)
+    level = jnp.ceil(jnp.log2(top))
+    out_ref[t * rows : (t + 1) * rows, :] = (
+        jnp.round(tile * (FULL * jnp.exp2(-level))).astype(jnp.int32).astype(jnp.int16)
+    )
+    levels_ref[t : t + 1, :] = level
+
+
+def unpack(ref, scale, t, rows):
+    block = ref[t * rows : (t + 1) * rows, :]
+    return block.astype(jnp.int32).astype(jnp.float32) * scale[t : t + 1, :]
+
+
+def scales(ref, tiles, rows):
+    raw = ref[tiles * rows :, :].astype(jnp.int32).astype(jnp.float32)
+    return jnp.exp2(raw) * (1.0 / FULL)
+
+
+def payload_of(tiles, rows, slices):
+    return jax.ShapeDtypeStruct((tiles * rows + round_up(tiles, 16), slices), jnp.int16)
+
+
+def split(value, size):
+    if size & (size - 1) == 0:
+        return lax.shift_right_logical(value, size.bit_length() - 1), value & (size - 1)
+    return lax.div(value, size), lax.rem(value, size)
+
+
+def cell_of(ray, zi, xi, tiles, outers, inners):
+    owner, tile = split(ray, tiles)
+    inner, outer = split(owner, outers)
+    return ((outer ^ xi) * inners + (inner ^ zi)) * tiles + tile
+
+
+def list_slots(cell_ref, tiles, groups, slot_list):
+    slots = cell_ref.shape[0]
+
+    def look(s, count):
+        slot_list[count] = s
+        cell = cell_ref[s]
+        hit = jnp.bool_(False)
+        for group in groups:
+            hit = hit | ((cell >= group * tiles) & (cell < (group + 1) * tiles))
+        return count + hit.astype(jnp.int32)
+
+    return lax.fori_loop(0, slots, look, jnp.int32(0), unroll=4)
+
+
+def project(count, base, spare, slot_list, cell_ref, pixel_ref, projector_ref, volume_ref, total):
+    per_slot = projector_ref.shape[1]
+
+    @pl.loop(0, (count + UNROLL - 1) // UNROLL)
+    def _(i):
+        parts, places = [], []
+        for u in range(UNROLL):
+            at = i * UNROLL + u
+            real = at < count
+            s = jnp.where(real, slot_list[at], 0)
+            left = jnp.concatenate([projector_ref[s, g] for g in range(per_slot)], axis=1)
+            right = jnp.concatenate([volume_ref[pixel_ref[g, s]] for g in range(per_slot)], axis=0)
+            parts.append(jnp.dot(left, right, preferred_element_type=jnp.float32))
+            places.append(jnp.where(real, cell_ref[s] - base, spare))
+        for place, part in zip(places, parts):
+            total[place] += part
+
+
+def send_out(total, base, tiles, arrived, send, levels):
+    rows = total.shape[1]
+    levels[...] = jnp.zeros_like(levels)
+    factors = [scales(ref, tiles, rows) for ref in arrived]
+    for t in range(tiles):
+        tile = total[base + t]
+        for ref, factor in zip(arrived, factors):
+            tile = tile + unpack(ref, factor, t, rows)
+        pack(tile, send, levels, t)
+    send[tiles * rows :, :] = levels[...].astype(jnp.int32).astype(jnp.int16)
+
+
+def first_kernel(
+    sizes, group, pos_ref, ray_hbm, pixel_hbm, projector_hbm, volume_hbm,
+    send, projector_ref, volume_ref, cell_ref, ray_ref, pixel_ref, slot_list, total, levels, sems,
+):
+    outers, inners, tiles = sizes
+    pairs = [
+        (ray_hbm, ray_ref),
+        (projector_hbm, projector_ref),
+        (volume_hbm, volume_ref),
+        (pixel_hbm, pixel_ref),
+    ]
+    copies = [
+        pltpu.make_async_copy(source, target, sems.at[i]) for i, (source, target) in enumerate(pairs)
+    ]
+    for copy in copies:
+        copy.start()
+    total[...] = jnp.zeros_like(total)
+    copies[0].wait()
+    zi, xi = pos_ref[0], pos_ref[1]
+
+    @pl.loop(0, ray_ref.shape[0], unroll=4)
+    def _(s):
+        cell_ref[s] = cell_of(ray_ref[s], zi, xi, tiles, outers, inners)
+
+    count = list_slots(cell_ref, tiles, [group], slot_list)
+    for copy in copies[1:]:
+        copy.wait()
+    project(
+        count, group * tiles, tiles, slot_list, cell_ref, pixel_ref, projector_ref, volume_ref, total
+    )
+    send_out(total, 0, tiles, [], send, levels)
+
+
+def hold(value):
+    return pltpu.with_memory_space_constraint(value, pltpu.HBM)
+
+
+def first_send(pos, slot_ray, pixel, projector, volume, sizes, group):
+    slots, per_slot, rows, cols = projector.shape
+    tiles = sizes[2]
+    slices = volume.shape[2]
+    return pl.pallas_call(
+        functools.partial(first_kernel, sizes, group),
+        in_specs=[SMEM, HBM, HBM, HBM, HBM],
+        out_specs=[VMEM, VMEM, VMEM, SMEM],
+        out_shape=[
+            payload_of(tiles, rows, slices),
+            jax.ShapeDtypeStruct(projector.shape, projector.dtype),
+            jax.ShapeDtypeStruct(volume.shape, volume.dtype),
+            jax.ShapeDtypeStruct(slot_ray.shape, jnp.int32),
+        ],
+        scratch_shapes=[
+            pltpu.SMEM(slot_ray.shape, jnp.int32),
+            pltpu.SMEM(pixel.shape, jnp.int32),
+            pltpu.SMEM((slots + UNROLL,), jnp.int32),
+            pltpu.VMEM((tiles + 1, rows, slices), jnp.float32),
+            pltpu.VMEM((round_up(tiles, 16), slices), jnp.float32),
+            pltpu.SemaphoreType.DMA((4,)),
+        ],
+        compiler_params=PARAMS,
+        cost_estimate=QUICK,
+    )(pos, hold(slot_ray), hold(pixel), hold(projector), hold(volume))
+
+
+def next_kernel(
+    tiles, group, count, cell_ref, pixel_ref, projector_ref, volume_ref, after, *rest
+):
+    arrived, (send, slot_list, total, levels) = rest[:count], rest[count:]
+    total[...] = jnp.zeros_like(total)
+    count = list_slots(cell_ref, tiles, [group], slot_list)
+    project(
+        count, group * tiles, tiles, slot_list, cell_ref, pixel_ref, projector_ref, volume_ref, total
+    )
+    send_out(total, 0, tiles, arrived, send, levels)
+
+
+def next_send(cells, pixel, projector, volume, tiles, group, arrived, after):
+    slots, per_slot, rows, cols = projector.shape
+    slices = volume.shape[2]
+    return pl.pallas_call(
+        functools.partial(next_kernel, tiles, group, len(arrived)),
+        in_specs=[SMEM, SMEM, VMEM, VMEM, ANY] + [VMEM] * len(arrived),
+        out_specs=VMEM,
+        out_shape=payload_of(tiles, rows, slices),
+        scratch_shapes=[
+            pltpu.SMEM((slots + UNROLL,), jnp.int32),
+            pltpu.VMEM((tiles + 1, rows, slices), jnp.float32),
+            pltpu.VMEM((round_up(tiles, 16), slices), jnp.float32),
+        ],
+        compiler_params=PARAMS,
+        cost_estimate=QUICK,
+    )(cells, pixel, projector, volume, after, *arrived)
+
+
+def own_kernel(
+    inners, tiles, cell_ref, pixel_ref, projector_ref, volume_ref, after, own_ref, slot_list
+):
+    own_ref[...] = jnp.zeros_like(own_ref)
+    count = list_slots(cell_ref, inners * tiles, [0], slot_list)
+    project(
+        count, 0, inners * tiles, slot_list, cell_ref, pixel_ref, projector_ref, volume_ref, own_ref
+    )
+
+
+def own_sums(cells, pixel, projector, volume, inners, tiles, after):
+    slots, per_slot, rows, cols = projector.shape
+    slices = volume.shape[2]
+    return pl.pallas_call(
+        functools.partial(own_kernel, inners, tiles),
+        in_specs=[SMEM, SMEM, VMEM, VMEM, ANY],
+        out_specs=VMEM,
+        out_shape=jax.ShapeDtypeStruct((inners * tiles + 1, rows, slices), jnp.float32),
+        scratch_shapes=[pltpu.SMEM((slots + UNROLL,), jnp.int32)],
+        compiler_params=PARAMS,
+        cost_estimate=QUICK,
+    )(cells, pixel, projector, volume, after)
+
+
+def combine_kernel(k, tiles, count, own_ref, after, *rest):
+    arrived, (out_ref, levels) = rest[:count], rest[count:]
+    send_out(own_ref, k * tiles, tiles, arrived, out_ref, levels)
+
+
+def combine(own, k, tiles, arrived, after):
+    _, rows, slices = own.shape
+    count = len(arrived)
+    return pl.pallas_call(
+        functools.partial(combine_kernel, k, tiles, count),
+        in_specs=[VMEM, ANY] + [VMEM] * count,
+        out_specs=VMEM,
+        out_shape=payload_of(tiles, rows, slices),
+        scratch_shapes=[pltpu.VMEM((round_up(tiles, 16), slices), jnp.float32)],
+        compiler_params=PARAMS,
+        cost_estimate=QUICK,
+    )(own, after, *arrived)
+
+
+def weight_kernel(table_ref, index_ref, after, out_ref):
+    looked = jnp.zeros(index_ref.shape, jnp.float32)
+    for c in range(table_ref.shape[0]):
+        looked = jnp.where(index_ref[...] == c, table_ref[c], looked)
+    for t in range(index_ref.shape[0]):
+        wide = jnp.broadcast_to(looked[t : t + 1, :], (out_ref.shape[2], out_ref.shape[1]))
+        out_ref[t] = wide.T.astype(jnp.bfloat16)
+
+
+def ray_weights(table, index, slices, after):
+    tiles, rows = index.shape
+    return pl.pallas_call(
+        weight_kernel,
+        in_specs=[SMEM, VMEM, ANY],
+        out_specs=VMEM,
+        out_shape=jax.ShapeDtypeStruct((tiles, rows, slices), jnp.bfloat16),
+        compiler_params=PARAMS,
+        cost_estimate=QUICK,
+    )(table.astype(jnp.float32), index, after)
+
+
+def residual_kernel(count, own_ref, sinogram_ref, weight_ref, *rest):
+    arrived, out_ref = rest[:count], rest[count]
+    tiles, rows, _ = sinogram_ref.shape
+    factors = [scales(ref, tiles, rows) for ref in arrived]
+    for t in range(tiles):
+        tile = own_ref[t]
+        for ref, factor in zip(arrived, factors):
+            tile = tile + unpack(ref, factor, t, rows)
+        gap = sinogram_ref[t].astype(jnp.float32) - tile
+        out_ref[t] = (weight_ref[t].astype(jnp.float32) * gap).astype(jnp.bfloat16)
+
+
+def residual_of(own, sinogram, weights, arrived):
+    return pl.pallas_call(
+        functools.partial(residual_kernel, len(arrived)),
+        in_specs=[VMEM, VMEM, VMEM] + [VMEM] * len(arrived),
+        out_specs=VMEM,
+        out_shape=jax.ShapeDtypeStruct(sinogram.shape, jnp.bfloat16),
+        compiler_params=PARAMS,
+        cost_estimate=QUICK,
+    )(own, sinogram, weights, *arrived)
+
+
+def column_kernel(pixel_ref, projector_ref, after, out_ref):
+    slots, per_slot, rows, cols = projector_ref.shape
+    out_ref[...] = jnp.zeros_like(out_ref)
+
+    @pl.loop(0, slots)
+    def _(s):
+        for g in range(per_slot):
+            column = jnp.sum(projector_ref[s, g].astype(jnp.float32), axis=0, keepdims=True)
+            out_ref[pixel_ref[g, s]] += column
+
+
+def column_sums(pixel, projector, patch_tiles, after):
+    slots, per_slot, rows, cols = projector.shape
+    return pl.pallas_call(
+        column_kernel,
+        in_specs=[SMEM, VMEM, ANY],
+        out_specs=VMEM,
+        out_shape=jax.ShapeDtypeStruct((patch_tiles, 1, cols), jnp.float32),
+        compiler_params=PARAMS,
+        cost_estimate=QUICK,
+    )(pixel, projector, after)
+
+
+def spread_kernel(groups, begin, cell_ref, pixel_ref, projector_ref, *rest):
+    if not begin:
+        before, rest = rest[0], rest[1:]
+    chunks, (total, slot_list, held) = rest[: len(groups)], rest[len(groups) :]
+    slots, per_slot, rows, cols = projector_ref.shape
+    tiles = chunks[0].shape[0]
+    patch_tiles = total.shape[0] - 1
+    for group, chunk in zip(groups, chunks):
+        held[group * tiles : (group + 1) * tiles] = chunk[...]
+    if begin:
+        total[...] = jnp.zeros_like(total)
+    else:
+        total[...] = before[...]
+    count = list_slots(cell_ref, tiles, groups, slot_list)
+
+    @pl.loop(0, (count + 1) // 2)
+    def _(i):
+        parts, places = [], []
+        for u in range(2):
+            real = i * 2 + u < count
+            s = jnp.where(real, slot_list[i * 2 + u], slot_list[0])
+            right = jnp.concatenate([projector_ref[s, g] for g in range(per_slot)], axis=1)
+            parts.append(
+                lax.dot_general(
+                    held[cell_ref[s]], right, (((0,), (0,)), ((), ())), preferred_element_type=jnp.float32
+                )
+            )
+            places.append([jnp.where(real, pixel_ref[g, s], patch_tiles) for g in range(per_slot)])
+        for part, place in zip(parts, places):
+            for g in range(per_slot):
+                total[place[g]] += part[:, g * cols : (g + 1) * cols]
+
+
+def spread(cells, pixel, projector, all_groups, groups, chunks, patch_tiles, before):
+    slots, per_slot, rows, cols = projector.shape
+    tiles, _, slices = chunks[0].shape
+    begin = before is None
+    return pl.pallas_call(
+        functools.partial(spread_kernel, groups, begin),
+        in_specs=[SMEM, SMEM, VMEM] + [VMEM] * (len(chunks) + (not begin)),
+        out_specs=VMEM,
+        out_shape=jax.ShapeDtypeStruct((patch_tiles + 1, slices, cols), jnp.float32),
+        scratch_shapes=[
+            pltpu.SMEM((slots + UNROLL,), jnp.int32),
+            pltpu.VMEM((all_groups * tiles, rows, slices), jnp.bfloat16),
+        ],
+        compiler_params=PARAMS,
+        cost_estimate=QUICK,
+    )(cells, pixel, projector, *([] if begin else [before]), *chunks)
+
+
+def update_kernel(volume_ref, column_ref, total_ref, out_ref):
+    for q in range(out_ref.shape[0]):
+        out_ref[q] = volume_ref[q].astype(jnp.float32) + (total_ref[q] / column_ref[q]).T
+
+
+def update(volume, columns, total):
+    return pl.pallas_call(
+        update_kernel,
+        in_specs=[VMEM, VMEM, VMEM],
+        out_specs=VMEM,
+        out_shape=jax.ShapeDtypeStruct(volume.shape, jnp.float32),
+        compiler_params=PARAMS,
+        cost_estimate=QUICK,
+    )(volume, columns, total)
+
+
+def gate(value, after):
+    return pl.pallas_call(
+        lambda value_ref, after_ref, out_ref: None,
+        in_specs=[VMEM, VMEM],
+        out_specs=VMEM,
+        out_shape=jax.ShapeDtypeStruct(value.shape, value.dtype),
+        input_output_aliases={0: 0},
+        compiler_params=PARAMS,
+        cost_estimate=QUICK,
+    )(value, after)
+
+
+def dense_plan(volume, projector, slot_ray, slot_pixel, sinogram, weight_index, weight_table):
+    inners = lax.axis_size("inner")
+    outers = lax.axis_size("outer")
+    tiles = sinogram.shape[0]
+    patch_tiles, _, slices = volume.shape
+    sizes = (outers, inners, tiles)
+    pos = jnp.stack([lax.axis_index("inner"), lax.axis_index("outer")]).astype(jnp.int32)
+    pixel = slot_pixel.T
+
+    turns = sorted(range(inners), key=lambda k: (bin(k).count("1"), k), reverse=True)
+    far = [k for k in turns if k > 1]
+    others = range(1, outers)
+    arrived = {g: [] for g in range(outers * inners)}
+    sends = []
+    for k in far[:1]:
+        sends += [(j * inners + k, "outer", j) for j in others]
+    if inners > 1:
+        sends += [(j * inners + 1, "inner", 1) for j in others]
+    for k in far[1:]:
+        sends += [(j * inners + k, "outer", j) for j in others]
+    cells = None
+    for group, axis, bits in sends:
+        if cells is None:
+            after, projector, volume, cells = first_send(
+                pos, slot_ray, pixel, projector, volume, sizes, group
+            )
+        else:
+            after = next_send(cells, pixel, projector, volume, tiles, group, [], after)
+        place = group ^ 1 if axis == "inner" else group % inners
+        arrived[place].append(swap(after, axis, bits))
+    after = own = own_sums(cells, pixel, projector, volume, inners, tiles, after)
+    for i, k in enumerate(far):
+        bit = k & -k
+        after = combine(own, k, tiles, arrived[k], after)
+        arrived[k ^ bit].append(swap(after, "inner", bit))
+        if i == 0:
+            for j in others:
+                group = j * inners
+                after = next_send(
+                    cells, pixel, projector, volume, tiles, group, arrived[group], after
+                )
+                arrived[0].append(swap(after, "outer", j))
+    after = combine(own, 1, tiles, [], after)
+    arrived[0].append(swap(after, "inner", 1))
+    weights = ray_weights(weight_table, weight_index, slices, after)
+    columns = column_sums(pixel, projector, patch_tiles, weights)
+    residual = residual_of(own, sinogram, weights, arrived[0])
+
+    turns = turns[::-1]
+    chunks = {0: residual}
+    total = None
+
+    def add(groups):
+        return spread(
+            cells, pixel, projector, outers * inners, groups, [chunks[g] for g in groups], patch_tiles, total
+        )
+
+    bit = inners // 2
+    while bit:
+        chunks[bit] = swap(residual, "inner", bit)
+        bit //= 2
+    for j in others:
+        chunks[j * inners] = swap(residual, "outer", j)
+        chunks[j * inners + 1] = swap(chunks[j * inners], "inner", 1)
+    total = add([0, 1] + [j * inners for j in others])
+    waiting = [j * inners + 1 for j in others]
+    for k in turns[2:]:
+        chunks[k] = gate(chunks[k], total)
+        bit = (k & -k) // 2
+        while bit:
+            chunks[k ^ bit] = swap(chunks[k], "inner", bit)
+            bit //= 2
+        for j in others:
+            chunks[j * inners + k] = swap(chunks[k], "outer", j)
+        total = add([k] + waiting)
+        waiting = [j * inners + k for j in others]
+    total = add(waiting)
+    return update(volume, columns, total)
+
+
+def slot_plan(volume, projector, slot_ray, slot_pixel, sinogram, weight_index, weight_table):
     inners = lax.axis_size("inner")
     outers = lax.axis_size("outer")
     slot_count = projector.shape[0]
@@ -77,14 +543,14 @@
     )
     slot_residual = returned.reshape(cell_count, tile_rows, slice_count)[position]
     owners = jnp.arange(patch_tiles)
-    backward = jnp.zeros((patch_tiles, tile_cols, slice_count), jnp.float32)
+    backward_sum = jnp.zeros((patch_tiles, tile_cols, slice_count), jnp.float32)
     column_sum = jnp.zeros((patch_tiles, tile_cols), jnp.float32)
     for column in range(per_slot):
         member = (owners[:, None] == slot_pixel[None, :, column]).astype(jnp.float32)
         spread = jnp.einsum(
             "srp,src->spc", projector[:, column], slot_residual, preferred_element_type=jnp.float32
         )
-        backward = backward + jnp.einsum(
+        backward_sum = backward_sum + jnp.einsum(
             "ts,spc->tpc", member, spread, precision=lax.Precision.HIGHEST
         )
         column_sum = column_sum + jnp.dot(
@@ -92,7 +558,16 @@
             jnp.sum(projector[:, column], axis=1, dtype=jnp.float32),
             precision=lax.Precision.HIGHEST,
         )
-    return volume.astype(jnp.float32) + backward / column_sum[:, :, None]
+    return volume.astype(jnp.float32) + backward_sum / column_sum[:, :, None]
+
+
+def on_device(volume, projector, slot_ray, slot_pixel, sinogram, weight_index, weight_table):
+    inners = lax.axis_size("inner")
+    outers = lax.axis_size("outer")
+    capacity = 2 * slot_ray.shape[0] // inners
+    powers = inners & (inners - 1) == 0 and outers & (outers - 1) == 0 and inners > 1 < outers
+    plan = dense_plan if powers and sinogram.shape[0] * outers <= capacity else slot_plan
+    return plan(volume, projector, slot_ray, slot_pixel, sinogram, weight_index, weight_table)
 
 
 def solution(mesh):

time: 269 us -> 69.4 us (0.26)
  waiting for transfers between devices: 154 us -> 28.5 us
  matrix products: 36.8 us -> 0 us
  local copies, waits for them, and re-layouts: 31 us -> 0.02 us
  Pallas kernels: 0 us -> 21.5 us
  between operations: 13.6 us -> 0.17 us
  blocking collectives: 8.74 us -> 0 us
  other arithmetic: 7.14 us -> 0.08 us
    all_to_all x3 -> x0, waiting for transfers between devices: 135 us -> none  [the longest x1 91.7 us: on_device(): lax.all_to_all(outgoing.reshape(inners, capacity, tile_rows, slice_count)...]
    dot_general x18 -> x0, matrix products: 36.8 us -> none  [the longest x4 13.9 us: on_device(): jnp.einsum('srp,spc->src', projector[:, column], pixels, preferred_elemen...]
    ppermute x0 -> x14, waiting for transfers between devices: none -> 28.5 us  [swap(): return lax.ppermute(value, axis, [(i, i ^ bits) for i in range(size)])]
    pallas_call x0 -> x18, Pallas kernels: none -> 21.5 us  [the longest x4 7.94 us: spread(): pl.pallas_call(functools.partial(spread_kernel, groups, begin), in_specs=...]
    reduce_scatter x1 -> x0, waiting for transfers between devices: 19.3 us -> none  [on_device(): lax.psum_scatter(block_sums, 'outer', scatter_dimension=0, tiled=True)]
    ppermute x0 -> x14, starting transfers between devices: none -> 18.6 us  [swap(): return lax.ppermute(value, axis, [(i, i ^ bits) for i in range(size)])]
    all_to_all x3 -> x0, starting transfers between devices: 16 us -> none  [the longest x1 6.32 us: on_device(): lax.all_to_all(labels.reshape(inners, capacity), 'inner', split_axis=0, c...]
    dot_general x4 -> x0, local copies, waits for them, and re-layouts: 10.7 us -> none  [on_device(): jnp.einsum('srp,src->spc', projector[:, column], slot_residual, preferred...]
  transfers between devices with their start and end apart: 4 -> 14, of which waited for: 3 -> 12; matrix products, arithmetic and copies ran while one was open for 13% -> 0% of each run, Pallas kernels for 0% -> 21%
where the time goes in v2:
time: 69.4 us; the launch traced here: 68.8 us
  waiting for transfers between devices  28.5 us (41%)
  Pallas kernels  21.5 us (31%)
  starting transfers between devices  18.6 us (27%)
    ppermute x14, waiting for transfers between devices, swap(): return lax.ppermute(value, axis, [(i, i ^ bits) for i in range(size)])  28.5 us
    ppermute x14, starting transfers between devices, swap(): return lax.ppermute(value, axis, [(i, i ^ bits) for i in range(size)])  18.6 us
    pallas_call x4, Pallas kernels, spread(): pl.pallas_call(functools.partial(spread_kernel, groups, begin), in_specs=...  7.94 us
    pallas_call x1, Pallas kernels, first_send(): pl.pallas_call(functools.partial(first_kernel, sizes, group), in_specs=[S...  3.97 us
    pallas_call x3, Pallas kernels, next_send(): pl.pallas_call(functools.partial(next_kernel, tiles, group, len(arrived))...  3.44 us
    pallas_call x1, Pallas kernels, own_sums(): pl.pallas_call(functools.partial(own_kernel, inners, tiles), in_specs=[SM...  2 us
    pallas_call x1, Pallas kernels, column_sums(): pl.pallas_call(column_kernel, in_specs=[SMEM, VMEM, ANY], out_specs=VMEM,...  1.68 us
  transfers between devices with their start and end apart: 14, of which 12 were waited for; matrix products, arithmetic and copies ran while one was open for 0% of the time, Pallas kernels for 21%

profile of v2, /device:TPU:0, one launch (start us, length us, event | category | flops | bytes accessed | tf_op | source)
XLA Modules:
  0.0 68.8 jit_solution(18147574398692619550)
XLA Ops:
  0.0 0.0 copy-start.1
  0.0 0.1 pad_add_fusion.pos_ref
  0.1 4.0 %shard_map.73 = (s16[1040,128]{1,0:T(8,128)(2,1)S(1)}, bf16[32,4,128,128]{3,2,1,0:T(8,128)(2,1)S(1)}, bf16[6,128,128]{2,1,0:T(8,128)(2,1)S(1)}, s32[32]{0:T(128)S(1)}) custom-call(s32[2]{0:T(128)S(1)} %pad_add_fusion.pos_ref, s32[32]{0:T(128)} %ray_hbm.1, s32[4,32]{1,0:T(4,128)} %bitcast.3, bf16[32,4,128,128]{3,2,1,0:T(8,128)(2,1)} %projector_hbm.1, ...), custom_call_target="tpu_custom_call" | custom-call | flops 1 | bytes 1 | tf_op jit(solution)/shard_map/pallas_call | solution.py:151
  4.1 3.3 %collective-permute-start = (s16[1040,128]{1,0:T(8,128)(2,1)S(1)}, s16[1040,128]{1,0:T(8,128)(2,1)S(1)}, u32[]{:S(2)}, u32[]{:S(2)}) collective-permute-start(s16[1040,128]{1,0:T(8,128)(2,1)S(1)} %get-tuple-element.12.after), channel_id=1, source_target_pairs={{0,2},{2,0},{1,3},{3,1},{4,6},{6,4},{5,7},{7,5},{8,10},{10,8},{9,1... | collective-permute-start | bytes 798728 | tf_op jit(solution)/shard_map/ppermute | solution.py:27
  7.4 0.0 copy-done.1
  7.4 1.1 %shard_map.74.after = s16[1040,128]{1,0:T(8,128)(2,1)S(1)} custom-call(s32[32]{0:T(128)S(1)} %get-tuple-element.11.cell_ref, s32[4,32]{1,0:T(4,128)S(1)} %bitcast.4, bf16[32,4,128,128]{3,2,1,0:T(8,128)(2,1)S(1)} %get-tuple-element.10.projector_ref, bf16[6,128,128]{2,1,0:T(8,128)(2,1)S(1)} %get-tuple-element.9.volume_ref, ...), custom_call_target="tpu_custom_call" | custom-call | flops 1 | bytes 1 | tf_op jit(solution)/shard_map/pallas_call | solution.py:189
  8.5 1.0 %collective-permute-start.1 = (s16[1040,128]{1,0:T(8,128)(2,1)S(1)}, s16[1040,128]{1,0:T(8,128)(2,1)S(1)}, u32[]{:S(2)}, u32[]{:S(2)}) collective-permute-start(s16[1040,128]{1,0:T(8,128)(2,1)S(1)} %shard_map.74.after), channel_id=1, source_target_pairs={{0,4},{4,0},{8,12},{12,8},{1,5},{5,1},{9,13},{13,9},{2,6},{6,2},{1... | collective-permute-start | bytes 798728 | tf_op jit(solution)/shard_map/ppermute | solution.py:27
  9.5 1.1 %shard_map.75.after = s16[1040,128]{1,0:T(8,128)(2,1)S(1)} custom-call(s32[32]{0:T(128)S(1)} %get-tuple-element.11.cell_ref, s32[4,32]{1,0:T(4,128)S(1)} %bitcast.5, bf16[32,4,128,128]{3,2,1,0:T(8,128)(2,1)S(1)} %get-tuple-element.10.projector_ref, bf16[6,128,128]{2,1,0:T(8,128)(2,1)S(1)} %get-tuple-element.9.volume_ref, s16[1040,128]{1,0:T(8,128)(2,1)S(1)} %shard_map.74.after), custom_call_target="tpu_custom_call" | custom-call | flops 1 | bytes 1 | tf_op jit(solution)/shard_map/pallas_call | solution.py:189
  10.7 0.6 collective-permute-start.2
  11.3 2.0 %shard_map.76.own_ref.after = f32[33,128,128]{2,1,0:T(8,128)S(1)} custom-call(s32[32]{0:T(128)S(1)} %get-tuple-element.11.cell_ref, s32[4,32]{1,0:T(4,128)S(1)} %bitcast.6, bf16[32,4,128,128]{3,2,1,0:T(8,128)(2,1)S(1)} %get-tuple-element.10.projector_ref, bf16[6,128,128]{2,1,0:T(8,128)(2,1)S(1)} %get-tuple-element.9.volume_ref, ...), custom_call_target="tpu_custom_call" | custom-call | flops 1 | bytes 1 | tf_op jit(solution)/shard_map/pallas_call | solution.py:217
  13.3 1.3 %collective-permute-done.rest_0_ = s16[1040,128]{1,0:T(8,128)(2,1)S(1)} collective-permute-done((s16[1040,128]{1,0:T(8,128)(2,1)S(1)}, s16[1040,128]{1,0:T(8,128)(2,1)S(1)}, u32[]{:S(2)}, u32[]{:S(2)}) %collective-permute-start) | collective-permute-done | bytes 266272 | tf_op jit(solution)/shard_map/ppermute | solution.py:27
  14.6 0.2 shard_map.77.after
  14.8 1.1 %collective-permute-start.3 = (s16[1040,128]{1,0:T(8,128)(2,1)S(1)}, s16[1040,128]{1,0:T(8,128)(2,1)S(1)}, u32[]{:S(2)}, u32[]{:S(2)}) collective-permute-start(s16[1040,128]{1,0:T(8,128)(2,1)S(1)} %shard_map.77.after), channel_id=1, source_target_pairs={{0,4},{4,0},{8,12},{12,8},{1,5},{5,1},{9,13},{13,9},{2,6},{6,2},{1... | collective-permute-start | bytes 798728 | tf_op jit(solution)/shard_map/ppermute | solution.py:27
  15.9 1.0 %collective-permute-done.1.rest_0_ = s16[1040,128]{1,0:T(8,128)(2,1)S(1)} collective-permute-done((s16[1040,128]{1,0:T(8,128)(2,1)S(1)}, s16[1040,128]{1,0:T(8,128)(2,1)S(1)}, u32[]{:S(2)}, u32[]{:S(2)}) %collective-permute-start.1) | collective-permute-done | bytes 266272 | tf_op jit(solution)/shard_map/ppermute | solution.py:27
  16.9 1.2 %shard_map.78.after = s16[1040,128]{1,0:T(8,128)(2,1)S(1)} custom-call(s32[32]{0:T(128)S(1)} %get-tuple-element.11.cell_ref, s32[4,32]{1,0:T(4,128)S(1)} %bitcast.7, bf16[32,4,128,128]{3,2,1,0:T(8,128)(2,1)S(1)} %get-tuple-element.10.projector_ref, bf16[6,128,128]{2,1,0:T(8,128)(2,1)S(1)} %get-tuple-element.9.volume_ref, ...), custom_call_target="tpu_custom_call" | custom-call | flops 1 | bytes 1 | tf_op jit(solution)/shard_map/pallas_call | solution.py:189
  18.1 0.0 copy-start.3
  18.1 0.0 copy-start.2
  18.1 0.0 copy-start
  18.1 1.3 %collective-permute-done.2.rest_0_ = s16[1040,128]{1,0:T(8,128)(2,1)S(1)} collective-permute-done((s16[1040,128]{1,0:T(8,128)(2,1)S(1)}, s16[1040,128]{1,0:T(8,128)(2,1)S(1)}, u32[]{:S(2)}, u32[]{:S(2)}) %collective-permute-start.2) | collective-permute-done | bytes 266272 | tf_op jit(solution)/shard_map/ppermute | solution.py:27
  19.5 2.7 %collective-permute-done.3.rest_1_ = s16[1040,128]{1,0:T(8,128)(2,1)S(1)} collective-permute-done((s16[1040,128]{1,0:T(8,128)(2,1)S(1)}, s16[1040,128]{1,0:T(8,128)(2,1)S(1)}, u32[]{:S(2)}, u32[]{:S(2)}) %collective-permute-start.3) | collective-permute-done | bytes 266272 | tf_op jit(solution)/shard_map/ppermute | solution.py:27
  22.1 0.2 shard_map.79.after
  22.4 1.3 %collective-permute-start.4 = (s16[1040,128]{1,0:T(8,128)(2,1)S(1)}, s16[1040,128]{1,0:T(8,128)(2,1)S(1)}, u32[]{:S(2)}, u32[]{:S(2)}) collective-permute-start(s16[1040,128]{1,0:T(8,128)(2,1)S(1)} %shard_map.78.after), channel_id=1, source_target_pairs={{0,2},{2,0},{1,3},{3,1},{4,6},{6,4},{5,7},{7,5},{8,10},{10,8},{9,1... | collective-permute-start | bytes 798728 | tf_op jit(solution)/shard_map/ppermute | solution.py:27
  23.6 0.1 shard_map.80.after
  23.7 1.0 %collective-permute-start.6 = (s16[1040,128]{1,0:T(8,128)(2,1)S(1)}, s16[1040,128]{1,0:T(8,128)(2,1)S(1)}, u32[]{:S(2)}, u32[]{:S(2)}) collective-permute-start(s16[1040,128]{1,0:T(8,128)(2,1)S(1)} %shard_map.80.after), channel_id=1, source_target_pairs={{0,4},{4,0},{8,12},{12,8},{1,5},{5,1},{9,13},{13,9},{2,6},{6,2},{1... | collective-permute-start | bytes 798728 | tf_op jit(solution)/shard_map/ppermute | solution.py:27
  24.8 2.6 %collective-permute-start.5 = (s16[1040,128]{1,0:T(8,128)(2,1)S(1)}, s16[1040,128]{1,0:T(8,128)(2,1)S(1)}, u32[]{:S(2)}, u32[]{:S(2)}) collective-permute-start(s16[1040,128]{1,0:T(8,128)(2,1)S(1)} %shard_map.79.after), channel_id=1, source_target_pairs={{0,8},{4,12},{8,0},{12,4},{1,9},{5,13},{9,1},{13,5},{2,10},{6,14},... | collective-permute-start | bytes 798728 | tf_op jit(solution)/shard_map/ppermute | solution.py:27
  27.3 0.0 copy-done.3
  27.4 0.0 copy-done.2
  27.4 0.7 shard_map.81.after.weight_ref
  28.0 0.8 %collective-permute-done.4.rest_0_ = s16[1040,128]{1,0:T(8,128)(2,1)S(1)} collective-permute-done((s16[1040,128]{1,0:T(8,128)(2,1)S(1)}, s16[1040,128]{1,0:T(8,128)(2,1)S(1)}, u32[]{:S(2)}, u32[]{:S(2)}) %collective-permute-start.4) | collective-permute-done | bytes 266272 | tf_op jit(solution)/shard_map/ppermute | solution.py:27
  28.8 5.7 %collective-permute-done.6.rest_2_ = s16[1040,128]{1,0:T(8,128)(2,1)S(1)} collective-permute-done((s16[1040,128]{1,0:T(8,128)(2,1)S(1)}, s16[1040,128]{1,0:T(8,128)(2,1)S(1)}, u32[]{:S(2)}, u32[]{:S(2)}) %collective-permute-start.6) | collective-permute-done | bytes 266272 | tf_op jit(solution)/shard_map/ppermute | solution.py:27
  34.5 2.2 %collective-permute-done.5.rest_1_ = s16[1040,128]{1,0:T(8,128)(2,1)S(1)} collective-permute-done((s16[1040,128]{1,0:T(8,128)(2,1)S(1)}, s16[1040,128]{1,0:T(8,128)(2,1)S(1)}, u32[]{:S(2)}, u32[]{:S(2)}) %collective-permute-start.5) | collective-permute-done | bytes 266272 | tf_op jit(solution)/shard_map/ppermute | solution.py:27
  36.7 0.0 copy-done
  36.7 0.3 shard_map.83.rest_0_
  37.0 1.1 %collective-permute-start.8 = (bf16[8,128,128]{2,1,0:T(8,128)(2,1)S(1)}, bf16[8,128,128]{2,1,0:T(8,128)(2,1)S(1)}, u32[]{:S(2)}, u32[]{:S(2)}) collective-permute-start(bf16[8,128,128]{2,1,0:T(8,128)(2,1)S(1)} %shard_map.83.rest_0_), channel_id=1, source_target_pairs={{0,2},{2,0},{1,3},{3,1},{4,6},{6,4},{5,7},{7,5},{8,10},{10,8},{9,1... | collective-permute-start | bytes 786440 | tf_op jit(solution)/shard_map/ppermute | solution.py:27
  38.1 1.1 %collective-permute-start.7 = (bf16[8,128,128]{2,1,0:T(8,128)(2,1)S(1)}, bf16[8,128,128]{2,1,0:T(8,128)(2,1)S(1)}, u32[]{:S(2)}, u32[]{:S(2)}) collective-permute-start(bf16[8,128,128]{2,1,0:T(8,128)(2,1)S(1)} %shard_map.83.rest_0_), channel_id=1, source_target_pairs={{0,4},{4,0},{8,12},{12,8},{1,5},{5,1},{9,13},{13,9},{2,6},{6,2},{1... | collective-permute-start | bytes 786440 | tf_op jit(solution)/shard_map/ppermute | solution.py:27
  39.2 2.7 %collective-permute-start.9 = (bf16[8,128,128]{2,1,0:T(8,128)(2,1)S(1)}, bf16[8,128,128]{2,1,0:T(8,128)(2,1)S(1)}, u32[]{:S(2)}, u32[]{:S(2)}) collective-permute-start(bf16[8,128,128]{2,1,0:T(8,128)(2,1)S(1)} %shard_map.83.rest_0_), channel_id=1, source_target_pairs={{0,8},{4,12},{8,0},{12,4},{1,9},{5,13},{9,1},{13,5},{2,10},{6,14},... | collective-permute-start | bytes 786440 | tf_op jit(solution)/shard_map/ppermute | solution.py:27
  41.9 1.5 %collective-permute-done.8.rest_2_ = bf16[8,128,128]{2,1,0:T(8,128)(2,1)S(1)} collective-permute-done((bf16[8,128,128]{2,1,0:T(8,128)(2,1)S(1)}, bf16[8,128,128]{2,1,0:T(8,128)(2,1)S(1)}, u32[]{:S(2)}, u32[]{:S(2)}) %collective-permute-start.8) | collective-permute-done | bytes 262176 | tf_op jit(solution)/shard_map/ppermute | solution.py:27
  43.4 0.3 collective-permute-start.10
  43.7 7.6 %collective-permute-done.7.rest_1_ = bf16[8,128,128]{2,1,0:T(8,128)(2,1)S(1)} collective-permute-done((bf16[8,128,128]{2,1,0:T(8,128)(2,1)S(1)}, bf16[8,128,128]{2,1,0:T(8,128)(2,1)S(1)}, u32[]{:S(2)}, u32[]{:S(2)}) %collective-permute-start.7) | collective-permute-done | bytes 262176 | tf_op jit(solution)/shard_map/ppermute | solution.py:27
  51.2 2.0 %shard_map.84.after_ref.rest_0_ = f32[7,128,128]{2,1,0:T(8,128)S(1)} custom-call(s32[32]{0:T(128)S(1)} %get-tuple-element.11.cell_ref, s32[4,32]{1,0:T(4,128)S(1)} %bitcast.8, bf16[32,4,128,128]{3,2,1,0:T(8,128)(2,1)S(1)} %get-tuple-element.10.projector_ref, bf16[8,128,128]{2,1,0:T(8,128)(2,1)S(1)} %shard_map.83.rest_0_, ...), custom_call_target="tpu_custom_call" | custom-call | flops 1 | bytes 1 | tf_op jit(solution)/shard_map/pallas_call | solution.py:351
  53.2 0.0 collective-permute-done.9.value_ref
  53.2 0.1 collective-permute-start.11
  53.3 1.6 %collective-permute-start.12 = (bf16[8,128,128]{2,1,0:T(8,128)(2,1)S(1)}, bf16[8,128,128]{2,1,0:T(8,128)(2,1)S(1)}, u32[]{:S(2)}, u32[]{:S(2)}) collective-permute-start(bf16[8,128,128]{2,1,0:T(8,128)(2,1)S(1)} %shard_map.85.rest_1_), channel_id=1, source_target_pairs={{0,2},{2,0},{1,3},{3,1},{4,6},{6,4},{5,7},{7,5},{8,10},{10,8},{9,1... | collective-permute-start | bytes 786440 | tf_op jit(solution)/shard_map/ppermute | solution.py:27
  54.9 1.3 %collective-permute-done.10.rest_2_ = bf16[8,128,128]{2,1,0:T(8,128)(2,1)S(1)} collective-permute-done((bf16[8,128,128]{2,1,0:T(8,128)(2,1)S(1)}, bf16[8,128,128]{2,1,0:T(8,128)(2,1)S(1)}, u32[]{:S(2)}, u32[]{:S(2)}) %collective-permute-start.10) | collective-permute-done | bytes 262176 | tf_op jit(solution)/shard_map/ppermute | solution.py:27
  56.2 1.6 %shard_map.86.after_ref.rest_0_ = f32[7,128,128]{2,1,0:T(8,128)S(1)} custom-call(s32[32]{0:T(128)S(1)} %get-tuple-element.11.cell_ref, s32[4,32]{1,0:T(4,128)S(1)} %bitcast.9, bf16[32,4,128,128]{3,2,1,0:T(8,128)(2,1)S(1)} %get-tuple-element.10.projector_ref, f32[7,128,128]{2,1,0:T(8,128)S(1)} %shard_map.84.after_ref.rest_0_, ...), custom_call_target="tpu_custom_call" | custom-call | flops 1 | bytes 1 | tf_op jit(solution)/shard_map/pallas_call | solution.py:351
  57.8 1.8 %collective-permute-done.11.value_ref = bf16[8,128,128]{2,1,0:T(8,128)(2,1)S(1)} collective-permute-done((bf16[8,128,128]{2,1,0:T(8,128)(2,1)S(1)}, bf16[8,128,128]{2,1,0:T(8,128)(2,1)S(1)}, u32[]{:S(2)}, u32[]{:S(2)}) %collective-permute-start.11) | collective-permute-done | bytes 262176 | tf_op jit(solution)/shard_map/ppermute | solution.py:27
  59.7 0.7 %collective-permute-start.13 = (bf16[8,128,128]{2,1,0:T(8,128)(2,1)S(1)}, bf16[8,128,128]{2,1,0:T(8,128)(2,1)S(1)}, u32[]{:S(2)}, u32[]{:S(2)}) collective-permute-start(bf16[8,128,128]{2,1,0:T(8,128)(2,1)S(1)} %shard_map.87.rest_1_), channel_id=1, source_target_pairs={{0,2},{2,0},{1,3},{3,1},{4,6},{6,4},{5,7},{7,5},{8,10},{10,8},{9,1... | collective-permute-start | bytes 786440 | tf_op jit(solution)/shard_map/ppermute | solution.py:27
  60.4 1.7 %shard_map.82.column_ref = f32[6,1,128]{2,1,0:T(1,128)S(1)} custom-call(s32[4,32]{1,0:T(4,128)S(1)} %bitcast.10, bf16[32,4,128,128]{3,2,1,0:T(8,128)(2,1)S(1)} %get-tuple-element.10.projector_ref, bf16[8,128,128]{2,1,0:T(8,128)(2,1)S(1)} %shard_map.81.after.weight_ref), custom_call_target="tpu_custom_call" | custom-call | flops 1 | bytes 1 | tf_op jit(solution)/shard_map/pallas_call | solution.py:304
  62.1 0.0 collective-permute-done.12.rest_2_
  62.1 2.5 %shard_map.88.rest_0_ = f32[7,128,128]{2,1,0:T(8,128)S(1)} custom-call(s32[32]{0:T(128)S(1)} %get-tuple-element.11.cell_ref, s32[4,32]{1,0:T(4,128)S(1)} %bitcast.11, bf16[32,4,128,128]{3,2,1,0:T(8,128)(2,1)S(1)} %get-tuple-element.10.projector_ref, f32[7,128,128]{2,1,0:T(8,128)S(1)} %shard_map.86.after_ref.rest_0_, ...), custom_call_target="tpu_custom_call" | custom-call | flops 1 | bytes 1 | tf_op jit(solution)/shard_map/pallas_call | solution.py:351
  64.6 1.5 %collective-permute-done.13.rest_1_ = bf16[8,128,128]{2,1,0:T(8,128)(2,1)S(1)} collective-permute-done((bf16[8,128,128]{2,1,0:T(8,128)(2,1)S(1)}, bf16[8,128,128]{2,1,0:T(8,128)(2,1)S(1)}, u32[]{:S(2)}, u32[]{:S(2)}) %collective-permute-start.13) | collective-permute-done | bytes 262176 | tf_op jit(solution)/shard_map/ppermute | solution.py:27
  66.1 1.8 %shard_map.89.total_ref = f32[7,128,128]{2,1,0:T(8,128)S(1)} custom-call(s32[32]{0:T(128)S(1)} %get-tuple-element.11.cell_ref, s32[4,32]{1,0:T(4,128)S(1)} %bitcast.12, bf16[32,4,128,128]{3,2,1,0:T(8,128)(2,1)S(1)} %get-tuple-element.10.projector_ref, f32[7,128,128]{2,1,0:T(8,128)S(1)} %shard_map.88.rest_0_, ...), custom_call_target="tpu_custom_call" | custom-call | flops 1 | bytes 1 | tf_op jit(solution)/shard_map/pallas_call | solution.py:351
  67.9 0.9 %shard_map.90 = f32[6,128,128]{2,1,0:T(8,128)} custom-call(bf16[6,128,128]{2,1,0:T(8,128)(2,1)S(1)} %get-tuple-element.9.volume_ref, f32[6,1,128]{2,1,0:T(1,128)S(1)} %shard_map.82.column_ref, f32[7,128,128]{2,1,0:T(8,128)S(1)} %shard_map.89.total_ref), custom_call_target="tpu_custom_call" | custom-call | flops 1 | bytes 1 | tf_op jit(solution)/shard_map/pallas_call | solution.py:371
  (3 shorter events, 0.0 us)
Async XLA Ops:
  0.0 7.4 %copy-start.1 = (s32[32,4]{0,1:T(4,128)S(1)}, s32[32,4]{0,1:T(4,128)}, u32[]{:S(2)}) copy-start(s32[32,4]{0,1:T(4,128)} %param.10) | copy-start | bytes 1540
  4.1 10.5 %collective-permute-start = (s16[1040,128]{1,0:T(8,128)(2,1)S(1)}, s16[1040,128]{1,0:T(8,128)(2,1)S(1)}, u32[]{:S(2)}, u32[]{:S(2)}) collective-permute-start(s16[1040,128]{1,0:T(8,128)(2,1)S(1)} %get-tuple-element.12.after), channel_id=1, source_target_pairs={{0,2},{2,0},{1,3},{3,1},{4,6},{6,4},{5,7},{7,5},{8,10},{10,8},{9,1... | collective-permute-start | bytes 798728 | tf_op jit(solution)/shard_map/ppermute | solution.py:27
  8.5 8.4 %collective-permute-start.1 = (s16[1040,128]{1,0:T(8,128)(2,1)S(1)}, s16[1040,128]{1,0:T(8,128)(2,1)S(1)}, u32[]{:S(2)}, u32[]{:S(2)}) collective-permute-start(s16[1040,128]{1,0:T(8,128)(2,1)S(1)} %shard_map.74.after), channel_id=1, source_target_pairs={{0,4},{4,0},{8,12},{12,8},{1,5},{5,1},{9,13},{13,9},{2,6},{6,2},{1... | collective-permute-start | bytes 798728 | tf_op jit(solution)/shard_map/ppermute | solution.py:27
  10.7 8.8 %collective-permute-start.2 = (s16[1040,128]{1,0:T(8,128)(2,1)S(1)}, s16[1040,128]{1,0:T(8,128)(2,1)S(1)}, u32[]{:S(2)}, u32[]{:S(2)}) collective-permute-start(s16[1040,128]{1,0:T(8,128)(2,1)S(1)} %shard_map.75.after), channel_id=1, source_target_pairs={{0,2},{2,0},{1,3},{3,1},{4,6},{6,4},{5,7},{7,5},{8,10},{10,8},{9,1... | collective-permute-start | bytes 798728 | tf_op jit(solution)/shard_map/ppermute | solution.py:27
  14.8 7.4 %collective-permute-start.3 = (s16[1040,128]{1,0:T(8,128)(2,1)S(1)}, s16[1040,128]{1,0:T(8,128)(2,1)S(1)}, u32[]{:S(2)}, u32[]{:S(2)}) collective-permute-start(s16[1040,128]{1,0:T(8,128)(2,1)S(1)} %shard_map.77.after), channel_id=1, source_target_pairs={{0,4},{4,0},{8,12},{12,8},{1,5},{5,1},{9,13},{13,9},{2,6},{6,2},{1... | collective-permute-start | bytes 798728 | tf_op jit(solution)/shard_map/ppermute | solution.py:27
  18.1 9.2 %copy-start.3 = (bf16[16]{0:T(256)(128)(2,1)S(1)}, bf16[16]{0:T(256)(128)(2,1)}, u32[]{:S(2)}) copy-start(bf16[16]{0:T(256)(128)(2,1)} %param.13) | copy-start | bytes 100
  18.1 9.2 %copy-start.2 = (s32[8,128]{1,0:T(8,128)S(1)}, s32[8,128]{1,0:T(8,128)}, u32[]{:S(2)}) copy-start(s32[8,128]{1,0:T(8,128)} %index_ref.1) | copy-start | bytes 12292
  18.1 18.5 %copy-start = (bf16[8,128,128]{2,1,0:T(8,128)(2,1)S(1)}, bf16[8,128,128]{2,1,0:T(8,128)(2,1)}, u32[]{:S(2)}) copy-start(bf16[8,128,128]{2,1,0:T(8,128)(2,1)} %sinogram_ref.1) | copy-start | bytes 786436
  22.4 6.5 %collective-permute-start.4 = (s16[1040,128]{1,0:T(8,128)(2,1)S(1)}, s16[1040,128]{1,0:T(8,128)(2,1)S(1)}, u32[]{:S(2)}, u32[]{:S(2)}) collective-permute-start(s16[1040,128]{1,0:T(8,128)(2,1)S(1)} %shard_map.78.after), channel_id=1, source_target_pairs={{0,2},{2,0},{1,3},{3,1},{4,6},{6,4},{5,7},{7,5},{8,10},{10,8},{9,1... | collective-permute-start | bytes 798728 | tf_op jit(solution)/shard_map/ppermute | solution.py:27
  23.7 10.8 %collective-permute-start.6 = (s16[1040,128]{1,0:T(8,128)(2,1)S(1)}, s16[1040,128]{1,0:T(8,128)(2,1)S(1)}, u32[]{:S(2)}, u32[]{:S(2)}) collective-permute-start(s16[1040,128]{1,0:T(8,128)(2,1)S(1)} %shard_map.80.after), channel_id=1, source_target_pairs={{0,4},{4,0},{8,12},{12,8},{1,5},{5,1},{9,13},{13,9},{2,6},{6,2},{1... | collective-permute-start | bytes 798728 | tf_op jit(solution)/shard_map/ppermute | solution.py:27
  24.8 11.9 %collective-permute-start.5 = (s16[1040,128]{1,0:T(8,128)(2,1)S(1)}, s16[1040,128]{1,0:T(8,128)(2,1)S(1)}, u32[]{:S(2)}, u32[]{:S(2)}) collective-permute-start(s16[1040,128]{1,0:T(8,128)(2,1)S(1)} %shard_map.79.after), channel_id=1, source_target_pairs={{0,8},{4,12},{8,0},{12,4},{1,9},{5,13},{9,1},{13,5},{2,10},{6,14},... | collective-permute-start | bytes 798728 | tf_op jit(solution)/shard_map/ppermute | solution.py:27
  37.0 6.4 %collective-permute-start.8 = (bf16[8,128,128]{2,1,0:T(8,128)(2,1)S(1)}, bf16[8,128,128]{2,1,0:T(8,128)(2,1)S(1)}, u32[]{:S(2)}, u32[]{:S(2)}) collective-permute-start(bf16[8,128,128]{2,1,0:T(8,128)(2,1)S(1)} %shard_map.83.rest_0_), channel_id=1, source_target_pairs={{0,2},{2,0},{1,3},{3,1},{4,6},{6,4},{5,7},{7,5},{8,10},{10,8},{9,1... | collective-permute-start | bytes 786440 | tf_op jit(solution)/shard_map/ppermute | solution.py:27
  38.1 13.2 %collective-permute-start.7 = (bf16[8,128,128]{2,1,0:T(8,128)(2,1)S(1)}, bf16[8,128,128]{2,1,0:T(8,128)(2,1)S(1)}, u32[]{:S(2)}, u32[]{:S(2)}) collective-permute-start(bf16[8,128,128]{2,1,0:T(8,128)(2,1)S(1)} %shard_map.83.rest_0_), channel_id=1, source_target_pairs={{0,4},{4,0},{8,12},{12,8},{1,5},{5,1},{9,13},{13,9},{2,6},{6,2},{1... | collective-permute-start | bytes 786440 | tf_op jit(solution)/shard_map/ppermute | solution.py:27
  39.2 14.0 %collective-permute-start.9 = (bf16[8,128,128]{2,1,0:T(8,128)(2,1)S(1)}, bf16[8,128,128]{2,1,0:T(8,128)(2,1)S(1)}, u32[]{:S(2)}, u32[]{:S(2)}) collective-permute-start(bf16[8,128,128]{2,1,0:T(8,128)(2,1)S(1)} %shard_map.83.rest_0_), channel_id=1, source_target_pairs={{0,8},{4,12},{8,0},{12,4},{1,9},{5,13},{9,1},{13,5},{2,10},{6,14},... | collective-permute-start | bytes 786440 | tf_op jit(solution)/shard_map/ppermute | solution.py:27
  43.4 12.8 %collective-permute-start.10 = (bf16[8,128,128]{2,1,0:T(8,128)(2,1)S(1)}, bf16[8,128,128]{2,1,0:T(8,128)(2,1)S(1)}, u32[]{:S(2)}, u32[]{:S(2)}) collective-permute-start(bf16[8,128,128]{2,1,0:T(8,128)(2,1)S(1)} %collective-permute-done.8.rest_2_), channel_id=1, source_target_pairs={{0,4},{4,0},{8,12},{12,8},{1,5},{5,1},{9,13},{13,9},{2,6},{6,2},{1... | collective-permute-start | bytes 786440 | tf_op jit(solution)/shard_map/ppermute | solution.py:27
  53.2 6.4 %collective-permute-start.11 = (bf16[8,128,128]{2,1,0:T(8,128)(2,1)S(1)}, bf16[8,128,128]{2,1,0:T(8,128)(2,1)S(1)}, u32[]{:S(2)}, u32[]{:S(2)}) collective-permute-start(bf16[8,128,128]{2,1,0:T(8,128)(2,1)S(1)} %shard_map.85.rest_1_), channel_id=1, source_target_pairs={{0,4},{4,0},{8,12},{12,8},{1,5},{5,1},{9,13},{13,9},{2,6},{6,2},{1... | collective-permute-start | bytes 786440 | tf_op jit(solution)/shard_map/ppermute | solution.py:27
  53.3 8.7 %collective-permute-start.12 = (bf16[8,128,128]{2,1,0:T(8,128)(2,1)S(1)}, bf16[8,128,128]{2,1,0:T(8,128)(2,1)S(1)}, u32[]{:S(2)}, u32[]{:S(2)}) collective-permute-start(bf16[8,128,128]{2,1,0:T(8,128)(2,1)S(1)} %shard_map.85.rest_1_), channel_id=1, source_target_pairs={{0,2},{2,0},{1,3},{3,1},{4,6},{6,4},{5,7},{7,5},{8,10},{10,8},{9,1... | collective-permute-start | bytes 786440 | tf_op jit(solution)/shard_map/ppermute | solution.py:27
  59.7 6.4 %collective-permute-start.13 = (bf16[8,128,128]{2,1,0:T(8,128)(2,1)S(1)}, bf16[8,128,128]{2,1,0:T(8,128)(2,1)S(1)}, u32[]{:S(2)}, u32[]{:S(2)}) collective-permute-start(bf16[8,128,128]{2,1,0:T(8,128)(2,1)S(1)} %shard_map.87.rest_1_), channel_id=1, source_target_pairs={{0,2},{2,0},{1,3},{3,1},{4,6},{6,4},{5,7},{7,5},{8,10},{10,8},{9,1... | collective-permute-start | bytes 786440 | tf_op jit(solution)/shard_map/ppermute | solution.py:27

commit v3 on v2

v3 whole, which is shorter than its diff:
```python
import functools
import math

import jax
import jax.numpy as jnp
from jax import lax
from jax.experimental import pallas as pl
from jax.experimental.pallas import tpu as pltpu
from jax.sharding import PartitionSpec as P

FULL = 32700.0
UNROLL = 4
LATER = True
EARLY = False
VMEM = pl.BlockSpec(memory_space=pltpu.VMEM)
SMEM = pl.BlockSpec(memory_space=pltpu.SMEM)
HBM = pl.BlockSpec(memory_space=pltpu.HBM)
ANY = pl.BlockSpec(memory_space=pl.ANY)
QUICK = pl.CostEstimate(flops=1, bytes_accessed=1, transcendentals=0)
PARAMS = pltpu.CompilerParams(vmem_limit_bytes=24 * 2**20)


def round_up(value, step):
    return -(-value // step) * step


def swap(value, axis, bits):
    size = lax.axis_size(axis)
    return lax.ppermute(value, axis, [(i, i ^ bits) for i in range(size)])


def pack(tile, out_ref, levels_ref, t):
    rows = tile.shape[0]
    top = jnp.maximum(jnp.max(jnp.abs(tile), axis=0, keepdims=True), 1e-30)
    level = jnp.ceil(jnp.log2(top))
    out_ref[t * rows : (t + 1) * rows, :] = (
        jnp.round(tile * (FULL * jnp.exp2(-level))).astype(jnp.int32).astype(jnp.int16)
    )
    levels_ref[t : t + 1, :] = level


def unpack(ref, scale, t, rows):
    block = ref[t * rows : (t + 1) * rows, :]
    return block.astype(jnp.int32).astype(jnp.float32) * scale[t : t + 1, :]


def scales(ref, tiles, rows):
    raw = ref[tiles * rows :, :].astype(jnp.int32).astype(jnp.float32)
    return jnp.exp2(raw) * (1.0 / FULL)


def payload_of(tiles, rows, slices):
    return jax.ShapeDtypeStruct((tiles * rows + round_up(tiles, 16), slices), jnp.int16)


def split(value, size):
    if size & (size - 1) == 0:
        return lax.shift_right_logical(value, size.bit_length() - 1), value & (size - 1)
    return lax.div(value, size), lax.rem(value, size)


def cell_of(ray, zi, xi, tiles, outers, inners):
    owner, tile = split(ray, tiles)
    inner, outer = split(owner, outers)
    return ((outer ^ xi) * inners + (inner ^ zi)) * tiles + tile


def place_slots(pos, ray_ref, cell_ref, sizes):
    outers, inners, tiles = sizes

    @pl.loop(0, ray_ref.shape[0], unroll=4)
    def _(s):
        cell_ref[s] = cell_of(ray_ref[s], pos[0], pos[1], tiles, outers, inners)


def list_slots(cell_ref, slots, ranges, slot_list):
    def look(s, count):
        slot_list[count] = s
        cell = cell_ref[s]
        hit = jnp.bool_(False)
        for low, high in ranges:
            hit = hit | ((cell >= low) & (cell < high))
        return count + hit.astype(jnp.int32)

    return lax.fori_loop(slots[0], slots[1], look, jnp.int32(0), unroll=4)


def project(count, together, low, spare, slot_list, cell_ref, pixel_ref, projector_ref, volume_ref, total):
    per_slot = projector_ref.shape[1]

    @pl.loop(0, (count + together - 1) // together)
    def _(i):
        parts, places = [], []
        for u in range(together):
            at = i * together + u
            real = at < count
            s = jnp.where(real, slot_list[at], 0)
            left = jnp.concatenate([projector_ref[s, g] for g in range(per_slot)], axis=1)
            right = jnp.concatenate([volume_ref[pixel_ref[g, s]] for g in range(per_slot)], axis=0)
            parts.append(jnp.dot(left, right, preferred_element_type=jnp.float32))
            places.append(jnp.where(real, cell_ref[s] - low, spare))
        for place, part in zip(places, parts):
            total[place] += part


def joined(tile, t, arrived):
    rows = tile.shape[0]
    for ref, first, count, factor in arrived:
        if first <= t < first + count:
            tile = tile + unpack(ref, factor, t - first, rows)
    return tile


def with_scales(refs, spans, rows):
    return [(ref, first, count, scales(ref, count, rows)) for ref, (first, count) in zip(refs, spans)]


def send_out(total, base, tiles, arrived, send, levels):
    rows = total.shape[1]
    levels[...] = jnp.zeros_like(levels)
    for t in range(tiles):
        pack(joined(total[base + t], t, arrived), send, levels, t)
    send[tiles * rows :, :] = levels[...].astype(jnp.int32).astype(jnp.int16)


def first_kernel(
    sizes, low, ray_hbm, pixel_hbm, projector_hbm, volume_hbm,
    send, projector_ref, volume_ref, out_ref, ray_ref, table_ref, slot_list, total, levels, sems,
):
    slots = ray_ref.shape[0]
    tiles = sizes[2]
    blocks = sems.shape[0] - 4
    cell_ref, pixel_ref = table_ref.at[0], table_ref.at[pl.ds(8, pixel_hbm.shape[0])]
    block = slots // blocks
    pairs = [(ray_hbm, ray_ref), (pixel_hbm, pixel_ref), (volume_hbm, volume_ref)]
    for b in range(blocks):
        span = pl.ds(b * block, block)
        pairs.append((projector_hbm.at[span], projector_ref.at[span]))
    copies = [
        pltpu.make_async_copy(source, target, sems.at[i]) for i, (source, target) in enumerate(pairs)
    ]
    for copy in copies:
        copy.start()
    total[...] = jnp.zeros_like(total)
    copies[0].wait()
    place_slots((lax.axis_index("inner"), lax.axis_index("outer")), ray_ref, cell_ref, sizes)
    copies[1].wait()
    table_copy = pltpu.make_async_copy(table_ref, out_ref, sems.at[3 + blocks])
    table_copy.start()
    copies[2].wait()
    for b in range(blocks):
        count = list_slots(cell_ref, (b * block, b * block + block), [(low, low + tiles)], slot_list)
        copies[3 + b].wait()
        project(
            count, 2, low, tiles, slot_list, cell_ref, pixel_ref, projector_ref, volume_ref, total
        )
    send_out(total, 0, tiles, [], send, levels)
    table_copy.wait()


def hold(value):
    return pltpu.with_memory_space_constraint(value, pltpu.HBM)


def first_send(slot_ray, pixel, projector, volume, sizes, low):
    slots, per_slot, rows, cols = projector.shape
    tiles = sizes[2]
    table = (8 + per_slot, slots)
    slices = volume.shape[2]
    return pl.pallas_call(
        functools.partial(first_kernel, sizes, low),
        in_specs=[HBM, HBM, HBM, HBM],
        out_specs=[VMEM, VMEM, VMEM, VMEM],
        out_shape=[
            payload_of(tiles, rows, slices),
            jax.ShapeDtypeStruct(projector.shape, projector.dtype),
            jax.ShapeDtypeStruct(volume.shape, volume.dtype),
            jax.ShapeDtypeStruct(table, jnp.int32),
        ],
        scratch_shapes=[
            pltpu.SMEM(slot_ray.shape, jnp.int32),
            pltpu.SMEM(table, jnp.int32),
            pltpu.SMEM((slots + UNROLL,), jnp.int32),
            pltpu.VMEM((tiles + 1, rows, slices), jnp.float32),
            pltpu.VMEM((round_up(tiles, 16), slices), jnp.float32),
            pltpu.SemaphoreType.DMA((4 + math.gcd(slots, 4),)),
        ],
        compiler_params=pltpu.CompilerParams(vmem_limit_bytes=48 * 2**20),
        cost_estimate=QUICK,
    )(hold(slot_ray), hold(pixel), hold(projector), hold(volume))


def further_kernel(tiles, sent, ranges, table_ref, projector_ref, volume_ref, after, *rest):
    sends = rest[: len(sent)]
    *own_ref, slot_list, total, levels = rest[len(sent) :]
    slots, per_slot = projector_ref.shape[:2]
    cell_ref, pixel_ref = table_ref.at[0], table_ref.at[pl.ds(8, per_slot)]
    for send, low in zip(sends, sent):
        total[...] = jnp.zeros_like(total)
        count = list_slots(cell_ref, (0, slots), [(low, low + tiles)], slot_list)
        project(
            count, 2, low, tiles, slot_list, cell_ref, pixel_ref, projector_ref, volume_ref, total
        )
        send_out(total, 0, tiles, [], send, levels)
    base = 0
    for ref in own_ref:
        ref[...] = jnp.zeros_like(ref)
        for low, high in ranges:
            count = list_slots(cell_ref, (0, slots), [(low, high)], slot_list)
            project(
                count, UNROLL, low - base, ref.shape[0] - 1, slot_list, cell_ref, pixel_ref,
                projector_ref, volume_ref, ref,
            )
            base += high - low


def further_sums(table, projector, volume, tiles, sent, ranges, after):
    slots, per_slot, rows, cols = projector.shape
    slices = volume.shape[2]
    kept = sum(high - low for low, high in ranges)
    out_shape = [payload_of(tiles, rows, slices)] * len(sent)
    if kept:
        out_shape.append(jax.ShapeDtypeStruct((kept + 1, rows, slices), jnp.float32))
    return pl.pallas_call(
        functools.partial(further_kernel, tiles, sent, ranges),
        in_specs=[SMEM, VMEM, VMEM, ANY],
        out_specs=[VMEM] * len(out_shape),
        out_shape=out_shape,
        scratch_shapes=[
            pltpu.SMEM((slots + UNROLL,), jnp.int32),
            pltpu.VMEM((tiles + 1, rows, slices), jnp.float32),
            pltpu.VMEM((round_up(tiles, 16), slices), jnp.float32),
        ],
        compiler_params=PARAMS,
        cost_estimate=QUICK,
    )(table, projector, volume, after)


def combine_kernel(low, part, spans, own_ref, after, *rest):
    refs, (out_ref, levels) = rest[: len(spans)], rest[len(spans) :]
    send_out(own_ref, low, part, with_scales(refs, spans, own_ref.shape[1]), out_ref, levels)


def combine(own, low, part, arrived, after):
    _, rows, slices = own.shape
    return pl.pallas_call(
        functools.partial(combine_kernel, low, part, [(0, part)] * len(arrived)),
        in_specs=[VMEM, ANY] + [VMEM] * len(arrived),
        out_specs=VMEM,
        out_shape=payload_of(part, rows, slices),
        scratch_shapes=[pltpu.VMEM((round_up(part, 16), slices), jnp.float32)],
        compiler_params=PARAMS,
        cost_estimate=QUICK,
    )(own, after, *arrived)


def gather_kernel(spans, own_ref, *rest):
    refs, out_ref = rest[: len(spans)], rest[len(spans)]
    arrived = with_scales(refs, spans, own_ref.shape[1])
    for t in range(out_ref.shape[0]):
        out_ref[t] = joined(own_ref[t], t, arrived)


def gather(own, tiles, spans, arrived):
    return pl.pallas_call(
        functools.partial(gather_kernel, spans),
        in_specs=[VMEM] * (1 + len(arrived)),
        out_specs=VMEM,
        out_shape=jax.ShapeDtypeStruct((tiles,) + own.shape[1:], jnp.float32),
        compiler_params=PARAMS,
        cost_estimate=QUICK,
    )(own, *arrived)


def weight_kernel(table_ref, index_ref, after, out_ref):
    looked = jnp.zeros(index_ref.shape, jnp.float32)
    for c in range(table_ref.shape[0]):
        looked = jnp.where(index_ref[...] == c, table_ref[c], looked)
    for t in range(index_ref.shape[0]):
        wide = jnp.broadcast_to(looked[t : t + 1, :], (out_ref.shape[2], out_ref.shape[1]))
        out_ref[t] = wide.T.astype(jnp.bfloat16)


def ray_weights(table, index, slices, after):
    tiles, rows = index.shape
    return pl.pallas_call(
        weight_kernel,
        in_specs=[SMEM, VMEM, ANY],
        out_specs=VMEM,
        out_shape=jax.ShapeDtypeStruct((tiles, rows, slices), jnp.bfloat16),
        compiler_params=PARAMS,
        cost_estimate=QUICK,
    )(table.astype(jnp.float32), index, after)


def residual_kernel(spans, sum_ref, sinogram_ref, weight_ref, *rest):
    refs, out_refs = rest[: len(spans)], rest[len(spans) :]
    arrived = with_scales(refs, spans, sum_ref.shape[1])
    part = out_refs[0].shape[0]
    for t in range(sum_ref.shape[0]):
        gap = sinogram_ref[t].astype(jnp.float32) - joined(sum_ref[t], t, arrived)
        out_refs[t // part][t % part] = (weight_ref[t].astype(jnp.float32) * gap).astype(
            jnp.bfloat16
        )


def residual_of(sums, sinogram, weights, part, spans, arrived):
    tiles, rows, slices = sinogram.shape
    return pl.pallas_call(
        functools.partial(residual_kernel, spans),
        in_specs=[VMEM] * (3 + len(arrived)),
        out_specs=[VMEM] * (tiles // part),
        out_shape=[jax.ShapeDtypeStruct((part, rows, slices), jnp.bfloat16)] * (tiles // part),
        compiler_params=PARAMS,
        cost_estimate=QUICK,
    )(sums, sinogram, weights, *arrived)


def column_kernel(table_ref, projector_ref, after, out_ref):
    slots, per_slot, rows, cols = projector_ref.shape
    out_ref[...] = jnp.zeros_like(out_ref)

    @pl.loop(0, slots)
    def _(s):
        for g in range(per_slot):
            column = jnp.sum(projector_ref[s, g].astype(jnp.float32), axis=0, keepdims=True)
            out_ref[table_ref[8 + g, s]] += column


def column_sums(table, projector, patch_tiles, after):
    slots, per_slot, rows, cols = projector.shape
    return pl.pallas_call(
        column_kernel,
        in_specs=[SMEM, VMEM, ANY],
        out_specs=VMEM,
        out_shape=jax.ShapeDtypeStruct((patch_tiles, 1, cols), jnp.float32),
        compiler_params=PARAMS,
        cost_estimate=QUICK,
    )(table, projector, after)


def spread_kernel(lows, begin, finish, table_ref, projector_ref, *rest):
    rest = list(rest)
    before = None if begin else rest.pop(0)
    volume_ref, column_ref = (rest.pop(0), rest.pop(0)) if finish else (None, None)
    chunks, (out_ref, slot_list, held), total = rest[: len(lows)], rest[len(lows) : len(lows) + 3], rest[-1]
    slots, per_slot, rows, cols = projector_ref.shape
    part = chunks[0].shape[0]
    patch_tiles = total.shape[0] - 1
    for low, chunk in zip(lows, chunks):
        held[low : low + part] = chunk[...]
    if begin:
        total[...] = jnp.zeros_like(total)
    else:
        total[...] = before[...]
    count = list_slots(table_ref.at[0], (0, slots), [(low, low + part) for low in lows], slot_list)

    @pl.loop(0, (count + UNROLL - 1) // UNROLL)
    def _(i):
        parts, places = [], []
        for u in range(UNROLL):
            real = i * UNROLL + u < count
            s = jnp.where(real, slot_list[i * UNROLL + u], slot_list[0])
            right = jnp.concatenate([projector_ref[s, g] for g in range(per_slot)], axis=1)
            parts.append(
                lax.dot_general(
                    held[table_ref[0, s]], right, (((0,), (0,)), ((), ())), preferred_element_type=jnp.float32
                )
            )
            places.append([jnp.where(real, table_ref[8 + g, s], patch_tiles) for g in range(per_slot)])
        for part, place in zip(parts, places):
            for g in range(per_slot):
                total[place[g]] += part[:, g * cols : (g + 1) * cols]

    if finish:
        for q in range(patch_tiles):
            out_ref[q] = volume_ref[q].astype(jnp.float32) + (total[q] / column_ref[q]).T


def spread(table, projector, all_cells, lows, chunks, patch_tiles, before, last=()):
    slots, per_slot, rows, cols = projector.shape
    slices = chunks[0].shape[2]
    begin, finish = before is None, bool(last)
    more = ([] if begin else [before]) + list(last) + chunks
    shape = (patch_tiles + 1, slices, cols)
    scratch = [
        pltpu.SMEM((slots + UNROLL,), jnp.int32),
        pltpu.VMEM((all_cells, rows, slices), jnp.bfloat16),
    ]
    kernel = functools.partial(spread_kernel, lows, begin, finish)
    if not finish:
        inner = kernel
        kernel = lambda *refs: inner(*refs, refs[-3])
    return pl.pallas_call(
        kernel,
        in_specs=[SMEM] + [VMEM] * (1 + len(more)),
        out_specs=VMEM,
        out_shape=jax.ShapeDtypeStruct((patch_tiles, cols, slices) if finish else shape, jnp.float32),
        scratch_shapes=scratch + ([pltpu.VMEM(shape, jnp.float32)] if finish else []),
        compiler_params=PARAMS,
        cost_estimate=QUICK,
    )(table, projector, *more)


def gate(value, *after):
    return pl.pallas_call(
        lambda *refs: None,
        in_specs=[VMEM] * (1 + len(after)),
        out_specs=VMEM,
        out_shape=jax.ShapeDtypeStruct(value.shape, value.dtype),
        input_output_aliases={0: 0},
        compiler_params=PARAMS,
        cost_estimate=QUICK,
    )(value, *after)


def dense_plan(volume, projector, slot_ray, slot_pixel, sinogram, weight_index, weight_table):
    inners = lax.axis_size("inner")
    outers = lax.axis_size("outer")
    tiles = sinogram.shape[0]
    patch_tiles, _, slices = volume.shape
    sizes = (outers, inners, tiles)
    pixel = slot_pixel.T

    turns = sorted(range(inners), key=lambda k: (bin(k).count("1"), k))
    far = [k for k in reversed(turns) if k > 1]
    others = range(1, outers)
    low = lambda j, k: (j * inners + k) * tiles
    arrived = {(j, k): [] for j in range(outers) for k in range(inners)}
    first, *sent = [(j, k) for k in far[:1] for j in others]
    near = [(j, 1) for j in others]
    sent += [(j, k) for k in far[1:] for j in others]
    payload, projector, volume, table = first_send(
        slot_ray, pixel, projector, volume, sizes, low(*first)
    )
    kept = [(0, inners * tiles)] + [(low(j, 0), low(j, 0) + tiles) for j in others]
    sends = {first: payload}
    payloads = further_sums(
        table, projector, volume, tiles, [low(*piece) for piece in near], [], payload
    )
    sends.update(zip(near, payloads))
    kept = [(low(0, 2), low(1, 0)), (0, low(0, 2)), (low(1, 0), low(1, 0) + tiles)]
    *payloads, own = further_sums(
        table, projector, volume, tiles, [low(*piece) for piece in sent], kept[:1], payloads[-1]
    )
    sends.update(zip(sent, payloads))
    for k in far[:1]:
        for j in others:
            arrived[0, k].append(swap(sends[j, k], "outer", j))
    for j in others:
        arrived[j, 0].append(swap(sends[j, 1], "inner", 1))
    after = own
    for i, k in enumerate(far):
        bit = k & -k
        after = combine(own, low(0, k) - low(0, 2), tiles, arrived[0, k], after)
        arrived[0, k ^ bit].append(swap(after, "inner", bit))
        if i == 0:
            (near_own,) = further_sums(table, projector, volume, tiles, [], kept[1:], after)
            for l in far[1:]:
                for j in others:
                    payload = gate(sends[j, l], after) if LATER else sends[j, l]
                    arrived[0, l].append(swap(payload, "outer", j))
            for j in others:
                after = combine(near_own, 2 * tiles, tiles, arrived[j, 0], after)
                arrived[0, 0].append(swap(after, "outer", j))
    after = combine(near_own, tiles, tiles, [], after)
    arrived[0, 0].append(swap(after, "inner", 1))
    columns = column_sums(table, projector, patch_tiles, after)
    weights = ray_weights(weight_table, weight_index, slices, columns)
    longest = arrived[0, 0][-2:-1]
    rest = arrived[0, 0][:-2] + arrived[0, 0][-1:]
    span = (0, tiles)
    sums = gather(near_own, tiles, [span] * len(longest), longest)
    residual = residual_of(sums, sinogram, weights, tiles, [span] * len(rest), rest)[0]

    chunks = {(0, 0): residual}
    total = None

    def add(pieces, last=()):
        nonlocal total
        total = spread(
            table, projector, outers * inners * tiles, [low(*piece) for piece in pieces],
            [chunks[piece] for piece in pieces], patch_tiles, total, last,
        )

    bit = inners // 2
    while bit:
        chunks[0, bit] = swap(residual, "inner", bit)
        bit //= 2
    for j in others:
        chunks[j, 0] = swap(residual, "outer", j)
    done = {(0, 0), (0, 1)} | {(j, 0) for j in others}
    for i, k in enumerate(turns[2:]):
        if i == 0 and EARLY:
            for j in others:
                chunks[j, 1] = swap(chunks[j, 0], "inner", 1)
            chunks[0, k] = gate(chunks[0, k], chunks[0, 1], *[chunks[j, 0] for j in others])
        if k == turns[-1]:
            done |= {(0, l) for l in turns[:-1]}
            add(sorted(done))
            chunks[0, k] = gate(chunks[0, k], total)
        bit = (k & -k) // 2
        while bit:
            chunks[0, k ^ bit] = swap(chunks[0, k], "inner", bit)
            bit //= 2
        for j in others:
            chunks[j, k] = swap(chunks[0, k], "outer", j)
    if not EARLY:
        for j in others:
            chunks[j, 1] = swap(gate(chunks[j, 0], chunks[0, turns[-1]]), "inner", 1)
    ends = [(j, turns[-1]) for j in others] + ([] if EARLY else [(j, 1) for j in others])
    add([piece for piece in chunks if piece not in ends and piece not in done])
    add(ends, (volume, columns))
    return total


def slot_plan(volume, projector, slot_ray, slot_pixel, sinogram, weight_index, weight_table):
    inners = lax.axis_size("inner")
    outers = lax.axis_size("outer")
    slot_count = projector.shape[0]
    per_slot = projector.shape[1]
    tile_rows = projector.shape[2]
    tile_cols = projector.shape[3]
    patch_tiles = volume.shape[0]
    slice_count = volume.shape[2]
    owned_rows = sinogram.shape[0]
    band_rows = owned_rows * outers
    capacity = 2 * slot_count // inners
    cell_count = inners * capacity
    target = slot_ray // band_rows
    offset = slot_ray % band_rows
    same_target = target[:, None] == target[None, :]
    earlier = jnp.arange(slot_count)[:, None] > jnp.arange(slot_count)[None, :]
    slot_rank = jnp.sum(jnp.logical_and(same_target, earlier), axis=1)
    position = target * capacity + slot_rank
    partial_value = jnp.zeros((slot_count, tile_rows, slice_count), jnp.float32)
    for column in range(per_slot):
        pixels = volume[slot_pixel[:, column]]
        partial_value = partial_value + jnp.einsum(
            "srp,spc->src", projector[:, column], pixels, preferred_element_type=jnp.float32
        )
    outgoing = (
        jnp.zeros((cell_count, tile_rows, slice_count), jnp.float32).at[position].set(partial_value)
    )
    labels = jnp.full((cell_count,), -1.0, jnp.float32).at[position].set(offset.astype(jnp.float32))
    arrived, arrived_rows = (
        lax.all_to_all(
            outgoing.reshape(inners, capacity, tile_rows, slice_count),
            "inner",
            split_axis=0,
            concat_axis=0,
            tiled=True,
        ),
        lax.all_to_all(
            labels.reshape(inners, capacity), "inner", split_axis=0, concat_axis=0, tiled=True
        ),
    )
    selector = (
        jnp.arange(band_rows, dtype=jnp.float32)[:, None] == arrived_rows.reshape(1, cell_count)
    ).astype(jnp.float32)
    block_sums = jnp.dot(
        selector,
        arrived.reshape(cell_count, tile_rows * slice_count),
        precision=lax.Precision.HIGHEST,
    ).reshape(band_rows, tile_rows, slice_count)
    classes = weight_table.shape[0]
    lookup = weight_index[:, :, None] == jnp.arange(classes)[None, None, :]
    weights = jnp.sum(
        jnp.where(lookup, weight_table[None, None, :], jnp.zeros((), weight_table.dtype)), axis=2
    )
    own_sums = lax.psum_scatter(block_sums, "outer", scatter_dimension=0, tiled=True)
    own_residual = (
        weights.astype(jnp.float32)[:, :, None] * (sinogram.astype(jnp.float32) - own_sums)
    ).astype(jnp.bfloat16)
    residual = lax.all_gather(own_residual, "outer", axis=0, tiled=True)
    picked = jnp.dot(
        selector.T.astype(jnp.bfloat16),
        residual.reshape(band_rows, tile_rows * slice_count),
        preferred_element_type=jnp.float32,
    ).astype(jnp.bfloat16)
    returned = lax.all_to_all(
        picked.reshape(inners, capacity, tile_rows, slice_count),
        "inner",
        split_axis=0,
        concat_axis=0,
        tiled=True,
    )
    slot_residual = returned.reshape(cell_count, tile_rows, slice_count)[position]
    owners = jnp.arange(patch_tiles)
    backward_sum = jnp.zeros((patch_tiles, tile_cols, slice_count), jnp.float32)
    column_sum = jnp.zeros((patch_tiles, tile_cols), jnp.float32)
    for column in range(per_slot):
        member = (owners[:, None] == slot_pixel[None, :, column]).astype(jnp.float32)
        spread = jnp.einsum(
            "srp,src->spc", projector[:, column], slot_residual, preferred_element_type=jnp.float32
        )
        backward_sum = backward_sum + jnp.einsum(
            "ts,spc->tpc", member, spread, precision=lax.Precision.HIGHEST
        )
        column_sum = column_sum + jnp.dot(
            member,
            jnp.sum(projector[:, column], axis=1, dtype=jnp.float32),
            precision=lax.Precision.HIGHEST,
        )
    return volume.astype(jnp.float32) + backward_sum / column_sum[:, :, None]


def on_device(volume, projector, slot_ray, slot_pixel, sinogram, weight_index, weight_table):
    inners = lax.axis_size("inner")
    outers = lax.axis_size("outer")
    capacity = 2 * slot_ray.shape[0] // inners
    powers = inners & (inners - 1) == 0 and outers & (outers - 1) == 0 and inners > 1 < outers
    plan = dense_plan if powers and sinogram.shape[0] * outers <= capacity else slot_plan
    return plan(volume, projector, slot_ray, slot_pixel, sinogram, weight_index, weight_table)


def solution(mesh):
    in_specs = (
        P(("group", "inner", "outer"), None, "cuts"),
        P(("inner", "outer"), None, None, None),
        P(("inner", "outer")),
        P(("inner", "outer"), None),
        P(("group", "inner", "outer"), None, "cuts"),
        P(("group", "inner", "outer"), None),
        P(),
    )
    out_specs = P(("group", "inner", "outer"), None, "cuts")
    return jax.shard_map(
        on_device, mesh=mesh, in_specs=in_specs, out_specs=out_specs, check_vma=False
    )
```

time: 69.4 us -> 64.5 us (0.929)
  waiting for transfers between devices: 28.5 us -> 22.7 us
  starting transfers between devices: 18.6 us -> 21.7 us
  Pallas kernels: 21.5 us -> 19.2 us
    ppermute x14, waiting for transfers between devices: 28.5 us -> 22.7 us  [swap(): return lax.ppermute(value, axis, [(i, i ^ bits) for i in range(size)])]
    ppermute x14, starting transfers between devices: 18.6 us -> 21.7 us  [swap(): return lax.ppermute(value, axis, [(i, i ^ bits) for i in range(size)])]
    pallas_call x16, Pallas kernels: 19.1 us -> 16.7 us  [the longest x3 7.25 us: spread(): pl.pallas_call(kernel, in_specs=[SMEM] + [VMEM] * (1 + len(more)), out_sp...]
  transfers between devices with their start and end apart: 14 -> 14, of which waited for: 12 -> 8; matrix products, arithmetic and copies ran while one was open for 0% -> 0% of each run, Pallas kernels for 21% -> 21%
where the time goes in v3:
time: 64.5 us; the launch traced here: 63.8 us
  waiting for transfers between devices  22.7 us (35%)
  starting transfers between devices  21.7 us (34%)
  Pallas kernels  19.2 us (30%)
    ppermute x14, waiting for transfers between devices, swap(): return lax.ppermute(value, axis, [(i, i ^ bits) for i in range(size)])  22.7 us
    ppermute x14, starting transfers between devices, swap(): return lax.ppermute(value, axis, [(i, i ^ bits) for i in range(size)])  21.7 us
    pallas_call x3, Pallas kernels, spread(): pl.pallas_call(kernel, in_specs=[SMEM] + [VMEM] * (1 + len(more)), out_sp...  7.25 us
    pallas_call x3, Pallas kernels, further_sums(): pl.pallas_call(functools.partial(further_kernel, tiles, sent, ranges), in...  5.79 us
    pallas_call x1, Pallas kernels, first_send(): pl.pallas_call(functools.partial(first_kernel, sizes, low), in_specs=[HBM...  2.69 us
    pallas_call x1, Pallas kernels, column_sums(): pl.pallas_call(column_kernel, in_specs=[SMEM, VMEM, ANY], out_specs=VMEM,...  1.78 us
  transfers between devices with their start and end apart: 14, of which 8 were waited for; matrix products, arithmetic and copies ran while one was open for 0% of the time, Pallas kernels for 21%

profile of v3, /device:TPU:0, one launch (start us, length us, event | category | flops | bytes accessed | tf_op | source)
XLA Modules:
  0.0 63.8 jit_solution(1494235025429839521)
XLA Ops:
  0.0 2.7 %shard_map.73 = (s16[1040,128]{1,0:T(8,128)(2,1)S(1)}, bf16[32,4,128,128]{3,2,1,0:T(8,128)(2,1)S(1)}, bf16[6,128,128]{2,1,0:T(8,128)(2,1)S(1)}, s32[12,32]{1,0:T(8,128)S(1)}) custom-call(s32[32]{0:T(128)} %ray_hbm.1, s32[4,32]{1,0:T(4,128)} %bitcast.1, bf16[32,4,128,128]{3,2,1,0:T(8,128)(2,1)} %projector_hbm.1, bf16[6,128,128]{2,1,0:T(8,128)(2,1)} %volume_hbm.1), custom_call_target="tpu_custom_call" | custom-call | flops 1 | bytes 1 | tf_op jit(solution)/shard_map/pallas_call | solution.py:170
  2.7 3.0 %collective-permute-start = (s16[1040,128]{1,0:T(8,128)(2,1)S(1)}, s16[1040,128]{1,0:T(8,128)(2,1)S(1)}, u32[]{:S(2)}, u32[]{:S(2)}) collective-permute-start(s16[1040,128]{1,0:T(8,128)(2,1)S(1)} %get-tuple-element.14.after), channel_id=1, source_target_pairs={{0,2},{2,0},{1,3},{3,1},{4,6},{6,4},{5,7},{7,5},{8,10},{10,8},{9,1... | collective-permute-start | bytes 798728 | tf_op jit(solution)/shard_map/ppermute | solution.py:29
  5.7 1.2 %shard_map.74.after = s16[1040,128]{1,0:T(8,128)(2,1)S(1)} custom-call(s32[12,32]{1,0:T(8,128)S(1)} %get-tuple-element.11.table_ref.refs_0_, bf16[32,4,128,128]{3,2,1,0:T(8,128)(2,1)S(1)} %get-tuple-element.12.projector_ref.refs_1_, bf16[6,128,128]{2,1,0:T(8,128)(2,1)S(1)} %get-tuple-element.13.volume_ref.rest_1_, s16[1040,128]{1,0:T(8,128)(2,1)S(1)} %get-tuple-element.14.after), custom_call_target="tpu_custom_call" | custom-call | flops 1 | bytes 1 | tf_op jit(solution)/shard_map/pallas_call | solution.py:224
  6.9 2.5 %collective-permute-start.1 = (s16[1040,128]{1,0:T(8,128)(2,1)S(1)}, s16[1040,128]{1,0:T(8,128)(2,1)S(1)}, u32[]{:S(2)}, u32[]{:S(2)}) collective-permute-start(s16[1040,128]{1,0:T(8,128)(2,1)S(1)} %shard_map.74.after), channel_id=1, source_target_pairs={{0,4},{4,0},{8,12},{12,8},{1,5},{5,1},{9,13},{13,9},{2,6},{6,2},{1... | collective-permute-start | bytes 798728 | tf_op jit(solution)/shard_map/ppermute | solution.py:29
  9.4 2.2 %shard_map.75 = (s16[1040,128]{1,0:T(8,128)(2,1)S(1)}, f32[17,128,128]{2,1,0:T(8,128)S(1)}) custom-call(s32[12,32]{1,0:T(8,128)S(1)} %get-tuple-element.11.table_ref.refs_0_, bf16[32,4,128,128]{3,2,1,0:T(8,128)(2,1)S(1)} %get-tuple-element.12.projector_ref.refs_1_, bf16[6,128,128]{2,1,0:T(8,128)(2,1)S(1)} %get-tuple-element.13.volume_ref.rest_1_, ...), custom_call_target="tpu_custom_call" | custom-call | flops 1 | bytes 1 | tf_op jit(solution)/shard_map/pallas_call | solution.py:224
  11.6 0.5 collective-permute-done.rest_0_
  12.1 0.2 shard_map.76.after.refs_1_
  12.3 1.8 %collective-permute-start.3 = (s16[1040,128]{1,0:T(8,128)(2,1)S(1)}, s16[1040,128]{1,0:T(8,128)(2,1)S(1)}, u32[]{:S(2)}, u32[]{:S(2)}) collective-permute-start(s16[1040,128]{1,0:T(8,128)(2,1)S(1)} %shard_map.79), channel_id=1, source_target_pairs={{0,2},{2,0},{1,3},{3,1},{4,6},{6,4},{5,7},{7,5},{8,10},{10,8},{9,1... | collective-permute-start | bytes 798728 | tf_op jit(solution)/shard_map/ppermute | solution.py:29
  14.1 1.6 %collective-permute-start.2 = (s16[1040,128]{1,0:T(8,128)(2,1)S(1)}, s16[1040,128]{1,0:T(8,128)(2,1)S(1)}, u32[]{:S(2)}, u32[]{:S(2)}) collective-permute-start(s16[1040,128]{1,0:T(8,128)(2,1)S(1)} %shard_map.76.after.refs_1_), channel_id=1, source_target_pairs={{0,4},{4,0},{8,12},{12,8},{1,5},{5,1},{9,13},{13,9},{2,6},{6,2},{1... | collective-permute-start | bytes 798728 | tf_op jit(solution)/shard_map/ppermute | solution.py:29
  15.7 2.5 %shard_map.77.own_ref = f32[25,128,128]{2,1,0:T(8,128)S(1)} custom-call(s32[12,32]{1,0:T(8,128)S(1)} %get-tuple-element.11.table_ref.refs_0_, bf16[32,4,128,128]{3,2,1,0:T(8,128)(2,1)S(1)} %get-tuple-element.12.projector_ref.refs_1_, bf16[6,128,128]{2,1,0:T(8,128)(2,1)S(1)} %get-tuple-element.13.volume_ref.rest_1_, s16[1040,128]{1,0:T(8,128)(2,1)S(1)} %shard_map.76.after.refs_1_), custom_call_target="tpu_custom_call" | custom-call | flops 1 | bytes 1 | tf_op jit(solution)/shard_map/pallas_call | solution.py:224
  18.2 0.0 copy-start.2
  18.2 0.0 collective-permute-done.1.rest_0_
  18.2 0.2 shard_map.78.after
  18.4 0.0 copy-start.1
  18.4 1.6 %collective-permute-done.3.rest_1_ = s16[1040,128]{1,0:T(8,128)(2,1)S(1)} collective-permute-done((s16[1040,128]{1,0:T(8,128)(2,1)S(1)}, s16[1040,128]{1,0:T(8,128)(2,1)S(1)}, u32[]{:S(2)}, u32[]{:S(2)}) %collective-permute-start.3) | collective-permute-done | bytes 266272 | tf_op jit(solution)/shard_map/ppermute | solution.py:29
  19.9 1.3 %collective-permute-done.2.rest_0_ = s16[1040,128]{1,0:T(8,128)(2,1)S(1)} collective-permute-done((s16[1040,128]{1,0:T(8,128)(2,1)S(1)}, s16[1040,128]{1,0:T(8,128)(2,1)S(1)}, u32[]{:S(2)}, u32[]{:S(2)}) %collective-permute-start.2) | collective-permute-done | bytes 266272 | tf_op jit(solution)/shard_map/ppermute | solution.py:29
  21.2 0.2 shard_map.80.after
  21.5 0.0 copy-start
  21.5 2.5 %collective-permute-start.4 = (s16[1040,128]{1,0:T(8,128)(2,1)S(1)}, s16[1040,128]{1,0:T(8,128)(2,1)S(1)}, u32[]{:S(2)}, u32[]{:S(2)}) collective-permute-start(s16[1040,128]{1,0:T(8,128)(2,1)S(1)} %shard_map.80.after), channel_id=1, source_target_pairs={{0,8},{4,12},{8,0},{12,4},{1,9},{5,13},{9,1},{13,5},{2,10},{6,14},... | collective-permute-start | bytes 798728 | tf_op jit(solution)/shard_map/ppermute | solution.py:29
  24.0 0.5 collective-permute-start.5
  24.4 0.1 shard_map.82.after
  24.5 1.8 %collective-permute-start.6 = (s16[1040,128]{1,0:T(8,128)(2,1)S(1)}, s16[1040,128]{1,0:T(8,128)(2,1)S(1)}, u32[]{:S(2)}, u32[]{:S(2)}) collective-permute-start(s16[1040,128]{1,0:T(8,128)(2,1)S(1)} %shard_map.82.after), channel_id=1, source_target_pairs={{0,4},{4,0},{8,12},{12,8},{1,5},{5,1},{9,13},{13,9},{2,6},{6,2},{1... | collective-permute-start | bytes 798728 | tf_op jit(solution)/shard_map/ppermute | solution.py:29
  26.4 0.0 copy-done.2
  26.4 1.8 %shard_map.83.after.rest_2_ = f32[6,1,128]{2,1,0:T(1,128)S(1)} custom-call(s32[12,32]{1,0:T(8,128)S(1)} %get-tuple-element.11.table_ref.refs_0_, bf16[32,4,128,128]{3,2,1,0:T(8,128)(2,1)S(1)} %get-tuple-element.12.projector_ref.refs_1_, s16[1040,128]{1,0:T(8,128)(2,1)S(1)} %shard_map.82.after), custom_call_target="tpu_custom_call" | custom-call | flops 1 | bytes 1 | tf_op jit(solution)/shard_map/pallas_call | solution.py:332
  28.1 0.0 copy-done.1
  28.2 0.7 %shard_map.84.weight_ref = bf16[8,128,128]{2,1,0:T(8,128)(2,1)S(1)} custom-call(f32[16]{0:T(128)S(1)} %convert_element_type.3.table_ref, s32[8,128]{1,0:T(8,128)S(1)} %copy-done.1, f32[6,1,128]{2,1,0:T(1,128)S(1)} %shard_map.83.after.rest_2_), custom_call_target="tpu_custom_call" | custom-call | flops 1 | bytes 1 | tf_op jit(solution)/shard_map/pallas_call | solution.py:286
  28.8 5.6 %collective-permute-done.4.rest_0_ = s16[1040,128]{1,0:T(8,128)(2,1)S(1)} collective-permute-done((s16[1040,128]{1,0:T(8,128)(2,1)S(1)}, s16[1040,128]{1,0:T(8,128)(2,1)S(1)}, u32[]{:S(2)}, u32[]{:S(2)}) %collective-permute-start.4) | collective-permute-done | bytes 266272 | tf_op jit(solution)/shard_map/ppermute | solution.py:29
  34.5 0.1 shard_map.81.sum_ref
  34.6 0.0 collective-permute-done.5.rest_0_
  34.6 0.3 collective-permute-done.6.rest_1_
  34.8 0.0 copy-done
  34.8 0.2 shard_map.85.refs_2_
  35.1 1.6 %collective-permute-start.8 = (bf16[8,128,128]{2,1,0:T(8,128)(2,1)S(1)}, bf16[8,128,128]{2,1,0:T(8,128)(2,1)S(1)}, u32[]{:S(2)}, u32[]{:S(2)}) collective-permute-start(bf16[8,128,128]{2,1,0:T(8,128)(2,1)S(1)} %shard_map.85.refs_2_), channel_id=1, source_target_pairs={{0,8},{4,12},{8,0},{12,4},{1,9},{5,13},{9,1},{13,5},{2,10},{6,14},... | collective-permute-start | bytes 786440 | tf_op jit(solution)/shard_map/ppermute | solution.py:29
  36.6 1.9 %collective-permute-start.7 = (bf16[8,128,128]{2,1,0:T(8,128)(2,1)S(1)}, bf16[8,128,128]{2,1,0:T(8,128)(2,1)S(1)}, u32[]{:S(2)}, u32[]{:S(2)}) collective-permute-start(bf16[8,128,128]{2,1,0:T(8,128)(2,1)S(1)} %shard_map.85.refs_2_), channel_id=1, source_target_pairs={{0,4},{4,0},{8,12},{12,8},{1,5},{5,1},{9,13},{13,9},{2,6},{6,2},{1... | collective-permute-start | bytes 786440 | tf_op jit(solution)/shard_map/ppermute | solution.py:29
  38.6 1.6 %collective-permute-start.9 = (bf16[8,128,128]{2,1,0:T(8,128)(2,1)S(1)}, bf16[8,128,128]{2,1,0:T(8,128)(2,1)S(1)}, u32[]{:S(2)}, u32[]{:S(2)}) collective-permute-start(bf16[8,128,128]{2,1,0:T(8,128)(2,1)S(1)} %shard_map.85.refs_2_), channel_id=1, source_target_pairs={{0,2},{2,0},{1,3},{3,1},{4,6},{6,4},{5,7},{7,5},{8,10},{10,8},{9,1... | collective-permute-start | bytes 786440 | tf_op jit(solution)/shard_map/ppermute | solution.py:29
  40.1 8.0 %collective-permute-done.8.refs_4_ = bf16[8,128,128]{2,1,0:T(8,128)(2,1)S(1)} collective-permute-done((bf16[8,128,128]{2,1,0:T(8,128)(2,1)S(1)}, bf16[8,128,128]{2,1,0:T(8,128)(2,1)S(1)}, u32[]{:S(2)}, u32[]{:S(2)}) %collective-permute-start.8) | collective-permute-done | bytes 262176 | tf_op jit(solution)/shard_map/ppermute | solution.py:29
  48.1 0.0 collective-permute-start.10
  48.1 1.2 %collective-permute-start.11 = (bf16[8,128,128]{2,1,0:T(8,128)(2,1)S(1)}, bf16[8,128,128]{2,1,0:T(8,128)(2,1)S(1)}, u32[]{:S(2)}, u32[]{:S(2)}) collective-permute-start(bf16[8,128,128]{2,1,0:T(8,128)(2,1)S(1)} %collective-permute-done.8.refs_4_), channel_id=1, source_target_pairs={{0,2},{2,0},{1,3},{3,1},{4,6},{6,4},{5,7},{7,5},{8,10},{10,8},{9,1... | collective-permute-start | bytes 786440 | tf_op jit(solution)/shard_map/ppermute | solution.py:29
  49.4 0.0 collective-permute-done.7.refs_3_
  49.4 0.0 collective-permute-done.9.refs_5_.refs_0_
  49.4 3.1 %shard_map.86.refs_1_.refs_2_ = f32[7,128,128]{2,1,0:T(8,128)S(1)} custom-call(s32[12,32]{1,0:T(8,128)S(1)} %get-tuple-element.11.table_ref.refs_0_, bf16[32,4,128,128]{3,2,1,0:T(8,128)(2,1)S(1)} %get-tuple-element.12.projector_ref.refs_1_, bf16[8,128,128]{2,1,0:T(8,128)(2,1)S(1)} %shard_map.85.refs_2_, ...), custom_call_target="tpu_custom_call" | custom-call | flops 1 | bytes 1 | tf_op jit(solution)/shard_map/pallas_call | solution.py:394
  52.5 2.4 %collective-permute-done.10.refs_0_ = bf16[8,128,128]{2,1,0:T(8,128)(2,1)S(1)} collective-permute-done((bf16[8,128,128]{2,1,0:T(8,128)(2,1)S(1)}, bf16[8,128,128]{2,1,0:T(8,128)(2,1)S(1)}, u32[]{:S(2)}, u32[]{:S(2)}) %collective-permute-start.10) | collective-permute-done | bytes 262176 | tf_op jit(solution)/shard_map/ppermute | solution.py:29
  54.9 0.0 collective-permute-start.13
  54.9 1.8 %collective-permute-start.12 = (bf16[8,128,128]{2,1,0:T(8,128)(2,1)S(1)}, bf16[8,128,128]{2,1,0:T(8,128)(2,1)S(1)}, u32[]{:S(2)}, u32[]{:S(2)}) collective-permute-start(bf16[8,128,128]{2,1,0:T(8,128)(2,1)S(1)} %shard_map.87.refs_3_.refs_1_), channel_id=1, source_target_pairs={{0,2},{2,0},{1,3},{3,1},{4,6},{6,4},{5,7},{7,5},{8,10},{10,8},{9,1... | collective-permute-start | bytes 786440 | tf_op jit(solution)/shard_map/ppermute | solution.py:29
  56.6 0.0 collective-permute-done.11.refs_4_
  56.6 1.6 %shard_map.88.rest_0_ = f32[7,128,128]{2,1,0:T(8,128)S(1)} custom-call(s32[12,32]{1,0:T(8,128)S(1)} %get-tuple-element.11.table_ref.refs_0_, bf16[32,4,128,128]{3,2,1,0:T(8,128)(2,1)S(1)} %get-tuple-element.12.projector_ref.refs_1_, f32[7,128,128]{2,1,0:T(8,128)S(1)} %shard_map.86.refs_1_.refs_2_, bf16[8,128,128]{2,1,0:T(8,128)(2,1)S(1)} %shard_map.87.refs_3_.refs_1_, ...), custom_call_target="tpu_custom_call" | custom-call | flops 1 | bytes 1 | tf_op jit(solution)/shard_map/pallas_call | solution.py:394
  58.3 3.0 %collective-permute-done.13.rest_4_ = bf16[8,128,128]{2,1,0:T(8,128)(2,1)S(1)} collective-permute-done((bf16[8,128,128]{2,1,0:T(8,128)(2,1)S(1)}, bf16[8,128,128]{2,1,0:T(8,128)(2,1)S(1)}, u32[]{:S(2)}, u32[]{:S(2)}) %collective-permute-start.13) | collective-permute-done | bytes 262176 | tf_op jit(solution)/shard_map/ppermute | solution.py:29
  61.3 0.0 collective-permute-done.12.rest_3_
  61.3 2.5 %shard_map.90 = f32[6,128,128]{2,1,0:T(8,128)} custom-call(s32[12,32]{1,0:T(8,128)S(1)} %get-tuple-element.11.table_ref.refs_0_, bf16[32,4,128,128]{3,2,1,0:T(8,128)(2,1)S(1)} %get-tuple-element.12.projector_ref.refs_1_, f32[7,128,128]{2,1,0:T(8,128)S(1)} %shard_map.88.rest_0_, bf16[6,128,128]{2,1,0:T(8,128)(2,1)S(1)} %get-tuple-element.13.volume_ref.rest_1_, ...), custom_call_target="tpu_custom_call" | custom-call | flops 1 | bytes 1 | tf_op jit(solution)/shard_map/pallas_call | solution.py:394
  (4 shorter events, 0.0 us)
Async XLA Ops:
  2.7 9.4 %collective-permute-start = (s16[1040,128]{1,0:T(8,128)(2,1)S(1)}, s16[1040,128]{1,0:T(8,128)(2,1)S(1)}, u32[]{:S(2)}, u32[]{:S(2)}) collective-permute-start(s16[1040,128]{1,0:T(8,128)(2,1)S(1)} %get-tuple-element.14.after), channel_id=1, source_target_pairs={{0,2},{2,0},{1,3},{3,1},{4,6},{6,4},{5,7},{7,5},{8,10},{10,8},{9,1... | collective-permute-start | bytes 798728 | tf_op jit(solution)/shard_map/ppermute | solution.py:29
  6.9 11.3 %collective-permute-start.1 = (s16[1040,128]{1,0:T(8,128)(2,1)S(1)}, s16[1040,128]{1,0:T(8,128)(2,1)S(1)}, u32[]{:S(2)}, u32[]{:S(2)}) collective-permute-start(s16[1040,128]{1,0:T(8,128)(2,1)S(1)} %shard_map.74.after), channel_id=1, source_target_pairs={{0,4},{4,0},{8,12},{12,8},{1,5},{5,1},{9,13},{13,9},{2,6},{6,2},{1... | collective-permute-start | bytes 798728 | tf_op jit(solution)/shard_map/ppermute | solution.py:29
  12.3 7.6 %collective-permute-start.3 = (s16[1040,128]{1,0:T(8,128)(2,1)S(1)}, s16[1040,128]{1,0:T(8,128)(2,1)S(1)}, u32[]{:S(2)}, u32[]{:S(2)}) collective-permute-start(s16[1040,128]{1,0:T(8,128)(2,1)S(1)} %shard_map.79), channel_id=1, source_target_pairs={{0,2},{2,0},{1,3},{3,1},{4,6},{6,4},{5,7},{7,5},{8,10},{10,8},{9,1... | collective-permute-start | bytes 798728 | tf_op jit(solution)/shard_map/ppermute | solution.py:29
  14.1 7.1 %collective-permute-start.2 = (s16[1040,128]{1,0:T(8,128)(2,1)S(1)}, s16[1040,128]{1,0:T(8,128)(2,1)S(1)}, u32[]{:S(2)}, u32[]{:S(2)}) collective-permute-start(s16[1040,128]{1,0:T(8,128)(2,1)S(1)} %shard_map.76.after.refs_1_), channel_id=1, source_target_pairs={{0,4},{4,0},{8,12},{12,8},{1,5},{5,1},{9,13},{13,9},{2,6},{6,2},{1... | collective-permute-start | bytes 798728 | tf_op jit(solution)/shard_map/ppermute | solution.py:29
  18.2 8.2 %copy-start.2 = (bf16[16]{0:T(256)(128)(2,1)S(1)}, bf16[16]{0:T(256)(128)(2,1)}, u32[]{:S(2)}) copy-start(bf16[16]{0:T(256)(128)(2,1)} %param.13) | copy-start | bytes 100
  18.4 9.8 %copy-start.1 = (s32[8,128]{1,0:T(8,128)S(1)}, s32[8,128]{1,0:T(8,128)}, u32[]{:S(2)}) copy-start(s32[8,128]{1,0:T(8,128)} %index_ref.1) | copy-start | bytes 12292
  21.5 13.4 %copy-start = (bf16[8,128,128]{2,1,0:T(8,128)(2,1)S(1)}, bf16[8,128,128]{2,1,0:T(8,128)(2,1)}, u32[]{:S(2)}) copy-start(bf16[8,128,128]{2,1,0:T(8,128)(2,1)} %sinogram_ref.1) | copy-start | bytes 786436
  21.5 13.0 %collective-permute-start.4 = (s16[1040,128]{1,0:T(8,128)(2,1)S(1)}, s16[1040,128]{1,0:T(8,128)(2,1)S(1)}, u32[]{:S(2)}, u32[]{:S(2)}) collective-permute-start(s16[1040,128]{1,0:T(8,128)(2,1)S(1)} %shard_map.80.after), channel_id=1, source_target_pairs={{0,8},{4,12},{8,0},{12,4},{1,9},{5,13},{9,1},{13,5},{2,10},{6,14},... | collective-permute-start | bytes 798728 | tf_op jit(solution)/shard_map/ppermute | solution.py:29
  24.0 10.6 %collective-permute-start.5 = (s16[1040,128]{1,0:T(8,128)(2,1)S(1)}, s16[1040,128]{1,0:T(8,128)(2,1)S(1)}, u32[]{:S(2)}, u32[]{:S(2)}) collective-permute-start(s16[1040,128]{1,0:T(8,128)(2,1)S(1)} %shard_map.78.after), channel_id=1, source_target_pairs={{0,2},{2,0},{1,3},{3,1},{4,6},{6,4},{5,7},{7,5},{8,10},{10,8},{9,1... | collective-permute-start | bytes 798728 | tf_op jit(solution)/shard_map/ppermute | solution.py:29
  24.5 10.3 %collective-permute-start.6 = (s16[1040,128]{1,0:T(8,128)(2,1)S(1)}, s16[1040,128]{1,0:T(8,128)(2,1)S(1)}, u32[]{:S(2)}, u32[]{:S(2)}) collective-permute-start(s16[1040,128]{1,0:T(8,128)(2,1)S(1)} %shard_map.82.after), channel_id=1, source_target_pairs={{0,4},{4,0},{8,12},{12,8},{1,5},{5,1},{9,13},{13,9},{2,6},{6,2},{1... | collective-permute-start | bytes 798728 | tf_op jit(solution)/shard_map/ppermute | solution.py:29
  35.1 13.1 %collective-permute-start.8 = (bf16[8,128,128]{2,1,0:T(8,128)(2,1)S(1)}, bf16[8,128,128]{2,1,0:T(8,128)(2,1)S(1)}, u32[]{:S(2)}, u32[]{:S(2)}) collective-permute-start(bf16[8,128,128]{2,1,0:T(8,128)(2,1)S(1)} %shard_map.85.refs_2_), channel_id=1, source_target_pairs={{0,8},{4,12},{8,0},{12,4},{1,9},{5,13},{9,1},{13,5},{2,10},{6,14},... | collective-permute-start | bytes 786440 | tf_op jit(solution)/shard_map/ppermute | solution.py:29
  36.6 12.7 %collective-permute-start.7 = (bf16[8,128,128]{2,1,0:T(8,128)(2,1)S(1)}, bf16[8,128,128]{2,1,0:T(8,128)(2,1)S(1)}, u32[]{:S(2)}, u32[]{:S(2)}) collective-permute-start(bf16[8,128,128]{2,1,0:T(8,128)(2,1)S(1)} %shard_map.85.refs_2_), channel_id=1, source_target_pairs={{0,4},{4,0},{8,12},{12,8},{1,5},{5,1},{9,13},{13,9},{2,6},{6,2},{1... | collective-permute-start | bytes 786440 | tf_op jit(solution)/shard_map/ppermute | solution.py:29
  38.6 10.8 %collective-permute-start.9 = (bf16[8,128,128]{2,1,0:T(8,128)(2,1)S(1)}, bf16[8,128,128]{2,1,0:T(8,128)(2,1)S(1)}, u32[]{:S(2)}, u32[]{:S(2)}) collective-permute-start(bf16[8,128,128]{2,1,0:T(8,128)(2,1)S(1)} %shard_map.85.refs_2_), channel_id=1, source_target_pairs={{0,2},{2,0},{1,3},{3,1},{4,6},{6,4},{5,7},{7,5},{8,10},{10,8},{9,1... | collective-permute-start | bytes 786440 | tf_op jit(solution)/shard_map/ppermute | solution.py:29
  48.1 6.8 %collective-permute-start.10 = (bf16[8,128,128]{2,1,0:T(8,128)(2,1)S(1)}, bf16[8,128,128]{2,1,0:T(8,128)(2,1)S(1)}, u32[]{:S(2)}, u32[]{:S(2)}) collective-permute-start(bf16[8,128,128]{2,1,0:T(8,128)(2,1)S(1)} %collective-permute-done.8.refs_4_), channel_id=1, source_target_pairs={{0,4},{4,0},{8,12},{12,8},{1,5},{5,1},{9,13},{13,9},{2,6},{6,2},{1... | collective-permute-start | bytes 786440 | tf_op jit(solution)/shard_map/ppermute | solution.py:29
  48.1 8.5 %collective-permute-start.11 = (bf16[8,128,128]{2,1,0:T(8,128)(2,1)S(1)}, bf16[8,128,128]{2,1,0:T(8,128)(2,1)S(1)}, u32[]{:S(2)}, u32[]{:S(2)}) collective-permute-start(bf16[8,128,128]{2,1,0:T(8,128)(2,1)S(1)} %collective-permute-done.8.refs_4_), channel_id=1, source_target_pairs={{0,2},{2,0},{1,3},{3,1},{4,6},{6,4},{5,7},{7,5},{8,10},{10,8},{9,1... | collective-permute-start | bytes 786440 | tf_op jit(solution)/shard_map/ppermute | solution.py:29
  54.9 6.4 %collective-permute-start.13 = (bf16[8,128,128]{2,1,0:T(8,128)(2,1)S(1)}, bf16[8,128,128]{2,1,0:T(8,128)(2,1)S(1)}, u32[]{:S(2)}, u32[]{:S(2)}) collective-permute-start(bf16[8,128,128]{2,1,0:T(8,128)(2,1)S(1)} %shard_map.89), channel_id=1, source_target_pairs={{0,4},{4,0},{8,12},{12,8},{1,5},{5,1},{9,13},{13,9},{2,6},{6,2},{1... | collective-permute-start | bytes 786440 | tf_op jit(solution)/shard_map/ppermute | solution.py:29
  54.9 6.4 %collective-permute-start.12 = (bf16[8,128,128]{2,1,0:T(8,128)(2,1)S(1)}, bf16[8,128,128]{2,1,0:T(8,128)(2,1)S(1)}, u32[]{:S(2)}, u32[]{:S(2)}) collective-permute-start(bf16[8,128,128]{2,1,0:T(8,128)(2,1)S(1)} %shard_map.87.refs_3_.refs_1_), channel_id=1, source_target_pairs={{0,2},{2,0},{1,3},{3,1},{4,6},{6,4},{5,7},{7,5},{8,10},{10,8},{9,1... | collective-permute-start | bytes 786440 | tf_op jit(solution)/shard_map/ppermute | solution.py:29

commit v4 on v3

--- a/solution.py
+++ b/solution.py
@@ -190,9 +190,14 @@
     )(hold(slot_ray), hold(pixel), hold(projector), hold(volume))
 
 
-def further_kernel(tiles, sent, ranges, table_ref, projector_ref, volume_ref, after, *rest):
+def further_kernel(tiles, sent, ranges, table_from, projector_ref, volume_ref, after, *rest):
     sends = rest[: len(sent)]
-    *own_ref, slot_list, total, levels = rest[len(sent) :]
+    *own_ref, table_ref, sem, slot_list, total, levels = rest[len(sent) :]
+    copy = pltpu.make_async_copy(table_from, table_ref, sem)
+    copy.start()
+    for ref in own_ref:
+        ref[...] = jnp.zeros_like(ref)
+    copy.wait()
     slots, per_slot = projector_ref.shape[:2]
     cell_ref, pixel_ref = table_ref.at[0], table_ref.at[pl.ds(8, per_slot)]
     for send, low in zip(sends, sent):
@@ -204,7 +209,6 @@
         send_out(total, 0, tiles, [], send, levels)
     base = 0
     for ref in own_ref:
-        ref[...] = jnp.zeros_like(ref)
         for low, high in ranges:
             count = list_slots(cell_ref, (0, slots), [(low, high)], slot_list)
             project(
@@ -223,10 +227,12 @@
         out_shape.append(jax.ShapeDtypeStruct((kept + 1, rows, slices), jnp.float32))
     return pl.pallas_call(
         functools.partial(further_kernel, tiles, sent, ranges),
-        in_specs=[SMEM, VMEM, VMEM, ANY],
+        in_specs=[VMEM, VMEM, VMEM, ANY],
         out_specs=[VMEM] * len(out_shape),
         out_shape=out_shape,
         scratch_shapes=[
+            pltpu.SMEM(table.shape, jnp.int32),
+            pltpu.SemaphoreType.DMA,
             pltpu.SMEM((slots + UNROLL,), jnp.int32),
             pltpu.VMEM((tiles + 1, rows, slices), jnp.float32),
             pltpu.VMEM((round_up(tiles, 16), slices), jnp.float32),
@@ -339,11 +345,14 @@
     )(table, projector, after)
 
 
-def spread_kernel(lows, begin, finish, table_ref, projector_ref, *rest):
+def spread_kernel(lows, begin, finish, table_from, projector_ref, *rest):
     rest = list(rest)
     before = None if begin else rest.pop(0)
     volume_ref, column_ref = (rest.pop(0), rest.pop(0)) if finish else (None, None)
-    chunks, (out_ref, slot_list, held), total = rest[: len(lows)], rest[len(lows) : len(lows) + 3], rest[-1]
+    chunks, (out_ref, table_ref, sem, slot_list, held) = rest[: len(lows)], rest[len(lows) : len(lows) + 5]
+    total = rest[-1]
+    copy = pltpu.make_async_copy(table_from, table_ref, sem)
+    copy.start()
     slots, per_slot, rows, cols = projector_ref.shape
     part = chunks[0].shape[0]
     patch_tiles = total.shape[0] - 1
@@ -353,6 +362,7 @@
         total[...] = jnp.zeros_like(total)
     else:
         total[...] = before[...]
+    copy.wait()
     count = list_slots(table_ref.at[0], (0, slots), [(low, low + part) for low in lows], slot_list)
 
     @pl.loop(0, (count + UNROLL - 1) // UNROLL)
@@ -384,16 +394,18 @@
     more = ([] if begin else [before]) + list(last) + chunks
     shape = (patch_tiles + 1, slices, cols)
     scratch = [
+        pltpu.SMEM(table.shape, jnp.int32),
+        pltpu.SemaphoreType.DMA,
         pltpu.SMEM((slots + UNROLL,), jnp.int32),
         pltpu.VMEM((all_cells, rows, slices), jnp.bfloat16),
     ]
     kernel = functools.partial(spread_kernel, lows, begin, finish)
     if not finish:
         inner = kernel
-        kernel = lambda *refs: inner(*refs, refs[-3])
+        kernel = lambda *refs: inner(*refs, refs[-5])
     return pl.pallas_call(
         kernel,
-        in_specs=[SMEM] + [VMEM] * (1 + len(more)),
+        in_specs=[VMEM] * (2 + len(more)),
         out_specs=VMEM,
         out_shape=jax.ShapeDtypeStruct((patch_tiles, cols, slices) if finish else shape, jnp.float32),
         scratch_shapes=scratch + ([pltpu.VMEM(shape, jnp.float32)] if finish else []),
@@ -467,8 +479,8 @@
     arrived[0, 0].append(swap(after, "inner", 1))
     columns = column_sums(table, projector, patch_tiles, after)
     weights = ray_weights(weight_table, weight_index, slices, columns)
-    longest = arrived[0, 0][-2:-1]
-    rest = arrived[0, 0][:-2] + arrived[0, 0][-1:]
+    longest = arrived[0, 0][-2:]
+    rest = arrived[0, 0][:-2]
     span = (0, tiles)
     sums = gather(near_own, tiles, [span] * len(longest), longest)
     residual = residual_of(sums, sinogram, weights, tiles, [span] * len(rest), rest)[0]

time: 64.5 us -> 64.9 us (level)
  waiting for transfers between devices: 22.7 us -> 27.9 us
  starting transfers between devices: 21.7 us -> 17.6 us
  Pallas kernels: 19.2 us -> 18.4 us
    ppermute x14, waiting for transfers between devices: 22.7 us -> 27.9 us  [swap(): return lax.ppermute(value, axis, [(i, i ^ bits) for i in range(size)])]
    ppermute x14, starting transfers between devices: 21.7 us -> 17.6 us  [swap(): return lax.ppermute(value, axis, [(i, i ^ bits) for i in range(size)])]
  transfers between devices with their start and end apart: 14 -> 14, of which waited for: 8 -> 8; matrix products, arithmetic and copies ran while one was open for 0% -> 0% of each run, Pallas kernels for 21% -> 20%
where the time goes in v4:
time: 64.9 us; the launch traced here: 64.1 us
  waiting for transfers between devices  27.9 us (43%)
  Pallas kernels  18.4 us (28%)
  starting transfers between devices  17.6 us (27%)
    ppermute x14, waiting for transfers between devices, swap(): return lax.ppermute(value, axis, [(i, i ^ bits) for i in range(size)])  27.9 us
    ppermute x14, starting transfers between devices, swap(): return lax.ppermute(value, axis, [(i, i ^ bits) for i in range(size)])  17.6 us
    pallas_call x3, Pallas kernels, spread(): pl.pallas_call(kernel, in_specs=[VMEM] * (2 + len(more)), out_specs=VMEM,...  6.62 us
    pallas_call x3, Pallas kernels, further_sums(): pl.pallas_call(functools.partial(further_kernel, tiles, sent, ranges), in...  5.59 us
    pallas_call x1, Pallas kernels, first_send(): pl.pallas_call(functools.partial(first_kernel, sizes, low), in_specs=[HBM...  2.69 us
    pallas_call x1, Pallas kernels, column_sums(): pl.pallas_call(column_kernel, in_specs=[SMEM, VMEM, ANY], out_specs=VMEM,...  1.78 us
  transfers between devices with their start and end apart: 14, of which 8 were waited for; matrix products, arithmetic and copies ran while one was open for 0% of the time, Pallas kernels for 20%

profile of v4, /device:TPU:0, one launch (start us, length us, event | category | flops | bytes accessed | tf_op | source)
XLA Modules:
  0.0 64.1 jit_solution(8962855084876244840)
XLA Ops:
  0.0 2.7 %shard_map.73 = (s16[1040,128]{1,0:T(8,128)(2,1)S(1)}, bf16[32,4,128,128]{3,2,1,0:T(8,128)(2,1)S(1)}, bf16[6,128,128]{2,1,0:T(8,128)(2,1)S(1)}, s32[12,32]{1,0:T(8,128)S(1)}) custom-call(s32[32]{0:T(128)} %ray_hbm.1, s32[4,32]{1,0:T(4,128)} %bitcast.1, bf16[32,4,128,128]{3,2,1,0:T(8,128)(2,1)} %projector_hbm.1, bf16[6,128,128]{2,1,0:T(8,128)(2,1)} %volume_hbm.1), custom_call_target="tpu_custom_call" | custom-call | flops 1 | bytes 1 | tf_op jit(solution)/shard_map/pallas_call | solution.py:170
  2.7 2.8 %collective-permute-start = (s16[1040,128]{1,0:T(8,128)(2,1)S(1)}, s16[1040,128]{1,0:T(8,128)(2,1)S(1)}, u32[]{:S(2)}, u32[]{:S(2)}) collective-permute-start(s16[1040,128]{1,0:T(8,128)(2,1)S(1)} %get-tuple-element.14.after), channel_id=1, source_target_pairs={{0,2},{2,0},{1,3},{3,1},{4,6},{6,4},{5,7},{7,5},{8,10},{10,8},{9,1... | collective-permute-start | bytes 798728 | tf_op jit(solution)/shard_map/ppermute | solution.py:29
  5.5 1.4 %shard_map.74.after = s16[1040,128]{1,0:T(8,128)(2,1)S(1)} custom-call(s32[12,32]{1,0:T(8,128)S(1)} %get-tuple-element.11.table_from.table_ref.refs_0_, bf16[32,4,128,128]{3,2,1,0:T(8,128)(2,1)S(1)} %get-tuple-element.12.projector_ref.refs_1_, bf16[6,128,128]{2,1,0:T(8,128)(2,1)S(1)} %get-tuple-element.13.volume_ref.rest_1_, ...), custom_call_target="tpu_custom_call" | custom-call | flops 1 | bytes 1 | tf_op jit(solution)/shard_map/pallas_call | solution.py:228
  6.8 2.5 %collective-permute-start.1 = (s16[1040,128]{1,0:T(8,128)(2,1)S(1)}, s16[1040,128]{1,0:T(8,128)(2,1)S(1)}, u32[]{:S(2)}, u32[]{:S(2)}) collective-permute-start(s16[1040,128]{1,0:T(8,128)(2,1)S(1)} %shard_map.74.after), channel_id=1, source_target_pairs={{0,4},{4,0},{8,12},{12,8},{1,5},{5,1},{9,13},{13,9},{2,6},{6,2},{1... | collective-permute-start | bytes 798728 | tf_op jit(solution)/shard_map/ppermute | solution.py:29
  9.3 2.7 %shard_map.75 = (s16[1040,128]{1,0:T(8,128)(2,1)S(1)}, f32[17,128,128]{2,1,0:T(8,128)S(1)}) custom-call(s32[12,32]{1,0:T(8,128)S(1)} %get-tuple-element.11.table_from.table_ref.refs_0_, bf16[32,4,128,128]{3,2,1,0:T(8,128)(2,1)S(1)} %get-tuple-element.12.projector_ref.refs_1_, bf16[6,128,128]{2,1,0:T(8,128)(2,1)S(1)} %get-tuple-element.13.volume_ref.rest_1_, ...), custom_call_target="tpu_custom_call" | custom-call | flops 1 | bytes 1 | tf_op jit(solution)/shard_map/pallas_call | solution.py:228
  12.1 0.0 collective-permute-done.rest_0_
  12.1 0.2 shard_map.76.after.refs_1_
  12.3 1.6 %collective-permute-start.3 = (s16[1040,128]{1,0:T(8,128)(2,1)S(1)}, s16[1040,128]{1,0:T(8,128)(2,1)S(1)}, u32[]{:S(2)}, u32[]{:S(2)}) collective-permute-start(s16[1040,128]{1,0:T(8,128)(2,1)S(1)} %shard_map.79), channel_id=1, source_target_pairs={{0,2},{2,0},{1,3},{3,1},{4,6},{6,4},{5,7},{7,5},{8,10},{10,8},{9,1... | collective-permute-start | bytes 798728 | tf_op jit(solution)/shard_map/ppermute | solution.py:29
  13.9 2.2 %collective-permute-start.2 = (s16[1040,128]{1,0:T(8,128)(2,1)S(1)}, s16[1040,128]{1,0:T(8,128)(2,1)S(1)}, u32[]{:S(2)}, u32[]{:S(2)}) collective-permute-start(s16[1040,128]{1,0:T(8,128)(2,1)S(1)} %shard_map.76.after.refs_1_), channel_id=1, source_target_pairs={{0,4},{4,0},{8,12},{12,8},{1,5},{5,1},{9,13},{13,9},{2,6},{6,2},{1... | collective-permute-start | bytes 798728 | tf_op jit(solution)/shard_map/ppermute | solution.py:29
  16.1 1.5 %shard_map.77.own_ref = f32[25,128,128]{2,1,0:T(8,128)S(1)} custom-call(s32[12,32]{1,0:T(8,128)S(1)} %get-tuple-element.11.table_from.table_ref.refs_0_, bf16[32,4,128,128]{3,2,1,0:T(8,128)(2,1)S(1)} %get-tuple-element.12.projector_ref.refs_1_, bf16[6,128,128]{2,1,0:T(8,128)(2,1)S(1)} %get-tuple-element.13.volume_ref.rest_1_, ...), custom_call_target="tpu_custom_call" | custom-call | flops 1 | bytes 1 | tf_op jit(solution)/shard_map/pallas_call | solution.py:228
  17.6 0.0 copy-start.2
  17.6 0.0 collective-permute-done.1.rest_0_
  17.6 0.2 shard_map.78.after
  17.8 0.0 copy-start.1
  17.8 2.2 %collective-permute-done.3.rest_1_ = s16[1040,128]{1,0:T(8,128)(2,1)S(1)} collective-permute-done((s16[1040,128]{1,0:T(8,128)(2,1)S(1)}, s16[1040,128]{1,0:T(8,128)(2,1)S(1)}, u32[]{:S(2)}, u32[]{:S(2)}) %collective-permute-start.3) | collective-permute-done | bytes 266272 | tf_op jit(solution)/shard_map/ppermute | solution.py:29
  19.9 1.4 %collective-permute-done.2.rest_0_ = s16[1040,128]{1,0:T(8,128)(2,1)S(1)} collective-permute-done((s16[1040,128]{1,0:T(8,128)(2,1)S(1)}, s16[1040,128]{1,0:T(8,128)(2,1)S(1)}, u32[]{:S(2)}, u32[]{:S(2)}) %collective-permute-start.2) | collective-permute-done | bytes 266272 | tf_op jit(solution)/shard_map/ppermute | solution.py:29
  21.3 0.2 shard_map.80.after
  21.5 0.1 shard_map.81.after
  21.7 0.0 copy-start
  21.7 1.8 %collective-permute-start.5 = (s16[1040,128]{1,0:T(8,128)(2,1)S(1)}, s16[1040,128]{1,0:T(8,128)(2,1)S(1)}, u32[]{:S(2)}, u32[]{:S(2)}) collective-permute-start(s16[1040,128]{1,0:T(8,128)(2,1)S(1)} %shard_map.81.after), channel_id=1, source_target_pairs={{0,4},{4,0},{8,12},{12,8},{1,5},{5,1},{9,13},{13,9},{2,6},{6,2},{1... | collective-permute-start | bytes 798728 | tf_op jit(solution)/shard_map/ppermute | solution.py:29
  23.5 2.2 %collective-permute-start.4 = (s16[1040,128]{1,0:T(8,128)(2,1)S(1)}, s16[1040,128]{1,0:T(8,128)(2,1)S(1)}, u32[]{:S(2)}, u32[]{:S(2)}) collective-permute-start(s16[1040,128]{1,0:T(8,128)(2,1)S(1)} %shard_map.80.after), channel_id=1, source_target_pairs={{0,8},{4,12},{8,0},{12,4},{1,9},{5,13},{9,1},{13,5},{2,10},{6,14},... | collective-permute-start | bytes 798728 | tf_op jit(solution)/shard_map/ppermute | solution.py:29
  25.7 0.5 collective-permute-start.6
  26.2 0.0 copy-done.2
  26.2 1.8 %shard_map.83.after.rest_2_ = f32[6,1,128]{2,1,0:T(1,128)S(1)} custom-call(s32[12,32]{1,0:T(8,128)S(1)} %get-tuple-element.11.table_from.table_ref.refs_0_, bf16[32,4,128,128]{3,2,1,0:T(8,128)(2,1)S(1)} %get-tuple-element.12.projector_ref.refs_1_, s16[1040,128]{1,0:T(8,128)(2,1)S(1)} %shard_map.81.after), custom_call_target="tpu_custom_call" | custom-call | flops 1 | bytes 1 | tf_op jit(solution)/shard_map/pallas_call | solution.py:338
  28.0 0.0 copy-done.1
  28.0 0.7 %shard_map.84.weight_ref = bf16[8,128,128]{2,1,0:T(8,128)(2,1)S(1)} custom-call(f32[16]{0:T(128)S(1)} %convert_element_type.3.table_ref, s32[8,128]{1,0:T(8,128)S(1)} %copy-done.1, f32[6,1,128]{2,1,0:T(1,128)S(1)} %shard_map.83.after.rest_2_), custom_call_target="tpu_custom_call" | custom-call | flops 1 | bytes 1 | tf_op jit(solution)/shard_map/pallas_call | solution.py:292
  28.7 4.3 %collective-permute-done.5.rest_1_ = s16[1040,128]{1,0:T(8,128)(2,1)S(1)} collective-permute-done((s16[1040,128]{1,0:T(8,128)(2,1)S(1)}, s16[1040,128]{1,0:T(8,128)(2,1)S(1)}, u32[]{:S(2)}, u32[]{:S(2)}) %collective-permute-start.5) | collective-permute-done | bytes 266272 | tf_op jit(solution)/shard_map/ppermute | solution.py:29
  33.0 6.4 %collective-permute-done.4.rest_0_ = s16[1040,128]{1,0:T(8,128)(2,1)S(1)} collective-permute-done((s16[1040,128]{1,0:T(8,128)(2,1)S(1)}, s16[1040,128]{1,0:T(8,128)(2,1)S(1)}, u32[]{:S(2)}, u32[]{:S(2)}) %collective-permute-start.4) | collective-permute-done | bytes 266272 | tf_op jit(solution)/shard_map/ppermute | solution.py:29
  39.5 0.2 shard_map.82.sum_ref
  39.6 0.0 collective-permute-done.6.rest_0_
  39.6 0.0 copy-done
  39.7 0.2 shard_map.85.refs_2_
  39.8 0.1 collective-permute-start.8
  39.9 1.9 %collective-permute-start.7 = (bf16[8,128,128]{2,1,0:T(8,128)(2,1)S(1)}, bf16[8,128,128]{2,1,0:T(8,128)(2,1)S(1)}, u32[]{:S(2)}, u32[]{:S(2)}) collective-permute-start(bf16[8,128,128]{2,1,0:T(8,128)(2,1)S(1)} %shard_map.85.refs_2_), channel_id=1, source_target_pairs={{0,4},{4,0},{8,12},{12,8},{1,5},{5,1},{9,13},{13,9},{2,6},{6,2},{1... | collective-permute-start | bytes 786440 | tf_op jit(solution)/shard_map/ppermute | solution.py:29
  41.8 0.7 %collective-permute-start.9 = (bf16[8,128,128]{2,1,0:T(8,128)(2,1)S(1)}, bf16[8,128,128]{2,1,0:T(8,128)(2,1)S(1)}, u32[]{:S(2)}, u32[]{:S(2)}) collective-permute-start(bf16[8,128,128]{2,1,0:T(8,128)(2,1)S(1)} %shard_map.85.refs_2_), channel_id=1, source_target_pairs={{0,2},{2,0},{1,3},{3,1},{4,6},{6,4},{5,7},{7,5},{8,10},{10,8},{9,1... | collective-permute-start | bytes 786440 | tf_op jit(solution)/shard_map/ppermute | solution.py:29
  42.4 6.0 %collective-permute-done.8.refs_4_ = bf16[8,128,128]{2,1,0:T(8,128)(2,1)S(1)} collective-permute-done((bf16[8,128,128]{2,1,0:T(8,128)(2,1)S(1)}, bf16[8,128,128]{2,1,0:T(8,128)(2,1)S(1)}, u32[]{:S(2)}, u32[]{:S(2)}) %collective-permute-start.8) | collective-permute-done | bytes 262176 | tf_op jit(solution)/shard_map/ppermute | solution.py:29
  48.5 0.0 collective-permute-start.10
  48.5 0.7 %collective-permute-start.11 = (bf16[8,128,128]{2,1,0:T(8,128)(2,1)S(1)}, bf16[8,128,128]{2,1,0:T(8,128)(2,1)S(1)}, u32[]{:S(2)}, u32[]{:S(2)}) collective-permute-start(bf16[8,128,128]{2,1,0:T(8,128)(2,1)S(1)} %collective-permute-done.8.refs_4_), channel_id=1, source_target_pairs={{0,2},{2,0},{1,3},{3,1},{4,6},{6,4},{5,7},{7,5},{8,10},{10,8},{9,1... | collective-permute-start | bytes 786440 | tf_op jit(solution)/shard_map/ppermute | solution.py:29
  49.1 2.4 %collective-permute-done.7.refs_3_ = bf16[8,128,128]{2,1,0:T(8,128)(2,1)S(1)} collective-permute-done((bf16[8,128,128]{2,1,0:T(8,128)(2,1)S(1)}, bf16[8,128,128]{2,1,0:T(8,128)(2,1)S(1)}, u32[]{:S(2)}, u32[]{:S(2)}) %collective-permute-start.7) | collective-permute-done | bytes 262176 | tf_op jit(solution)/shard_map/ppermute | solution.py:29
  51.5 0.0 collective-permute-done.9.refs_5_.refs_0_
  51.5 2.3 %shard_map.86.refs_1_.refs_2_ = f32[7,128,128]{2,1,0:T(8,128)S(1)} custom-call(s32[12,32]{1,0:T(8,128)S(1)} %get-tuple-element.11.table_from.table_ref.refs_0_, bf16[32,4,128,128]{3,2,1,0:T(8,128)(2,1)S(1)} %get-tuple-element.12.projector_ref.refs_1_, bf16[8,128,128]{2,1,0:T(8,128)(2,1)S(1)} %shard_map.85.refs_2_, ...), custom_call_target="tpu_custom_call" | custom-call | flops 1 | bytes 1 | tf_op jit(solution)/shard_map/pallas_call | solution.py:406
  53.8 1.4 %collective-permute-done.10.refs_0_ = bf16[8,128,128]{2,1,0:T(8,128)(2,1)S(1)} collective-permute-done((bf16[8,128,128]{2,1,0:T(8,128)(2,1)S(1)}, bf16[8,128,128]{2,1,0:T(8,128)(2,1)S(1)}, u32[]{:S(2)}, u32[]{:S(2)}) %collective-permute-start.10) | collective-permute-done | bytes 262176 | tf_op jit(solution)/shard_map/ppermute | solution.py:29
  55.3 0.0 collective-permute-start.13
  55.3 0.7 %collective-permute-start.12 = (bf16[8,128,128]{2,1,0:T(8,128)(2,1)S(1)}, bf16[8,128,128]{2,1,0:T(8,128)(2,1)S(1)}, u32[]{:S(2)}, u32[]{:S(2)}) collective-permute-start(bf16[8,128,128]{2,1,0:T(8,128)(2,1)S(1)} %shard_map.87.refs_3_.refs_1_), channel_id=1, source_target_pairs={{0,2},{2,0},{1,3},{3,1},{4,6},{6,4},{5,7},{7,5},{8,10},{10,8},{9,1... | collective-permute-start | bytes 786440 | tf_op jit(solution)/shard_map/ppermute | solution.py:29
  56.0 0.0 collective-permute-done.11.refs_4_
  56.0 1.9 %shard_map.88.rest_0_ = f32[7,128,128]{2,1,0:T(8,128)S(1)} custom-call(s32[12,32]{1,0:T(8,128)S(1)} %get-tuple-element.11.table_from.table_ref.refs_0_, bf16[32,4,128,128]{3,2,1,0:T(8,128)(2,1)S(1)} %get-tuple-element.12.projector_ref.refs_1_, f32[7,128,128]{2,1,0:T(8,128)S(1)} %shard_map.86.refs_1_.refs_2_, ...), custom_call_target="tpu_custom_call" | custom-call | flops 1 | bytes 1 | tf_op jit(solution)/shard_map/pallas_call | solution.py:406
  57.9 3.8 %collective-permute-done.13.rest_4_ = bf16[8,128,128]{2,1,0:T(8,128)(2,1)S(1)} collective-permute-done((bf16[8,128,128]{2,1,0:T(8,128)(2,1)S(1)}, bf16[8,128,128]{2,1,0:T(8,128)(2,1)S(1)}, u32[]{:S(2)}, u32[]{:S(2)}) %collective-permute-start.13) | collective-permute-done | bytes 262176 | tf_op jit(solution)/shard_map/ppermute | solution.py:29
  61.6 0.0 collective-permute-done.12.rest_3_
  61.6 2.4 %shard_map.90 = f32[6,128,128]{2,1,0:T(8,128)} custom-call(s32[12,32]{1,0:T(8,128)S(1)} %get-tuple-element.11.table_from.table_ref.refs_0_, bf16[32,4,128,128]{3,2,1,0:T(8,128)(2,1)S(1)} %get-tuple-element.12.projector_ref.refs_1_, f32[7,128,128]{2,1,0:T(8,128)S(1)} %shard_map.88.rest_0_, bf16[6,128,128]{2,1,0:T(8,128)(2,1)S(1)} %get-tuple-element.13.volume_ref.rest_1_, ...), custom_call_target="tpu_custom_call" | custom-call | flops 1 | bytes 1 | tf_op jit(solution)/shard_map/pallas_call | solution.py:406
  (4 shorter events, 0.0 us)
Async XLA Ops:
  2.7 9.4 %collective-permute-start = (s16[1040,128]{1,0:T(8,128)(2,1)S(1)}, s16[1040,128]{1,0:T(8,128)(2,1)S(1)}, u32[]{:S(2)}, u32[]{:S(2)}) collective-permute-start(s16[1040,128]{1,0:T(8,128)(2,1)S(1)} %get-tuple-element.14.after), channel_id=1, source_target_pairs={{0,2},{2,0},{1,3},{3,1},{4,6},{6,4},{5,7},{7,5},{8,10},{10,8},{9,1... | collective-permute-start | bytes 798728 | tf_op jit(solution)/shard_map/ppermute | solution.py:29
  6.8 10.7 %collective-permute-start.1 = (s16[1040,128]{1,0:T(8,128)(2,1)S(1)}, s16[1040,128]{1,0:T(8,128)(2,1)S(1)}, u32[]{:S(2)}, u32[]{:S(2)}) collective-permute-start(s16[1040,128]{1,0:T(8,128)(2,1)S(1)} %shard_map.74.after), channel_id=1, source_target_pairs={{0,4},{4,0},{8,12},{12,8},{1,5},{5,1},{9,13},{13,9},{2,6},{6,2},{1... | collective-permute-start | bytes 798728 | tf_op jit(solution)/shard_map/ppermute | solution.py:29
  12.3 7.6 %collective-permute-start.3 = (s16[1040,128]{1,0:T(8,128)(2,1)S(1)}, s16[1040,128]{1,0:T(8,128)(2,1)S(1)}, u32[]{:S(2)}, u32[]{:S(2)}) collective-permute-start(s16[1040,128]{1,0:T(8,128)(2,1)S(1)} %shard_map.79), channel_id=1, source_target_pairs={{0,2},{2,0},{1,3},{3,1},{4,6},{6,4},{5,7},{7,5},{8,10},{10,8},{9,1... | collective-permute-start | bytes 798728 | tf_op jit(solution)/shard_map/ppermute | solution.py:29
  13.9 7.4 %collective-permute-start.2 = (s16[1040,128]{1,0:T(8,128)(2,1)S(1)}, s16[1040,128]{1,0:T(8,128)(2,1)S(1)}, u32[]{:S(2)}, u32[]{:S(2)}) collective-permute-start(s16[1040,128]{1,0:T(8,128)(2,1)S(1)} %shard_map.76.after.refs_1_), channel_id=1, source_target_pairs={{0,4},{4,0},{8,12},{12,8},{1,5},{5,1},{9,13},{13,9},{2,6},{6,2},{1... | collective-permute-start | bytes 798728 | tf_op jit(solution)/shard_map/ppermute | solution.py:29
  17.6 8.6 %copy-start.2 = (bf16[16]{0:T(256)(128)(2,1)S(1)}, bf16[16]{0:T(256)(128)(2,1)}, u32[]{:S(2)}) copy-start(bf16[16]{0:T(256)(128)(2,1)} %param.13) | copy-start | bytes 100
  17.8 10.2 %copy-start.1 = (s32[8,128]{1,0:T(8,128)S(1)}, s32[8,128]{1,0:T(8,128)}, u32[]{:S(2)}) copy-start(s32[8,128]{1,0:T(8,128)} %index_ref.1) | copy-start | bytes 12292
  21.7 18.0 %copy-start = (bf16[8,128,128]{2,1,0:T(8,128)(2,1)S(1)}, bf16[8,128,128]{2,1,0:T(8,128)(2,1)}, u32[]{:S(2)}) copy-start(bf16[8,128,128]{2,1,0:T(8,128)(2,1)} %sinogram_ref.1) | copy-start | bytes 786436
  21.7 11.4 %collective-permute-start.5 = (s16[1040,128]{1,0:T(8,128)(2,1)S(1)}, s16[1040,128]{1,0:T(8,128)(2,1)S(1)}, u32[]{:S(2)}, u32[]{:S(2)}) collective-permute-start(s16[1040,128]{1,0:T(8,128)(2,1)S(1)} %shard_map.81.after), channel_id=1, source_target_pairs={{0,4},{4,0},{8,12},{12,8},{1,5},{5,1},{9,13},{13,9},{2,6},{6,2},{1... | collective-permute-start | bytes 798728 | tf_op jit(solution)/shard_map/ppermute | solution.py:29
  23.5 16.0 %collective-permute-start.4 = (s16[1040,128]{1,0:T(8,128)(2,1)S(1)}, s16[1040,128]{1,0:T(8,128)(2,1)S(1)}, u32[]{:S(2)}, u32[]{:S(2)}) collective-permute-start(s16[1040,128]{1,0:T(8,128)(2,1)S(1)} %shard_map.80.after), channel_id=1, source_target_pairs={{0,8},{4,12},{8,0},{12,4},{1,9},{5,13},{9,1},{13,5},{2,10},{6,14},... | collective-permute-start | bytes 798728 | tf_op jit(solution)/shard_map/ppermute | solution.py:29
  25.7 14.0 %collective-permute-start.6 = (s16[1040,128]{1,0:T(8,128)(2,1)S(1)}, s16[1040,128]{1,0:T(8,128)(2,1)S(1)}, u32[]{:S(2)}, u32[]{:S(2)}) collective-permute-start(s16[1040,128]{1,0:T(8,128)(2,1)S(1)} %shard_map.78.after), channel_id=1, source_target_pairs={{0,2},{2,0},{1,3},{3,1},{4,6},{6,4},{5,7},{7,5},{8,10},{10,8},{9,1... | collective-permute-start | bytes 798728 | tf_op jit(solution)/shard_map/ppermute | solution.py:29
  39.8 8.7 %collective-permute-start.8 = (bf16[8,128,128]{2,1,0:T(8,128)(2,1)S(1)}, bf16[8,128,128]{2,1,0:T(8,128)(2,1)S(1)}, u32[]{:S(2)}, u32[]{:S(2)}) collective-permute-start(bf16[8,128,128]{2,1,0:T(8,128)(2,1)S(1)} %shard_map.85.refs_2_), channel_id=1, source_target_pairs={{0,8},{4,12},{8,0},{12,4},{1,9},{5,13},{9,1},{13,5},{2,10},{6,14},... | collective-permute-start | bytes 786440 | tf_op jit(solution)/shard_map/ppermute | solution.py:29
  39.9 11.6 %collective-permute-start.7 = (bf16[8,128,128]{2,1,0:T(8,128)(2,1)S(1)}, bf16[8,128,128]{2,1,0:T(8,128)(2,1)S(1)}, u32[]{:S(2)}, u32[]{:S(2)}) collective-permute-start(bf16[8,128,128]{2,1,0:T(8,128)(2,1)S(1)} %shard_map.85.refs_2_), channel_id=1, source_target_pairs={{0,4},{4,0},{8,12},{12,8},{1,5},{5,1},{9,13},{13,9},{2,6},{6,2},{1... | collective-permute-start | bytes 786440 | tf_op jit(solution)/shard_map/ppermute | solution.py:29
  41.8 9.8 %collective-permute-start.9 = (bf16[8,128,128]{2,1,0:T(8,128)(2,1)S(1)}, bf16[8,128,128]{2,1,0:T(8,128)(2,1)S(1)}, u32[]{:S(2)}, u32[]{:S(2)}) collective-permute-start(bf16[8,128,128]{2,1,0:T(8,128)(2,1)S(1)} %shard_map.85.refs_2_), channel_id=1, source_target_pairs={{0,2},{2,0},{1,3},{3,1},{4,6},{6,4},{5,7},{7,5},{8,10},{10,8},{9,1... | collective-permute-start | bytes 786440 | tf_op jit(solution)/shard_map/ppermute | solution.py:29
  48.5 6.8 %collective-permute-start.10 = (bf16[8,128,128]{2,1,0:T(8,128)(2,1)S(1)}, bf16[8,128,128]{2,1,0:T(8,128)(2,1)S(1)}, u32[]{:S(2)}, u32[]{:S(2)}) collective-permute-start(bf16[8,128,128]{2,1,0:T(8,128)(2,1)S(1)} %collective-permute-done.8.refs_4_), channel_id=1, source_target_pairs={{0,4},{4,0},{8,12},{12,8},{1,5},{5,1},{9,13},{13,9},{2,6},{6,2},{1... | collective-permute-start | bytes 786440 | tf_op jit(solution)/shard_map/ppermute | solution.py:29
  48.5 7.5 %collective-permute-start.11 = (bf16[8,128,128]{2,1,0:T(8,128)(2,1)S(1)}, bf16[8,128,128]{2,1,0:T(8,128)(2,1)S(1)}, u32[]{:S(2)}, u32[]{:S(2)}) collective-permute-start(bf16[8,128,128]{2,1,0:T(8,128)(2,1)S(1)} %collective-permute-done.8.refs_4_), channel_id=1, source_target_pairs={{0,2},{2,0},{1,3},{3,1},{4,6},{6,4},{5,7},{7,5},{8,10},{10,8},{9,1... | collective-permute-start | bytes 786440 | tf_op jit(solution)/shard_map/ppermute | solution.py:29
  55.3 6.4 %collective-permute-start.13 = (bf16[8,128,128]{2,1,0:T(8,128)(2,1)S(1)}, bf16[8,128,128]{2,1,0:T(8,128)(2,1)S(1)}, u32[]{:S(2)}, u32[]{:S(2)}) collective-permute-start(bf16[8,128,128]{2,1,0:T(8,128)(2,1)S(1)} %shard_map.89), channel_id=1, source_target_pairs={{0,4},{4,0},{8,12},{12,8},{1,5},{5,1},{9,13},{13,9},{2,6},{6,2},{1... | collective-permute-start | bytes 786440 | tf_op jit(solution)/shard_map/ppermute | solution.py:29
  55.3 6.4 %collective-permute-start.12 = (bf16[8,128,128]{2,1,0:T(8,128)(2,1)S(1)}, bf16[8,128,128]{2,1,0:T(8,128)(2,1)S(1)}, u32[]{:S(2)}, u32[]{:S(2)}) collective-permute-start(bf16[8,128,128]{2,1,0:T(8,128)(2,1)S(1)} %shard_map.87.refs_3_.refs_1_), channel_id=1, source_target_pairs={{0,2},{2,0},{1,3},{3,1},{4,6},{6,4},{5,7},{7,5},{8,10},{10,8},{9,1... | collective-permute-start | bytes 786440 | tf_op jit(solution)/shard_map/ppermute | solution.py:29

commit v5 on v4

--- a/solution.py
+++ b/solution.py
@@ -11,12 +11,17 @@
 FULL = 32700.0
 UNROLL = 4
 LATER = True
-EARLY = False
 VMEM = pl.BlockSpec(memory_space=pltpu.VMEM)
 SMEM = pl.BlockSpec(memory_space=pltpu.SMEM)
 HBM = pl.BlockSpec(memory_space=pltpu.HBM)
 ANY = pl.BlockSpec(memory_space=pl.ANY)
-QUICK = pl.CostEstimate(flops=1, bytes_accessed=1, transcendentals=0)
+
+
+def weighs(weight):
+    return pl.CostEstimate(flops=max(int(weight * 1e9), 1), bytes_accessed=1, transcendentals=0)
+
+
+QUICK = weighs(0)
 PARAMS = pltpu.CompilerParams(vmem_limit_bytes=24 * 2**20)
 
 
@@ -414,7 +419,7 @@
     )(table, projector, *more)
 
 
-def gate(value, *after):
+def gate(value, *after, weight=0):
     return pl.pallas_call(
         lambda *refs: None,
         in_specs=[VMEM] * (1 + len(after)),
@@ -422,7 +427,7 @@
         out_shape=jax.ShapeDtypeStruct(value.shape, value.dtype),
         input_output_aliases={0: 0},
         compiler_params=PARAMS,
-        cost_estimate=QUICK,
+        cost_estimate=weighs(weight),
     )(value, *after)
 
 
@@ -458,14 +463,14 @@
     sends.update(zip(sent, payloads))
     for k in far[:1]:
         for j in others:
-            arrived[0, k].append(swap(sends[j, k], "outer", j))
+            arrived[0, k].append(gate(swap(sends[j, k], "outer", j), weight=4))
     for j in others:
         arrived[j, 0].append(swap(sends[j, 1], "inner", 1))
     after = own
     for i, k in enumerate(far):
         bit = k & -k
         after = combine(own, low(0, k) - low(0, 2), tiles, arrived[0, k], after)
-        arrived[0, k ^ bit].append(swap(after, "inner", bit))
+        arrived[0, k ^ bit].append(swap(after, "inner", bit) if i == 0 else gate(swap(after, "inner", bit)))
         if i == 0:
             (near_own,) = further_sums(table, projector, volume, tiles, [], kept[1:], after)
             for l in far[1:]:
@@ -476,7 +481,7 @@
                 after = combine(near_own, 2 * tiles, tiles, arrived[j, 0], after)
                 arrived[0, 0].append(swap(after, "outer", j))
     after = combine(near_own, tiles, tiles, [], after)
-    arrived[0, 0].append(swap(after, "inner", 1))
+    arrived[0, 0].append(gate(swap(after, "inner", 1)))
     columns = column_sums(table, projector, patch_tiles, after)
     weights = ray_weights(weight_table, weight_index, slices, columns)
     longest = arrived[0, 0][-2:]
@@ -495,34 +500,18 @@
             [chunks[piece] for piece in pieces], patch_tiles, total, last,
         )
 
-    bit = inners // 2
-    while bit:
-        chunks[0, bit] = swap(residual, "inner", bit)
-        bit //= 2
-    for j in others:
-        chunks[j, 0] = swap(residual, "outer", j)
-    done = {(0, 0), (0, 1)} | {(j, 0) for j in others}
-    for i, k in enumerate(turns[2:]):
-        if i == 0 and EARLY:
-            for j in others:
-                chunks[j, 1] = swap(chunks[j, 0], "inner", 1)
-            chunks[0, k] = gate(chunks[0, k], chunks[0, 1], *[chunks[j, 0] for j in others])
-        if k == turns[-1]:
-            done |= {(0, l) for l in turns[:-1]}
-            add(sorted(done))
-            chunks[0, k] = gate(chunks[0, k], total)
-        bit = (k & -k) // 2
-        while bit:
-            chunks[0, k ^ bit] = swap(chunks[0, k], "inner", bit)
-            bit //= 2
-        for j in others:
-            chunks[j, k] = swap(chunks[0, k], "outer", j)
-    if not EARLY:
-        for j in others:
-            chunks[j, 1] = swap(gate(chunks[j, 0], chunks[0, turns[-1]]), "inner", 1)
-    ends = [(j, turns[-1]) for j in others] + ([] if EARLY else [(j, 1) for j in others])
-    add([piece for piece in chunks if piece not in ends and piece not in done])
-    add(ends, (volume, columns))
+    chunks[0, 2] = swap(residual, "inner", 2)
+    chunks[0, 1] = gate(swap(residual, "inner", 1), weight=2)
+    chunks[1, 0] = swap(residual, "outer", 1)
+    chunks[0, 3] = swap(chunks[0, 2], "inner", 1)
+    chunks[1, 2] = swap(chunks[0, 2], "outer", 1)
+    done = [(0, 0), (0, 1), (0, 2), (1, 0)]
+    add(done)
+    chunks[0, 3] = gate(chunks[0, 3], total)
+    chunks[1, 3] = swap(chunks[0, 3], "outer", 1)
+    chunks[1, 1] = swap(gate(chunks[1, 0], chunks[0, 3]), "inner", 1)
+    add([(0, 3), (1, 2)])
+    add([(1, 3), (1, 1)], (volume, columns))
     return total
 
 
@@ -621,8 +610,8 @@
     inners = lax.axis_size("inner")
     outers = lax.axis_size("outer")
     capacity = 2 * slot_ray.shape[0] // inners
-    powers = inners & (inners - 1) == 0 and outers & (outers - 1) == 0 and inners > 1 < outers
-    plan = dense_plan if powers and sinogram.shape[0] * outers <= capacity else slot_plan
+    dense = (inners, outers) == (4, 2) and sinogram.shape[0] * outers <= capacity
+    plan = dense_plan if dense else slot_plan
     return plan(volume, projector, slot_ray, slot_pixel, sinogram, weight_index, weight_table)
 
 

time: 64.9 us -> 64.5 us (level); the launches traced: 64.1 us -> 64.5 us
  starting transfers between devices: 17.6 us -> 23.9 us
  waiting for transfers between devices: 27.9 us -> 22.1 us
    ppermute x14, starting transfers between devices: 17.6 us -> 23.9 us  [swap(): return lax.ppermute(value, axis, [(i, i ^ bits) for i in range(size)])]
    ppermute x14, waiting for transfers between devices: 27.9 us -> 22.1 us  [swap(): return lax.ppermute(value, axis, [(i, i ^ bits) for i in range(size)])]
  transfers between devices with their start and end apart: 14 -> 14, of which waited for: 8 -> 10; matrix products, arithmetic and copies ran while one was open for 0% -> 0% of each run, Pallas kernels for 20% -> 19%
where the time goes in v5:
time: 64.5 us
  starting transfers between devices  23.9 us (37%)
  waiting for transfers between devices  22.1 us (34%)
  Pallas kernels  18.3 us (28%)
    ppermute x14, starting transfers between devices, swap(): return lax.ppermute(value, axis, [(i, i ^ bits) for i in range(size)])  23.9 us
    ppermute x14, waiting for transfers between devices, swap(): return lax.ppermute(value, axis, [(i, i ^ bits) for i in range(size)])  22.1 us
    pallas_call x3, Pallas kernels, spread(): pl.pallas_call(kernel, in_specs=[VMEM] * (2 + len(more)), out_specs=VMEM,...  6.62 us
    pallas_call x3, Pallas kernels, further_sums(): pl.pallas_call(functools.partial(further_kernel, tiles, sent, ranges), in...  5.72 us
    pallas_call x1, Pallas kernels, first_send(): pl.pallas_call(functools.partial(first_kernel, sizes, low), in_specs=[HBM...  2.53 us
    pallas_call x1, Pallas kernels, column_sums(): pl.pallas_call(column_kernel, in_specs=[SMEM, VMEM, ANY], out_specs=VMEM,...  1.78 us
  transfers between devices with their start and end apart: 14, of which 10 were waited for; matrix products, arithmetic and copies ran while one was open for 0% of the time, Pallas kernels for 19%

profile of v5, /device:TPU:0, one launch (start us, length us, event | category | flops | bytes accessed | tf_op | source)
XLA Modules:
  0.0 64.5 jit_solution(13466118640378799699)
XLA Ops:
  0.0 2.5 %shard_map.73 = (s16[1040,128]{1,0:T(8,128)(2,1)S(1)}, bf16[32,4,128,128]{3,2,1,0:T(8,128)(2,1)S(1)}, bf16[6,128,128]{2,1,0:T(8,128)(2,1)S(1)}, s32[12,32]{1,0:T(8,128)S(1)}) custom-call(s32[32]{0:T(128)} %ray_hbm.1, s32[4,32]{1,0:T(4,128)} %bitcast.1, bf16[32,4,128,128]{3,2,1,0:T(8,128)(2,1)} %projector_hbm.1, bf16[6,128,128]{2,1,0:T(8,128)(2,1)} %volume_hbm.1), custom_call_target="tpu_custom_call" | custom-call | flops 1 | bytes 1 | tf_op jit(solution)/shard_map/pallas_call | solution.py:175
  2.5 3.4 %collective-permute-start = (s16[1040,128]{1,0:T(8,128)(2,1)S(1)}, s16[1040,128]{1,0:T(8,128)(2,1)S(1)}, u32[]{:S(2)}, u32[]{:S(2)}) collective-permute-start(s16[1040,128]{1,0:T(8,128)(2,1)S(1)} %get-tuple-element.14.after), channel_id=1, source_target_pairs={{0,2},{2,0},{1,3},{3,1},{4,6},{6,4},{5,7},{7,5},{8,10},{10,8},{9,1... | collective-permute-start | bytes 798728 | tf_op jit(solution)/shard_map/ppermute | solution.py:34
  5.9 1.6 %shard_map.74.after = s16[1040,128]{1,0:T(8,128)(2,1)S(1)} custom-call(s32[12,32]{1,0:T(8,128)S(1)} %get-tuple-element.11.table_from.table_ref.refs_0_, bf16[32,4,128,128]{3,2,1,0:T(8,128)(2,1)S(1)} %get-tuple-element.12.projector_ref.refs_1_, bf16[6,128,128]{2,1,0:T(8,128)(2,1)S(1)} %get-tuple-element.13.volume_ref.rest_1_, ...), custom_call_target="tpu_custom_call" | custom-call | flops 1 | bytes 1 | tf_op jit(solution)/shard_map/pallas_call | solution.py:233
  7.5 1.2 %collective-permute-start.1 = (s16[1040,128]{1,0:T(8,128)(2,1)S(1)}, s16[1040,128]{1,0:T(8,128)(2,1)S(1)}, u32[]{:S(2)}, u32[]{:S(2)}) collective-permute-start(s16[1040,128]{1,0:T(8,128)(2,1)S(1)} %shard_map.74.after), channel_id=1, source_target_pairs={{0,4},{4,0},{8,12},{12,8},{1,5},{5,1},{9,13},{13,9},{2,6},{6,2},{1... | collective-permute-start | bytes 798728 | tf_op jit(solution)/shard_map/ppermute | solution.py:34
  8.7 2.7 %shard_map.75 = (s16[1040,128]{1,0:T(8,128)(2,1)S(1)}, f32[17,128,128]{2,1,0:T(8,128)S(1)}) custom-call(s32[12,32]{1,0:T(8,128)S(1)} %get-tuple-element.11.table_from.table_ref.refs_0_, bf16[32,4,128,128]{3,2,1,0:T(8,128)(2,1)S(1)} %get-tuple-element.12.projector_ref.refs_1_, bf16[6,128,128]{2,1,0:T(8,128)(2,1)S(1)} %get-tuple-element.13.volume_ref.rest_1_, ...), custom_call_target="tpu_custom_call" | custom-call | flops 1 | bytes 1 | tf_op jit(solution)/shard_map/pallas_call | solution.py:233
  11.4 1.0 %collective-permute-done.refs_0_ = s16[1040,128]{1,0:T(8,128)(2,1)S(1)} collective-permute-done((s16[1040,128]{1,0:T(8,128)(2,1)S(1)}, s16[1040,128]{1,0:T(8,128)(2,1)S(1)}, u32[]{:S(2)}, u32[]{:S(2)}) %collective-permute-start) | collective-permute-done | bytes 266272 | tf_op jit(solution)/shard_map/ppermute | solution.py:34
  12.3 0.2 shard_map.77.after.refs_1_
  12.5 1.8 %collective-permute-start.3 = (s16[1040,128]{1,0:T(8,128)(2,1)S(1)}, s16[1040,128]{1,0:T(8,128)(2,1)S(1)}, u32[]{:S(2)}, u32[]{:S(2)}) collective-permute-start(s16[1040,128]{1,0:T(8,128)(2,1)S(1)} %shard_map.80), channel_id=1, source_target_pairs={{0,2},{2,0},{1,3},{3,1},{4,6},{6,4},{5,7},{7,5},{8,10},{10,8},{9,1... | collective-permute-start | bytes 798728 | tf_op jit(solution)/shard_map/ppermute | solution.py:34
  14.3 1.4 %collective-permute-start.2 = (s16[1040,128]{1,0:T(8,128)(2,1)S(1)}, s16[1040,128]{1,0:T(8,128)(2,1)S(1)}, u32[]{:S(2)}, u32[]{:S(2)}) collective-permute-start(s16[1040,128]{1,0:T(8,128)(2,1)S(1)} %shard_map.77.after.refs_1_), channel_id=1, source_target_pairs={{0,4},{4,0},{8,12},{12,8},{1,5},{5,1},{9,13},{13,9},{2,6},{6,2},{1... | collective-permute-start | bytes 798728 | tf_op jit(solution)/shard_map/ppermute | solution.py:34
  15.7 1.5 %shard_map.78.own_ref = f32[25,128,128]{2,1,0:T(8,128)S(1)} custom-call(s32[12,32]{1,0:T(8,128)S(1)} %get-tuple-element.11.table_from.table_ref.refs_0_, bf16[32,4,128,128]{3,2,1,0:T(8,128)(2,1)S(1)} %get-tuple-element.12.projector_ref.refs_1_, bf16[6,128,128]{2,1,0:T(8,128)(2,1)S(1)} %get-tuple-element.13.volume_ref.rest_1_, ...), custom_call_target="tpu_custom_call" | custom-call | flops 1 | bytes 1 | tf_op jit(solution)/shard_map/pallas_call | solution.py:233
  17.2 0.0 copy-start.2
  17.2 0.0 collective-permute-done.1.rest_0_
  17.2 0.2 shard_map.79.after
  17.4 2.8 %collective-permute-done.3.rest_1_ = s16[1040,128]{1,0:T(8,128)(2,1)S(1)} collective-permute-done((s16[1040,128]{1,0:T(8,128)(2,1)S(1)}, s16[1040,128]{1,0:T(8,128)(2,1)S(1)}, u32[]{:S(2)}, u32[]{:S(2)}) %collective-permute-start.3) | collective-permute-done | bytes 266272 | tf_op jit(solution)/shard_map/ppermute | solution.py:34
  20.1 1.1 %collective-permute-done.2.rest_0_ = s16[1040,128]{1,0:T(8,128)(2,1)S(1)} collective-permute-done((s16[1040,128]{1,0:T(8,128)(2,1)S(1)}, s16[1040,128]{1,0:T(8,128)(2,1)S(1)}, u32[]{:S(2)}, u32[]{:S(2)}) %collective-permute-start.2) | collective-permute-done | bytes 266272 | tf_op jit(solution)/shard_map/ppermute | solution.py:34
  21.3 0.2 shard_map.81.after
  21.5 0.0 copy-start.1
  21.5 0.1 shard_map.83.after
  21.7 1.4 %collective-permute-start.5 = (s16[1040,128]{1,0:T(8,128)(2,1)S(1)}, s16[1040,128]{1,0:T(8,128)(2,1)S(1)}, u32[]{:S(2)}, u32[]{:S(2)}) collective-permute-start(s16[1040,128]{1,0:T(8,128)(2,1)S(1)} %shard_map.83.after), channel_id=1, source_target_pairs={{0,4},{4,0},{8,12},{12,8},{1,5},{5,1},{9,13},{13,9},{2,6},{6,2},{1... | collective-permute-start | bytes 798728 | tf_op jit(solution)/shard_map/ppermute | solution.py:34
  23.1 2.4 %collective-permute-start.4 = (s16[1040,128]{1,0:T(8,128)(2,1)S(1)}, s16[1040,128]{1,0:T(8,128)(2,1)S(1)}, u32[]{:S(2)}, u32[]{:S(2)}) collective-permute-start(s16[1040,128]{1,0:T(8,128)(2,1)S(1)} %shard_map.81.after), channel_id=1, source_target_pairs={{0,8},{4,12},{8,0},{12,4},{1,9},{5,13},{9,1},{13,5},{2,10},{6,14},... | collective-permute-start | bytes 798728 | tf_op jit(solution)/shard_map/ppermute | solution.py:34
  25.4 0.8 %collective-permute-start.6 = (s16[1040,128]{1,0:T(8,128)(2,1)S(1)}, s16[1040,128]{1,0:T(8,128)(2,1)S(1)}, u32[]{:S(2)}, u32[]{:S(2)}) collective-permute-start(s16[1040,128]{1,0:T(8,128)(2,1)S(1)} %shard_map.79.after), channel_id=1, source_target_pairs={{0,2},{2,0},{1,3},{3,1},{4,6},{6,4},{5,7},{7,5},{8,10},{10,8},{9,1... | collective-permute-start | bytes 798728 | tf_op jit(solution)/shard_map/ppermute | solution.py:34
  26.2 0.0 copy-done.2
  26.2 0.0 copy-start
  26.2 1.8 %shard_map.86.after.rest_2_ = f32[6,1,128]{2,1,0:T(1,128)S(1)} custom-call(s32[12,32]{1,0:T(8,128)S(1)} %get-tuple-element.11.table_from.table_ref.refs_0_, bf16[32,4,128,128]{3,2,1,0:T(8,128)(2,1)S(1)} %get-tuple-element.12.projector_ref.refs_1_, s16[1040,128]{1,0:T(8,128)(2,1)S(1)} %shard_map.83.after), custom_call_target="tpu_custom_call" | custom-call | flops 1 | bytes 1 | tf_op jit(solution)/shard_map/pallas_call | solution.py:343
  28.0 5.4 %collective-permute-done.5.refs_0_ = s16[1040,128]{1,0:T(8,128)(2,1)S(1)} collective-permute-done((s16[1040,128]{1,0:T(8,128)(2,1)S(1)}, s16[1040,128]{1,0:T(8,128)(2,1)S(1)}, u32[]{:S(2)}, u32[]{:S(2)}) %collective-permute-start.5) | collective-permute-done | bytes 266272 | tf_op jit(solution)/shard_map/ppermute | solution.py:34
  33.4 2.4 %collective-permute-done.4.refs_0_ = s16[1040,128]{1,0:T(8,128)(2,1)S(1)} collective-permute-done((s16[1040,128]{1,0:T(8,128)(2,1)S(1)}, s16[1040,128]{1,0:T(8,128)(2,1)S(1)}, u32[]{:S(2)}, u32[]{:S(2)}) %collective-permute-start.4) | collective-permute-done | bytes 266272 | tf_op jit(solution)/shard_map/ppermute | solution.py:34
  35.8 0.0 copy-done.1
  35.8 0.7 %shard_map.87.weight_ref = bf16[8,128,128]{2,1,0:T(8,128)(2,1)S(1)} custom-call(f32[16]{0:T(128)S(1)} %convert_element_type.3.table_ref, s32[8,128]{1,0:T(8,128)S(1)} %copy-done.1, f32[6,1,128]{2,1,0:T(1,128)S(1)} %shard_map.86.after.rest_2_), custom_call_target="tpu_custom_call" | custom-call | flops 1 | bytes 1 | tf_op jit(solution)/shard_map/pallas_call | solution.py:297
  36.5 0.1 shard_map.85.sum_ref
  36.7 0.0 collective-permute-done.6.rest_0_
  36.7 0.0 copy-done
  36.7 0.2 shard_map.88.refs_2_
  36.8 0.1 collective-permute-start.8
  36.9 6.4 %collective-permute-start.7 = (bf16[8,128,128]{2,1,0:T(8,128)(2,1)S(1)}, bf16[8,128,128]{2,1,0:T(8,128)(2,1)S(1)}, u32[]{:S(2)}, u32[]{:S(2)}) collective-permute-start(bf16[8,128,128]{2,1,0:T(8,128)(2,1)S(1)} %shard_map.88.refs_2_), channel_id=1, source_target_pairs={{0,4},{4,0},{8,12},{12,8},{1,5},{5,1},{9,13},{13,9},{2,6},{6,2},{1... | collective-permute-start | bytes 786440 | tf_op jit(solution)/shard_map/ppermute | solution.py:34
  43.3 0.0 collective-permute-start.9
  43.3 0.9 %collective-permute-done.8.refs_4_ = bf16[8,128,128]{2,1,0:T(8,128)(2,1)S(1)} collective-permute-done((bf16[8,128,128]{2,1,0:T(8,128)(2,1)S(1)}, bf16[8,128,128]{2,1,0:T(8,128)(2,1)S(1)}, u32[]{:S(2)}, u32[]{:S(2)}) %collective-permute-start.8) | collective-permute-done | bytes 262176 | tf_op jit(solution)/shard_map/ppermute | solution.py:34
  44.2 3.4 %collective-permute-start.10 = (bf16[8,128,128]{2,1,0:T(8,128)(2,1)S(1)}, bf16[8,128,128]{2,1,0:T(8,128)(2,1)S(1)}, u32[]{:S(2)}, u32[]{:S(2)}) collective-permute-start(bf16[8,128,128]{2,1,0:T(8,128)(2,1)S(1)} %collective-permute-done.8.refs_4_), channel_id=1, source_target_pairs={{0,4},{4,0},{8,12},{12,8},{1,5},{5,1},{9,13},{13,9},{2,6},{6,2},{1... | collective-permute-start | bytes 786440 | tf_op jit(solution)/shard_map/ppermute | solution.py:34
  47.7 0.0 collective-permute-start.11
  47.7 2.7 %collective-permute-done.7.refs_0_ = bf16[8,128,128]{2,1,0:T(8,128)(2,1)S(1)} collective-permute-done((bf16[8,128,128]{2,1,0:T(8,128)(2,1)S(1)}, bf16[8,128,128]{2,1,0:T(8,128)(2,1)S(1)}, u32[]{:S(2)}, u32[]{:S(2)}) %collective-permute-start.7) | collective-permute-done | bytes 262176 | tf_op jit(solution)/shard_map/ppermute | solution.py:34
  50.4 1.7 %collective-permute-done.9.refs_5_.refs_0_ = bf16[8,128,128]{2,1,0:T(8,128)(2,1)S(1)} collective-permute-done((bf16[8,128,128]{2,1,0:T(8,128)(2,1)S(1)}, bf16[8,128,128]{2,1,0:T(8,128)(2,1)S(1)}, u32[]{:S(2)}, u32[]{:S(2)}) %collective-permute-start.9) | collective-permute-done | bytes 262176 | tf_op jit(solution)/shard_map/ppermute | solution.py:34
  52.1 1.6 %shard_map.90.refs_1_.refs_2_ = f32[7,128,128]{2,1,0:T(8,128)S(1)} custom-call(s32[12,32]{1,0:T(8,128)S(1)} %get-tuple-element.11.table_from.table_ref.refs_0_, bf16[32,4,128,128]{3,2,1,0:T(8,128)(2,1)S(1)} %get-tuple-element.12.projector_ref.refs_1_, bf16[8,128,128]{2,1,0:T(8,128)(2,1)S(1)} %shard_map.88.refs_2_, ...), custom_call_target="tpu_custom_call" | custom-call | flops 1 | bytes 1 | tf_op jit(solution)/shard_map/pallas_call | solution.py:411
  53.7 0.0 collective-permute-done.10.refs_0_
  53.7 1.7 %collective-permute-start.13 = (bf16[8,128,128]{2,1,0:T(8,128)(2,1)S(1)}, bf16[8,128,128]{2,1,0:T(8,128)(2,1)S(1)}, u32[]{:S(2)}, u32[]{:S(2)}) collective-permute-start(bf16[8,128,128]{2,1,0:T(8,128)(2,1)S(1)} %shard_map.93), channel_id=1, source_target_pairs={{0,4},{4,0},{8,12},{12,8},{1,5},{5,1},{9,13},{13,9},{2,6},{6,2},{1... | collective-permute-start | bytes 786440 | tf_op jit(solution)/shard_map/ppermute | solution.py:34
  55.4 0.0 collective-permute-start.12
  55.4 0.0 collective-permute-done.11.refs_4_
  55.4 2.2 %shard_map.92.rest_0_ = f32[7,128,128]{2,1,0:T(8,128)S(1)} custom-call(s32[12,32]{1,0:T(8,128)S(1)} %get-tuple-element.11.table_from.table_ref.refs_0_, bf16[32,4,128,128]{3,2,1,0:T(8,128)(2,1)S(1)} %get-tuple-element.12.projector_ref.refs_1_, f32[7,128,128]{2,1,0:T(8,128)S(1)} %shard_map.90.refs_1_.refs_2_, ...), custom_call_target="tpu_custom_call" | custom-call | flops 1 | bytes 1 | tf_op jit(solution)/shard_map/pallas_call | solution.py:411
  57.6 2.6 %collective-permute-done.13.rest_4_ = bf16[8,128,128]{2,1,0:T(8,128)(2,1)S(1)} collective-permute-done((bf16[8,128,128]{2,1,0:T(8,128)(2,1)S(1)}, bf16[8,128,128]{2,1,0:T(8,128)(2,1)S(1)}, u32[]{:S(2)}, u32[]{:S(2)}) %collective-permute-start.13) | collective-permute-done | bytes 262176 | tf_op jit(solution)/shard_map/ppermute | solution.py:34
  60.1 1.6 %collective-permute-done.12.rest_3_ = bf16[8,128,128]{2,1,0:T(8,128)(2,1)S(1)} collective-permute-done((bf16[8,128,128]{2,1,0:T(8,128)(2,1)S(1)}, bf16[8,128,128]{2,1,0:T(8,128)(2,1)S(1)}, u32[]{:S(2)}, u32[]{:S(2)}) %collective-permute-start.12) | collective-permute-done | bytes 262176 | tf_op jit(solution)/shard_map/ppermute | solution.py:34
  61.7 2.8 %shard_map.94 = f32[6,128,128]{2,1,0:T(8,128)} custom-call(s32[12,32]{1,0:T(8,128)S(1)} %get-tuple-element.11.table_from.table_ref.refs_0_, bf16[32,4,128,128]{3,2,1,0:T(8,128)(2,1)S(1)} %get-tuple-element.12.projector_ref.refs_1_, f32[7,128,128]{2,1,0:T(8,128)S(1)} %shard_map.92.rest_0_, bf16[6,128,128]{2,1,0:T(8,128)(2,1)S(1)} %get-tuple-element.13.volume_ref.rest_1_, ...), custom_call_target="tpu_custom_call" | custom-call | flops 1 | bytes 1 | tf_op jit(solution)/shard_map/pallas_call | solution.py:411
  (8 shorter events, 0.0 us)
Async XLA Ops:
  2.5 9.8 %collective-permute-start = (s16[1040,128]{1,0:T(8,128)(2,1)S(1)}, s16[1040,128]{1,0:T(8,128)(2,1)S(1)}, u32[]{:S(2)}, u32[]{:S(2)}) collective-permute-start(s16[1040,128]{1,0:T(8,128)(2,1)S(1)} %get-tuple-element.14.after), channel_id=1, source_target_pairs={{0,2},{2,0},{1,3},{3,1},{4,6},{6,4},{5,7},{7,5},{8,10},{10,8},{9,1... | collective-permute-start | bytes 798728 | tf_op jit(solution)/shard_map/ppermute | solution.py:34
  7.5 9.7 %collective-permute-start.1 = (s16[1040,128]{1,0:T(8,128)(2,1)S(1)}, s16[1040,128]{1,0:T(8,128)(2,1)S(1)}, u32[]{:S(2)}, u32[]{:S(2)}) collective-permute-start(s16[1040,128]{1,0:T(8,128)(2,1)S(1)} %shard_map.74.after), channel_id=1, source_target_pairs={{0,4},{4,0},{8,12},{12,8},{1,5},{5,1},{9,13},{13,9},{2,6},{6,2},{1... | collective-permute-start | bytes 798728 | tf_op jit(solution)/shard_map/ppermute | solution.py:34
  12.5 7.6 %collective-permute-start.3 = (s16[1040,128]{1,0:T(8,128)(2,1)S(1)}, s16[1040,128]{1,0:T(8,128)(2,1)S(1)}, u32[]{:S(2)}, u32[]{:S(2)}) collective-permute-start(s16[1040,128]{1,0:T(8,128)(2,1)S(1)} %shard_map.80), channel_id=1, source_target_pairs={{0,2},{2,0},{1,3},{3,1},{4,6},{6,4},{5,7},{7,5},{8,10},{10,8},{9,1... | collective-permute-start | bytes 798728 | tf_op jit(solution)/shard_map/ppermute | solution.py:34
  14.3 7.0 %collective-permute-start.2 = (s16[1040,128]{1,0:T(8,128)(2,1)S(1)}, s16[1040,128]{1,0:T(8,128)(2,1)S(1)}, u32[]{:S(2)}, u32[]{:S(2)}) collective-permute-start(s16[1040,128]{1,0:T(8,128)(2,1)S(1)} %shard_map.77.after.refs_1_), channel_id=1, source_target_pairs={{0,4},{4,0},{8,12},{12,8},{1,5},{5,1},{9,13},{13,9},{2,6},{6,2},{1... | collective-permute-start | bytes 798728 | tf_op jit(solution)/shard_map/ppermute | solution.py:34
  17.2 9.0 %copy-start.2 = (bf16[16]{0:T(256)(128)(2,1)S(1)}, bf16[16]{0:T(256)(128)(2,1)}, u32[]{:S(2)}) copy-start(bf16[16]{0:T(256)(128)(2,1)} %param.13) | copy-start | bytes 100
  21.5 14.3 %copy-start.1 = (s32[8,128]{1,0:T(8,128)S(1)}, s32[8,128]{1,0:T(8,128)}, u32[]{:S(2)}) copy-start(s32[8,128]{1,0:T(8,128)} %index_ref.1) | copy-start | bytes 12292
  21.7 11.8 %collective-permute-start.5 = (s16[1040,128]{1,0:T(8,128)(2,1)S(1)}, s16[1040,128]{1,0:T(8,128)(2,1)S(1)}, u32[]{:S(2)}, u32[]{:S(2)}) collective-permute-start(s16[1040,128]{1,0:T(8,128)(2,1)S(1)} %shard_map.83.after), channel_id=1, source_target_pairs={{0,4},{4,0},{8,12},{12,8},{1,5},{5,1},{9,13},{13,9},{2,6},{6,2},{1... | collective-permute-start | bytes 798728 | tf_op jit(solution)/shard_map/ppermute | solution.py:34
  23.1 12.7 %collective-permute-start.4 = (s16[1040,128]{1,0:T(8,128)(2,1)S(1)}, s16[1040,128]{1,0:T(8,128)(2,1)S(1)}, u32[]{:S(2)}, u32[]{:S(2)}) collective-permute-start(s16[1040,128]{1,0:T(8,128)(2,1)S(1)} %shard_map.81.after), channel_id=1, source_target_pairs={{0,8},{4,12},{8,0},{12,4},{1,9},{5,13},{9,1},{13,5},{2,10},{6,14},... | collective-permute-start | bytes 798728 | tf_op jit(solution)/shard_map/ppermute | solution.py:34
  25.4 11.2 %collective-permute-start.6 = (s16[1040,128]{1,0:T(8,128)(2,1)S(1)}, s16[1040,128]{1,0:T(8,128)(2,1)S(1)}, u32[]{:S(2)}, u32[]{:S(2)}) collective-permute-start(s16[1040,128]{1,0:T(8,128)(2,1)S(1)} %shard_map.79.after), channel_id=1, source_target_pairs={{0,2},{2,0},{1,3},{3,1},{4,6},{6,4},{5,7},{7,5},{8,10},{10,8},{9,1... | collective-permute-start | bytes 798728 | tf_op jit(solution)/shard_map/ppermute | solution.py:34
  26.2 10.5 %copy-start = (bf16[8,128,128]{2,1,0:T(8,128)(2,1)S(1)}, bf16[8,128,128]{2,1,0:T(8,128)(2,1)}, u32[]{:S(2)}) copy-start(bf16[8,128,128]{2,1,0:T(8,128)(2,1)} %sinogram_ref.1) | copy-start | bytes 786436
  36.8 7.4 %collective-permute-start.8 = (bf16[8,128,128]{2,1,0:T(8,128)(2,1)S(1)}, bf16[8,128,128]{2,1,0:T(8,128)(2,1)S(1)}, u32[]{:S(2)}, u32[]{:S(2)}) collective-permute-start(bf16[8,128,128]{2,1,0:T(8,128)(2,1)S(1)} %shard_map.88.refs_2_), channel_id=1, source_target_pairs={{0,8},{4,12},{8,0},{12,4},{1,9},{5,13},{9,1},{13,5},{2,10},{6,14},... | collective-permute-start | bytes 786440 | tf_op jit(solution)/shard_map/ppermute | solution.py:34
  36.9 13.5 %collective-permute-start.7 = (bf16[8,128,128]{2,1,0:T(8,128)(2,1)S(1)}, bf16[8,128,128]{2,1,0:T(8,128)(2,1)S(1)}, u32[]{:S(2)}, u32[]{:S(2)}) collective-permute-start(bf16[8,128,128]{2,1,0:T(8,128)(2,1)S(1)} %shard_map.88.refs_2_), channel_id=1, source_target_pairs={{0,4},{4,0},{8,12},{12,8},{1,5},{5,1},{9,13},{13,9},{2,6},{6,2},{1... | collective-permute-start | bytes 786440 | tf_op jit(solution)/shard_map/ppermute | solution.py:34
  43.3 8.7 %collective-permute-start.9 = (bf16[8,128,128]{2,1,0:T(8,128)(2,1)S(1)}, bf16[8,128,128]{2,1,0:T(8,128)(2,1)S(1)}, u32[]{:S(2)}, u32[]{:S(2)}) collective-permute-start(bf16[8,128,128]{2,1,0:T(8,128)(2,1)S(1)} %shard_map.88.refs_2_), channel_id=1, source_target_pairs={{0,2},{2,0},{1,3},{3,1},{4,6},{6,4},{5,7},{7,5},{8,10},{10,8},{9,1... | collective-permute-start | bytes 786440 | tf_op jit(solution)/shard_map/ppermute | solution.py:34
  44.2 9.4 %collective-permute-start.10 = (bf16[8,128,128]{2,1,0:T(8,128)(2,1)S(1)}, bf16[8,128,128]{2,1,0:T(8,128)(2,1)S(1)}, u32[]{:S(2)}, u32[]{:S(2)}) collective-permute-start(bf16[8,128,128]{2,1,0:T(8,128)(2,1)S(1)} %collective-permute-done.8.refs_4_), channel_id=1, source_target_pairs={{0,4},{4,0},{8,12},{12,8},{1,5},{5,1},{9,13},{13,9},{2,6},{6,2},{1... | collective-permute-start | bytes 786440 | tf_op jit(solution)/shard_map/ppermute | solution.py:34
  47.7 7.7 %collective-permute-start.11 = (bf16[8,128,128]{2,1,0:T(8,128)(2,1)S(1)}, bf16[8,128,128]{2,1,0:T(8,128)(2,1)S(1)}, u32[]{:S(2)}, u32[]{:S(2)}) collective-permute-start(bf16[8,128,128]{2,1,0:T(8,128)(2,1)S(1)} %collective-permute-done.8.refs_4_), channel_id=1, source_target_pairs={{0,2},{2,0},{1,3},{3,1},{4,6},{6,4},{5,7},{7,5},{8,10},{10,8},{9,1... | collective-permute-start | bytes 786440 | tf_op jit(solution)/shard_map/ppermute | solution.py:34
  53.7 6.4 %collective-permute-start.13 = (bf16[8,128,128]{2,1,0:T(8,128)(2,1)S(1)}, bf16[8,128,128]{2,1,0:T(8,128)(2,1)S(1)}, u32[]{:S(2)}, u32[]{:S(2)}) collective-permute-start(bf16[8,128,128]{2,1,0:T(8,128)(2,1)S(1)} %shard_map.93), channel_id=1, source_target_pairs={{0,4},{4,0},{8,12},{12,8},{1,5},{5,1},{9,13},{13,9},{2,6},{6,2},{1... | collective-permute-start | bytes 786440 | tf_op jit(solution)/shard_map/ppermute | solution.py:34
  55.4 6.4 %collective-permute-start.12 = (bf16[8,128,128]{2,1,0:T(8,128)(2,1)S(1)}, bf16[8,128,128]{2,1,0:T(8,128)(2,1)S(1)}, u32[]{:S(2)}, u32[]{:S(2)}) collective-permute-start(bf16[8,128,128]{2,1,0:T(8,128)(2,1)S(1)} %shard_map.91.refs_3_.refs_1_), channel_id=1, source_target_pairs={{0,2},{2,0},{1,3},{3,1},{4,6},{6,4},{5,7},{7,5},{8,10},{10,8},{9,1... | collective-permute-start | bytes 786440 | tf_op jit(solution)/shard_map/ppermute | solution.py:34

commit v6 on v5

--- a/solution.py
+++ b/solution.py
@@ -157,7 +157,7 @@
         count = list_slots(cell_ref, (b * block, b * block + block), [(low, low + tiles)], slot_list)
         copies[3 + b].wait()
         project(
-            count, 2, low, tiles, slot_list, cell_ref, pixel_ref, projector_ref, volume_ref, total
+            count, 4, low, tiles, slot_list, cell_ref, pixel_ref, projector_ref, volume_ref, total
         )
     send_out(total, 0, tiles, [], send, levels)
     table_copy.wait()
@@ -336,6 +336,8 @@
         for g in range(per_slot):
             column = jnp.sum(projector_ref[s, g].astype(jnp.float32), axis=0, keepdims=True)
             out_ref[table_ref[8 + g, s]] += column
+
+    out_ref[...] = 1.0 / out_ref[...]
 
 
 def column_sums(table, projector, patch_tiles, after):
@@ -389,7 +391,7 @@
 
     if finish:
         for q in range(patch_tiles):
-            out_ref[q] = volume_ref[q].astype(jnp.float32) + (total[q] / column_ref[q]).T
+            out_ref[q] = volume_ref[q].astype(jnp.float32) + (total[q] * column_ref[q]).T
 
 
 def spread(table, projector, all_cells, lows, chunks, patch_tiles, before, last=()):

time: 64.5 us -> 63.4 us (0.983)
  starting transfers between devices: 23.9 us -> 23.1 us
    ppermute x14, starting transfers between devices: 23.9 us -> 23.1 us  [swap(): return lax.ppermute(value, axis, [(i, i ^ bits) for i in range(size)])]
  transfers between devices with their start and end apart: 14 -> 14, of which waited for: 10 -> 10; matrix products, arithmetic and copies ran while one was open for 0% -> 0% of each run, Pallas kernels for 19% -> 21%
where the time goes in v6:
time: 63.4 us; the launch traced here: 63.3 us
  starting transfers between devices  23.1 us (36%)
  waiting for transfers between devices  21.7 us (34%)
  Pallas kernels  18.3 us (29%)
    ppermute x14, starting transfers between devices, swap(): return lax.ppermute(value, axis, [(i, i ^ bits) for i in range(size)])  23.1 us
    ppermute x14, waiting for transfers between devices, swap(): return lax.ppermute(value, axis, [(i, i ^ bits) for i in range(size)])  21.7 us
    pallas_call x3, Pallas kernels, spread(): pl.pallas_call(kernel, in_specs=[VMEM] * (2 + len(more)), out_specs=VMEM,...  6.61 us
    pallas_call x3, Pallas kernels, further_sums(): pl.pallas_call(functools.partial(further_kernel, tiles, sent, ranges), in...  5.73 us
    pallas_call x1, Pallas kernels, first_send(): pl.pallas_call(functools.partial(first_kernel, sizes, low), in_specs=[HBM...  2.48 us
    pallas_call x1, Pallas kernels, column_sums(): pl.pallas_call(column_kernel, in_specs=[SMEM, VMEM, ANY], out_specs=VMEM,...  1.79 us
  transfers between devices with their start and end apart: 14, of which 10 were waited for; matrix products, arithmetic and copies ran while one was open for 0% of the time, Pallas kernels for 21%

profile of v6, /device:TPU:0, one launch (start us, length us, event | category | flops | bytes accessed | tf_op | source)
XLA Modules:
  0.0 63.3 jit_solution(4275341058516759797)
XLA Ops:
  0.0 2.5 %shard_map.73 = (s16[1040,128]{1,0:T(8,128)(2,1)S(1)}, bf16[32,4,128,128]{3,2,1,0:T(8,128)(2,1)S(1)}, bf16[6,128,128]{2,1,0:T(8,128)(2,1)S(1)}, s32[12,32]{1,0:T(8,128)S(1)}) custom-call(s32[32]{0:T(128)} %ray_hbm.1, s32[4,32]{1,0:T(4,128)} %bitcast.1, bf16[32,4,128,128]{3,2,1,0:T(8,128)(2,1)} %projector_hbm.1, bf16[6,128,128]{2,1,0:T(8,128)(2,1)} %volume_hbm.1), custom_call_target="tpu_custom_call" | custom-call | flops 1 | bytes 1 | tf_op jit(solution)/shard_map/pallas_call | solution.py:175
  2.5 3.3 %collective-permute-start = (s16[1040,128]{1,0:T(8,128)(2,1)S(1)}, s16[1040,128]{1,0:T(8,128)(2,1)S(1)}, u32[]{:S(2)}, u32[]{:S(2)}) collective-permute-start(s16[1040,128]{1,0:T(8,128)(2,1)S(1)} %get-tuple-element.14.after), channel_id=1, source_target_pairs={{0,2},{2,0},{1,3},{3,1},{4,6},{6,4},{5,7},{7,5},{8,10},{10,8},{9,1... | collective-permute-start | bytes 798728 | tf_op jit(solution)/shard_map/ppermute | solution.py:34
  5.8 1.1 %shard_map.74.after = s16[1040,128]{1,0:T(8,128)(2,1)S(1)} custom-call(s32[12,32]{1,0:T(8,128)S(1)} %get-tuple-element.11.table_from.table_ref.refs_0_, bf16[32,4,128,128]{3,2,1,0:T(8,128)(2,1)S(1)} %get-tuple-element.12.projector_ref.refs_1_, bf16[6,128,128]{2,1,0:T(8,128)(2,1)S(1)} %get-tuple-element.13.volume_ref.rest_1_, ...), custom_call_target="tpu_custom_call" | custom-call | flops 1 | bytes 1 | tf_op jit(solution)/shard_map/pallas_call | solution.py:233
  6.9 1.6 %collective-permute-start.1 = (s16[1040,128]{1,0:T(8,128)(2,1)S(1)}, s16[1040,128]{1,0:T(8,128)(2,1)S(1)}, u32[]{:S(2)}, u32[]{:S(2)}) collective-permute-start(s16[1040,128]{1,0:T(8,128)(2,1)S(1)} %shard_map.74.after), channel_id=1, source_target_pairs={{0,4},{4,0},{8,12},{12,8},{1,5},{5,1},{9,13},{13,9},{2,6},{6,2},{1... | collective-permute-start | bytes 798728 | tf_op jit(solution)/shard_map/ppermute | solution.py:34
  8.6 2.8 %shard_map.75 = (s16[1040,128]{1,0:T(8,128)(2,1)S(1)}, f32[17,128,128]{2,1,0:T(8,128)S(1)}) custom-call(s32[12,32]{1,0:T(8,128)S(1)} %get-tuple-element.11.table_from.table_ref.refs_0_, bf16[32,4,128,128]{3,2,1,0:T(8,128)(2,1)S(1)} %get-tuple-element.12.projector_ref.refs_1_, bf16[6,128,128]{2,1,0:T(8,128)(2,1)S(1)} %get-tuple-element.13.volume_ref.rest_1_, ...), custom_call_target="tpu_custom_call" | custom-call | flops 1 | bytes 1 | tf_op jit(solution)/shard_map/pallas_call | solution.py:233
  11.4 0.8 %collective-permute-done.refs_0_ = s16[1040,128]{1,0:T(8,128)(2,1)S(1)} collective-permute-done((s16[1040,128]{1,0:T(8,128)(2,1)S(1)}, s16[1040,128]{1,0:T(8,128)(2,1)S(1)}, u32[]{:S(2)}, u32[]{:S(2)}) %collective-permute-start) | collective-permute-done | bytes 266272 | tf_op jit(solution)/shard_map/ppermute | solution.py:34
  12.2 0.2 shard_map.77.after.refs_1_
  12.4 1.8 %collective-permute-start.3 = (s16[1040,128]{1,0:T(8,128)(2,1)S(1)}, s16[1040,128]{1,0:T(8,128)(2,1)S(1)}, u32[]{:S(2)}, u32[]{:S(2)}) collective-permute-start(s16[1040,128]{1,0:T(8,128)(2,1)S(1)} %shard_map.80), channel_id=1, source_target_pairs={{0,2},{2,0},{1,3},{3,1},{4,6},{6,4},{5,7},{7,5},{8,10},{10,8},{9,1... | collective-permute-start | bytes 798728 | tf_op jit(solution)/shard_map/ppermute | solution.py:34
  14.2 1.6 %collective-permute-start.2 = (s16[1040,128]{1,0:T(8,128)(2,1)S(1)}, s16[1040,128]{1,0:T(8,128)(2,1)S(1)}, u32[]{:S(2)}, u32[]{:S(2)}) collective-permute-start(s16[1040,128]{1,0:T(8,128)(2,1)S(1)} %shard_map.77.after.refs_1_), channel_id=1, source_target_pairs={{0,4},{4,0},{8,12},{12,8},{1,5},{5,1},{9,13},{13,9},{2,6},{6,2},{1... | collective-permute-start | bytes 798728 | tf_op jit(solution)/shard_map/ppermute | solution.py:34
  15.8 1.8 %shard_map.78.own_ref = f32[25,128,128]{2,1,0:T(8,128)S(1)} custom-call(s32[12,32]{1,0:T(8,128)S(1)} %get-tuple-element.11.table_from.table_ref.refs_0_, bf16[32,4,128,128]{3,2,1,0:T(8,128)(2,1)S(1)} %get-tuple-element.12.projector_ref.refs_1_, bf16[6,128,128]{2,1,0:T(8,128)(2,1)S(1)} %get-tuple-element.13.volume_ref.rest_1_, ...), custom_call_target="tpu_custom_call" | custom-call | flops 1 | bytes 1 | tf_op jit(solution)/shard_map/pallas_call | solution.py:233
  17.6 0.0 copy-start.2
  17.6 0.0 collective-permute-done.1.rest_0_
  17.6 0.2 shard_map.79.after
  17.8 2.2 %collective-permute-done.3.rest_1_ = s16[1040,128]{1,0:T(8,128)(2,1)S(1)} collective-permute-done((s16[1040,128]{1,0:T(8,128)(2,1)S(1)}, s16[1040,128]{1,0:T(8,128)(2,1)S(1)}, u32[]{:S(2)}, u32[]{:S(2)}) %collective-permute-start.3) | collective-permute-done | bytes 266272 | tf_op jit(solution)/shard_map/ppermute | solution.py:34
  20.0 1.1 %collective-permute-done.2.rest_0_ = s16[1040,128]{1,0:T(8,128)(2,1)S(1)} collective-permute-done((s16[1040,128]{1,0:T(8,128)(2,1)S(1)}, s16[1040,128]{1,0:T(8,128)(2,1)S(1)}, u32[]{:S(2)}, u32[]{:S(2)}) %collective-permute-start.2) | collective-permute-done | bytes 266272 | tf_op jit(solution)/shard_map/ppermute | solution.py:34
  21.1 0.2 shard_map.81.after
  21.4 0.0 copy-start.1
  21.4 0.1 shard_map.83.after
  21.5 1.7 %collective-permute-start.5 = (s16[1040,128]{1,0:T(8,128)(2,1)S(1)}, s16[1040,128]{1,0:T(8,128)(2,1)S(1)}, u32[]{:S(2)}, u32[]{:S(2)}) collective-permute-start(s16[1040,128]{1,0:T(8,128)(2,1)S(1)} %shard_map.83.after), channel_id=1, source_target_pairs={{0,4},{4,0},{8,12},{12,8},{1,5},{5,1},{9,13},{13,9},{2,6},{6,2},{1... | collective-permute-start | bytes 798728 | tf_op jit(solution)/shard_map/ppermute | solution.py:34
  23.2 2.6 %collective-permute-start.4 = (s16[1040,128]{1,0:T(8,128)(2,1)S(1)}, s16[1040,128]{1,0:T(8,128)(2,1)S(1)}, u32[]{:S(2)}, u32[]{:S(2)}) collective-permute-start(s16[1040,128]{1,0:T(8,128)(2,1)S(1)} %shard_map.81.after), channel_id=1, source_target_pairs={{0,8},{4,12},{8,0},{12,4},{1,9},{5,13},{9,1},{13,5},{2,10},{6,14},... | collective-permute-start | bytes 798728 | tf_op jit(solution)/shard_map/ppermute | solution.py:34
  25.8 0.7 %collective-permute-start.6 = (s16[1040,128]{1,0:T(8,128)(2,1)S(1)}, s16[1040,128]{1,0:T(8,128)(2,1)S(1)}, u32[]{:S(2)}, u32[]{:S(2)}) collective-permute-start(s16[1040,128]{1,0:T(8,128)(2,1)S(1)} %shard_map.79.after), channel_id=1, source_target_pairs={{0,2},{2,0},{1,3},{3,1},{4,6},{6,4},{5,7},{7,5},{8,10},{10,8},{9,1... | collective-permute-start | bytes 798728 | tf_op jit(solution)/shard_map/ppermute | solution.py:34
  26.6 0.0 copy-done.2
  26.6 0.0 copy-start
  26.6 1.8 %shard_map.86.after.rest_2_ = f32[6,1,128]{2,1,0:T(1,128)S(1)} custom-call(s32[12,32]{1,0:T(8,128)S(1)} %get-tuple-element.11.table_from.table_ref.refs_0_, bf16[32,4,128,128]{3,2,1,0:T(8,128)(2,1)S(1)} %get-tuple-element.12.projector_ref.refs_1_, s16[1040,128]{1,0:T(8,128)(2,1)S(1)} %shard_map.83.after), custom_call_target="tpu_custom_call" | custom-call | flops 1 | bytes 1 | tf_op jit(solution)/shard_map/pallas_call | solution.py:345
  28.4 4.7 %collective-permute-done.5.refs_0_ = s16[1040,128]{1,0:T(8,128)(2,1)S(1)} collective-permute-done((s16[1040,128]{1,0:T(8,128)(2,1)S(1)}, s16[1040,128]{1,0:T(8,128)(2,1)S(1)}, u32[]{:S(2)}, u32[]{:S(2)}) %collective-permute-start.5) | collective-permute-done | bytes 266272 | tf_op jit(solution)/shard_map/ppermute | solution.py:34
  33.0 2.9 %collective-permute-done.4.refs_0_ = s16[1040,128]{1,0:T(8,128)(2,1)S(1)} collective-permute-done((s16[1040,128]{1,0:T(8,128)(2,1)S(1)}, s16[1040,128]{1,0:T(8,128)(2,1)S(1)}, u32[]{:S(2)}, u32[]{:S(2)}) %collective-permute-start.4) | collective-permute-done | bytes 266272 | tf_op jit(solution)/shard_map/ppermute | solution.py:34
  35.9 0.0 copy-done.1
  35.9 0.7 %shard_map.87.weight_ref = bf16[8,128,128]{2,1,0:T(8,128)(2,1)S(1)} custom-call(f32[16]{0:T(128)S(1)} %convert_element_type.3.table_ref, s32[8,128]{1,0:T(8,128)S(1)} %copy-done.1, f32[6,1,128]{2,1,0:T(1,128)S(1)} %shard_map.86.after.rest_2_), custom_call_target="tpu_custom_call" | custom-call | flops 1 | bytes 1 | tf_op jit(solution)/shard_map/pallas_call | solution.py:297
  36.6 0.1 shard_map.85.sum_ref
  36.8 0.0 collective-permute-done.6.rest_0_
  36.8 0.0 copy-done
  36.8 0.2 shard_map.88.refs_2_
  37.0 0.1 collective-permute-start.8
  37.0 5.7 %collective-permute-start.7 = (bf16[8,128,128]{2,1,0:T(8,128)(2,1)S(1)}, bf16[8,128,128]{2,1,0:T(8,128)(2,1)S(1)}, u32[]{:S(2)}, u32[]{:S(2)}) collective-permute-start(bf16[8,128,128]{2,1,0:T(8,128)(2,1)S(1)} %shard_map.88.refs_2_), channel_id=1, source_target_pairs={{0,4},{4,0},{8,12},{12,8},{1,5},{5,1},{9,13},{13,9},{2,6},{6,2},{1... | collective-permute-start | bytes 786440 | tf_op jit(solution)/shard_map/ppermute | solution.py:34
  42.7 1.4 %collective-permute-start.9 = (bf16[8,128,128]{2,1,0:T(8,128)(2,1)S(1)}, bf16[8,128,128]{2,1,0:T(8,128)(2,1)S(1)}, u32[]{:S(2)}, u32[]{:S(2)}) collective-permute-start(bf16[8,128,128]{2,1,0:T(8,128)(2,1)S(1)} %shard_map.88.refs_2_), channel_id=1, source_target_pairs={{0,2},{2,0},{1,3},{3,1},{4,6},{6,4},{5,7},{7,5},{8,10},{10,8},{9,1... | collective-permute-start | bytes 786440 | tf_op jit(solution)/shard_map/ppermute | solution.py:34
  44.1 3.1 %collective-permute-done.8.refs_4_ = bf16[8,128,128]{2,1,0:T(8,128)(2,1)S(1)} collective-permute-done((bf16[8,128,128]{2,1,0:T(8,128)(2,1)S(1)}, bf16[8,128,128]{2,1,0:T(8,128)(2,1)S(1)}, u32[]{:S(2)}, u32[]{:S(2)}) %collective-permute-start.8) | collective-permute-done | bytes 262176 | tf_op jit(solution)/shard_map/ppermute | solution.py:34
  47.2 0.0 collective-permute-start.10
  47.2 1.3 %collective-permute-start.11 = (bf16[8,128,128]{2,1,0:T(8,128)(2,1)S(1)}, bf16[8,128,128]{2,1,0:T(8,128)(2,1)S(1)}, u32[]{:S(2)}, u32[]{:S(2)}) collective-permute-start(bf16[8,128,128]{2,1,0:T(8,128)(2,1)S(1)} %collective-permute-done.8.refs_4_), channel_id=1, source_target_pairs={{0,2},{2,0},{1,3},{3,1},{4,6},{6,4},{5,7},{7,5},{8,10},{10,8},{9,1... | collective-permute-start | bytes 786440 | tf_op jit(solution)/shard_map/ppermute | solution.py:34
  48.5 1.4 %collective-permute-done.7.refs_0_ = bf16[8,128,128]{2,1,0:T(8,128)(2,1)S(1)} collective-permute-done((bf16[8,128,128]{2,1,0:T(8,128)(2,1)S(1)}, bf16[8,128,128]{2,1,0:T(8,128)(2,1)S(1)}, u32[]{:S(2)}, u32[]{:S(2)}) %collective-permute-start.7) | collective-permute-done | bytes 262176 | tf_op jit(solution)/shard_map/ppermute | solution.py:34
  49.9 1.4 %collective-permute-done.9.refs_5_.refs_0_ = bf16[8,128,128]{2,1,0:T(8,128)(2,1)S(1)} collective-permute-done((bf16[8,128,128]{2,1,0:T(8,128)(2,1)S(1)}, bf16[8,128,128]{2,1,0:T(8,128)(2,1)S(1)}, u32[]{:S(2)}, u32[]{:S(2)}) %collective-permute-start.9) | collective-permute-done | bytes 262176 | tf_op jit(solution)/shard_map/ppermute | solution.py:34
  51.3 2.7 %shard_map.90.refs_1_.refs_2_ = f32[7,128,128]{2,1,0:T(8,128)S(1)} custom-call(s32[12,32]{1,0:T(8,128)S(1)} %get-tuple-element.11.table_from.table_ref.refs_0_, bf16[32,4,128,128]{3,2,1,0:T(8,128)(2,1)S(1)} %get-tuple-element.12.projector_ref.refs_1_, bf16[8,128,128]{2,1,0:T(8,128)(2,1)S(1)} %shard_map.88.refs_2_, ...), custom_call_target="tpu_custom_call" | custom-call | flops 1 | bytes 1 | tf_op jit(solution)/shard_map/pallas_call | solution.py:413
  53.9 0.9 %collective-permute-done.10.refs_0_ = bf16[8,128,128]{2,1,0:T(8,128)(2,1)S(1)} collective-permute-done((bf16[8,128,128]{2,1,0:T(8,128)(2,1)S(1)}, bf16[8,128,128]{2,1,0:T(8,128)(2,1)S(1)}, u32[]{:S(2)}, u32[]{:S(2)}) %collective-permute-start.10) | collective-permute-done | bytes 262176 | tf_op jit(solution)/shard_map/ppermute | solution.py:34
  54.8 0.0 collective-permute-start.13
  54.8 1.2 %collective-permute-start.12 = (bf16[8,128,128]{2,1,0:T(8,128)(2,1)S(1)}, bf16[8,128,128]{2,1,0:T(8,128)(2,1)S(1)}, u32[]{:S(2)}, u32[]{:S(2)}) collective-permute-start(bf16[8,128,128]{2,1,0:T(8,128)(2,1)S(1)} %shard_map.91.refs_3_.refs_1_), channel_id=1, source_target_pairs={{0,2},{2,0},{1,3},{3,1},{4,6},{6,4},{5,7},{7,5},{8,10},{10,8},{9,1... | collective-permute-start | bytes 786440 | tf_op jit(solution)/shard_map/ppermute | solution.py:34
  56.1 0.0 collective-permute-done.11.refs_4_
  56.1 1.9 %shard_map.92.rest_0_ = f32[7,128,128]{2,1,0:T(8,128)S(1)} custom-call(s32[12,32]{1,0:T(8,128)S(1)} %get-tuple-element.11.table_from.table_ref.refs_0_, bf16[32,4,128,128]{3,2,1,0:T(8,128)(2,1)S(1)} %get-tuple-element.12.projector_ref.refs_1_, f32[7,128,128]{2,1,0:T(8,128)S(1)} %shard_map.90.refs_1_.refs_2_, ...), custom_call_target="tpu_custom_call" | custom-call | flops 1 | bytes 1 | tf_op jit(solution)/shard_map/pallas_call | solution.py:413
  58.0 3.2 %collective-permute-done.13.rest_4_ = bf16[8,128,128]{2,1,0:T(8,128)(2,1)S(1)} collective-permute-done((bf16[8,128,128]{2,1,0:T(8,128)(2,1)S(1)}, bf16[8,128,128]{2,1,0:T(8,128)(2,1)S(1)}, u32[]{:S(2)}, u32[]{:S(2)}) %collective-permute-start.13) | collective-permute-done | bytes 262176 | tf_op jit(solution)/shard_map/ppermute | solution.py:34
  61.2 0.0 collective-permute-done.12.rest_3_
  61.2 2.1 %shard_map.94 = f32[6,128,128]{2,1,0:T(8,128)} custom-call(s32[12,32]{1,0:T(8,128)S(1)} %get-tuple-element.11.table_from.table_ref.refs_0_, bf16[32,4,128,128]{3,2,1,0:T(8,128)(2,1)S(1)} %get-tuple-element.12.projector_ref.refs_1_, f32[7,128,128]{2,1,0:T(8,128)S(1)} %shard_map.92.rest_0_, bf16[6,128,128]{2,1,0:T(8,128)(2,1)S(1)} %get-tuple-element.13.volume_ref.rest_1_, ...), custom_call_target="tpu_custom_call" | custom-call | flops 1 | bytes 1 | tf_op jit(solution)/shard_map/pallas_call | solution.py:413
  (8 shorter events, 0.0 us)
Async XLA Ops:
  2.5 9.7 %collective-permute-start = (s16[1040,128]{1,0:T(8,128)(2,1)S(1)}, s16[1040,128]{1,0:T(8,128)(2,1)S(1)}, u32[]{:S(2)}, u32[]{:S(2)}) collective-permute-start(s16[1040,128]{1,0:T(8,128)(2,1)S(1)} %get-tuple-element.14.after), channel_id=1, source_target_pairs={{0,2},{2,0},{1,3},{3,1},{4,6},{6,4},{5,7},{7,5},{8,10},{10,8},{9,1... | collective-permute-start | bytes 798728 | tf_op jit(solution)/shard_map/ppermute | solution.py:34
  6.9 10.6 %collective-permute-start.1 = (s16[1040,128]{1,0:T(8,128)(2,1)S(1)}, s16[1040,128]{1,0:T(8,128)(2,1)S(1)}, u32[]{:S(2)}, u32[]{:S(2)}) collective-permute-start(s16[1040,128]{1,0:T(8,128)(2,1)S(1)} %shard_map.74.after), channel_id=1, source_target_pairs={{0,4},{4,0},{8,12},{12,8},{1,5},{5,1},{9,13},{13,9},{2,6},{6,2},{1... | collective-permute-start | bytes 798728 | tf_op jit(solution)/shard_map/ppermute | solution.py:34
  12.4 7.6 %collective-permute-start.3 = (s16[1040,128]{1,0:T(8,128)(2,1)S(1)}, s16[1040,128]{1,0:T(8,128)(2,1)S(1)}, u32[]{:S(2)}, u32[]{:S(2)}) collective-permute-start(s16[1040,128]{1,0:T(8,128)(2,1)S(1)} %shard_map.80), channel_id=1, source_target_pairs={{0,2},{2,0},{1,3},{3,1},{4,6},{6,4},{5,7},{7,5},{8,10},{10,8},{9,1... | collective-permute-start | bytes 798728 | tf_op jit(solution)/shard_map/ppermute | solution.py:34
  14.2 7.0 %collective-permute-start.2 = (s16[1040,128]{1,0:T(8,128)(2,1)S(1)}, s16[1040,128]{1,0:T(8,128)(2,1)S(1)}, u32[]{:S(2)}, u32[]{:S(2)}) collective-permute-start(s16[1040,128]{1,0:T(8,128)(2,1)S(1)} %shard_map.77.after.refs_1_), channel_id=1, source_target_pairs={{0,4},{4,0},{8,12},{12,8},{1,5},{5,1},{9,13},{13,9},{2,6},{6,2},{1... | collective-permute-start | bytes 798728 | tf_op jit(solution)/shard_map/ppermute | solution.py:34
  17.6 9.0 %copy-start.2 = (bf16[16]{0:T(256)(128)(2,1)S(1)}, bf16[16]{0:T(256)(128)(2,1)}, u32[]{:S(2)}) copy-start(bf16[16]{0:T(256)(128)(2,1)} %param.13) | copy-start | bytes 100
  21.4 14.5 %copy-start.1 = (s32[8,128]{1,0:T(8,128)S(1)}, s32[8,128]{1,0:T(8,128)}, u32[]{:S(2)}) copy-start(s32[8,128]{1,0:T(8,128)} %index_ref.1) | copy-start | bytes 12292
  21.5 11.5 %collective-permute-start.5 = (s16[1040,128]{1,0:T(8,128)(2,1)S(1)}, s16[1040,128]{1,0:T(8,128)(2,1)S(1)}, u32[]{:S(2)}, u32[]{:S(2)}) collective-permute-start(s16[1040,128]{1,0:T(8,128)(2,1)S(1)} %shard_map.83.after), channel_id=1, source_target_pairs={{0,4},{4,0},{8,12},{12,8},{1,5},{5,1},{9,13},{13,9},{2,6},{6,2},{1... | collective-permute-start | bytes 798728 | tf_op jit(solution)/shard_map/ppermute | solution.py:34
  23.2 12.7 %collective-permute-start.4 = (s16[1040,128]{1,0:T(8,128)(2,1)S(1)}, s16[1040,128]{1,0:T(8,128)(2,1)S(1)}, u32[]{:S(2)}, u32[]{:S(2)}) collective-permute-start(s16[1040,128]{1,0:T(8,128)(2,1)S(1)} %shard_map.81.after), channel_id=1, source_target_pairs={{0,8},{4,12},{8,0},{12,4},{1,9},{5,13},{9,1},{13,5},{2,10},{6,14},... | collective-permute-start | bytes 798728 | tf_op jit(solution)/shard_map/ppermute | solution.py:34
  25.8 11.0 %collective-permute-start.6 = (s16[1040,128]{1,0:T(8,128)(2,1)S(1)}, s16[1040,128]{1,0:T(8,128)(2,1)S(1)}, u32[]{:S(2)}, u32[]{:S(2)}) collective-permute-start(s16[1040,128]{1,0:T(8,128)(2,1)S(1)} %shard_map.79.after), channel_id=1, source_target_pairs={{0,2},{2,0},{1,3},{3,1},{4,6},{6,4},{5,7},{7,5},{8,10},{10,8},{9,1... | collective-permute-start | bytes 798728 | tf_op jit(solution)/shard_map/ppermute | solution.py:34
  26.6 10.2 %copy-start = (bf16[8,128,128]{2,1,0:T(8,128)(2,1)S(1)}, bf16[8,128,128]{2,1,0:T(8,128)(2,1)}, u32[]{:S(2)}) copy-start(bf16[8,128,128]{2,1,0:T(8,128)(2,1)} %sinogram_ref.1) | copy-start | bytes 786436
  37.0 10.2 %collective-permute-start.8 = (bf16[8,128,128]{2,1,0:T(8,128)(2,1)S(1)}, bf16[8,128,128]{2,1,0:T(8,128)(2,1)S(1)}, u32[]{:S(2)}, u32[]{:S(2)}) collective-permute-start(bf16[8,128,128]{2,1,0:T(8,128)(2,1)S(1)} %shard_map.88.refs_2_), channel_id=1, source_target_pairs={{0,8},{4,12},{8,0},{12,4},{1,9},{5,13},{9,1},{13,5},{2,10},{6,14},... | collective-permute-start | bytes 786440 | tf_op jit(solution)/shard_map/ppermute | solution.py:34
  37.0 12.9 %collective-permute-start.7 = (bf16[8,128,128]{2,1,0:T(8,128)(2,1)S(1)}, bf16[8,128,128]{2,1,0:T(8,128)(2,1)S(1)}, u32[]{:S(2)}, u32[]{:S(2)}) collective-permute-start(bf16[8,128,128]{2,1,0:T(8,128)(2,1)S(1)} %shard_map.88.refs_2_), channel_id=1, source_target_pairs={{0,4},{4,0},{8,12},{12,8},{1,5},{5,1},{9,13},{13,9},{2,6},{6,2},{1... | collective-permute-start | bytes 786440 | tf_op jit(solution)/shard_map/ppermute | solution.py:34
  42.7 8.6 %collective-permute-start.9 = (bf16[8,128,128]{2,1,0:T(8,128)(2,1)S(1)}, bf16[8,128,128]{2,1,0:T(8,128)(2,1)S(1)}, u32[]{:S(2)}, u32[]{:S(2)}) collective-permute-start(bf16[8,128,128]{2,1,0:T(8,128)(2,1)S(1)} %shard_map.88.refs_2_), channel_id=1, source_target_pairs={{0,2},{2,0},{1,3},{3,1},{4,6},{6,4},{5,7},{7,5},{8,10},{10,8},{9,1... | collective-permute-start | bytes 786440 | tf_op jit(solution)/shard_map/ppermute | solution.py:34
  47.2 7.6 %collective-permute-start.10 = (bf16[8,128,128]{2,1,0:T(8,128)(2,1)S(1)}, bf16[8,128,128]{2,1,0:T(8,128)(2,1)S(1)}, u32[]{:S(2)}, u32[]{:S(2)}) collective-permute-start(bf16[8,128,128]{2,1,0:T(8,128)(2,1)S(1)} %collective-permute-done.8.refs_4_), channel_id=1, source_target_pairs={{0,4},{4,0},{8,12},{12,8},{1,5},{5,1},{9,13},{13,9},{2,6},{6,2},{1... | collective-permute-start | bytes 786440 | tf_op jit(solution)/shard_map/ppermute | solution.py:34
  47.2 8.9 %collective-permute-start.11 = (bf16[8,128,128]{2,1,0:T(8,128)(2,1)S(1)}, bf16[8,128,128]{2,1,0:T(8,128)(2,1)S(1)}, u32[]{:S(2)}, u32[]{:S(2)}) collective-permute-start(bf16[8,128,128]{2,1,0:T(8,128)(2,1)S(1)} %collective-permute-done.8.refs_4_), channel_id=1, source_target_pairs={{0,2},{2,0},{1,3},{3,1},{4,6},{6,4},{5,7},{7,5},{8,10},{10,8},{9,1... | collective-permute-start | bytes 786440 | tf_op jit(solution)/shard_map/ppermute | solution.py:34
  54.8 6.4 %collective-permute-start.13 = (bf16[8,128,128]{2,1,0:T(8,128)(2,1)S(1)}, bf16[8,128,128]{2,1,0:T(8,128)(2,1)S(1)}, u32[]{:S(2)}, u32[]{:S(2)}) collective-permute-start(bf16[8,128,128]{2,1,0:T(8,128)(2,1)S(1)} %shard_map.93), channel_id=1, source_target_pairs={{0,4},{4,0},{8,12},{12,8},{1,5},{5,1},{9,13},{13,9},{2,6},{6,2},{1... | collective-permute-start | bytes 786440 | tf_op jit(solution)/shard_map/ppermute | solution.py:34
  54.8 6.4 %collective-permute-start.12 = (bf16[8,128,128]{2,1,0:T(8,128)(2,1)S(1)}, bf16[8,128,128]{2,1,0:T(8,128)(2,1)S(1)}, u32[]{:S(2)}, u32[]{:S(2)}) collective-permute-start(bf16[8,128,128]{2,1,0:T(8,128)(2,1)S(1)} %shard_map.91.refs_3_.refs_1_), channel_id=1, source_target_pairs={{0,2},{2,0},{1,3},{3,1},{4,6},{6,4},{5,7},{7,5},{8,10},{10,8},{9,1... | collective-permute-start | bytes 786440 | tf_op jit(solution)/shard_map/ppermute | solution.py:34

commit v7 on v5

--- a/solution.py
+++ b/solution.py
@@ -388,8 +388,14 @@
                 total[place[g]] += part[:, g * cols : (g + 1) * cols]
 
     if finish:
+        stage, sems = rest[len(lows) + 5 : len(lows) + 7]
+        copies = []
         for q in range(patch_tiles):
-            out_ref[q] = volume_ref[q].astype(jnp.float32) + (total[q] / column_ref[q]).T
+            stage[q] = volume_ref[q].astype(jnp.float32) + (total[q] / column_ref[q]).T
+            copies.append(pltpu.make_async_copy(stage.at[q], out_ref.at[q], sems.at[q]))
+            copies[-1].start()
+        for copy in copies:
+            copy.wait()
 
 
 def spread(table, projector, all_cells, lows, chunks, patch_tiles, before, last=()):
@@ -411,9 +417,18 @@
     return pl.pallas_call(
         kernel,
         in_specs=[VMEM] * (2 + len(more)),
-        out_specs=VMEM,
+        out_specs=HBM if finish else VMEM,
         out_shape=jax.ShapeDtypeStruct((patch_tiles, cols, slices) if finish else shape, jnp.float32),
-        scratch_shapes=scratch + ([pltpu.VMEM(shape, jnp.float32)] if finish else []),
+        scratch_shapes=scratch
+        + (
+            [
+                pltpu.VMEM((patch_tiles, cols, slices), jnp.float32),
+                pltpu.SemaphoreType.DMA((patch_tiles,)),
+                pltpu.VMEM(shape, jnp.float32),
+            ]
+            if finish
+            else []
+        ),
         compiler_params=PARAMS,
         cost_estimate=QUICK,
     )(table, projector, *more)

time: 64.5 us -> 64 us (level)
  starting transfers between devices: 23.9 us -> 21.8 us
  waiting for transfers between devices: 22.1 us -> 22.9 us
    ppermute x14, starting transfers between devices: 23.9 us -> 21.8 us  [swap(): return lax.ppermute(value, axis, [(i, i ^ bits) for i in range(size)])]
    ppermute x14, waiting for transfers between devices: 22.1 us -> 22.9 us  [swap(): return lax.ppermute(value, axis, [(i, i ^ bits) for i in range(size)])]
  transfers between devices with their start and end apart: 14 -> 14, of which waited for: 10 -> 11; matrix products, arithmetic and copies ran while one was open for 0% -> 0% of each run, Pallas kernels for 19% -> 21%
where the time goes in v7:
time: 64 us; the launch traced here: 63.5 us
  waiting for transfers between devices  22.9 us (36%)
  starting transfers between devices  21.8 us (34%)
  Pallas kernels  18.7 us (29%)
    ppermute x14, waiting for transfers between devices, swap(): return lax.ppermute(value, axis, [(i, i ^ bits) for i in range(size)])  22.9 us
    ppermute x14, starting transfers between devices, swap(): return lax.ppermute(value, axis, [(i, i ^ bits) for i in range(size)])  21.8 us
    pallas_call x3, Pallas kernels, spread(): pl.pallas_call(kernel, in_specs=[VMEM] * (2 + len(more)), out_specs=HBM i...  6.96 us
    pallas_call x3, Pallas kernels, further_sums(): pl.pallas_call(functools.partial(further_kernel, tiles, sent, ranges), in...  5.57 us
    pallas_call x1, Pallas kernels, first_send(): pl.pallas_call(functools.partial(first_kernel, sizes, low), in_specs=[HBM...  2.69 us
    pallas_call x1, Pallas kernels, column_sums(): pl.pallas_call(column_kernel, in_specs=[SMEM, VMEM, ANY], out_specs=VMEM,...  1.78 us
  transfers between devices with their start and end apart: 14, of which 11 were waited for; matrix products, arithmetic and copies ran while one was open for 0% of the time, Pallas kernels for 21%

profile of v7, /device:TPU:0, one launch (start us, length us, event | category | flops | bytes accessed | tf_op | source)
XLA Modules:
  0.0 63.5 jit_solution(10095919840556863580)
XLA Ops:
  0.0 2.7 %shard_map.73 = (s16[1040,128]{1,0:T(8,128)(2,1)S(1)}, bf16[32,4,128,128]{3,2,1,0:T(8,128)(2,1)S(1)}, bf16[6,128,128]{2,1,0:T(8,128)(2,1)S(1)}, s32[12,32]{1,0:T(8,128)S(1)}) custom-call(s32[32]{0:T(128)} %ray_hbm.1, s32[4,32]{1,0:T(4,128)} %bitcast.1, bf16[32,4,128,128]{3,2,1,0:T(8,128)(2,1)} %projector_hbm.1, bf16[6,128,128]{2,1,0:T(8,128)(2,1)} %volume_hbm.1), custom_call_target="tpu_custom_call" | custom-call | flops 1 | bytes 1 | tf_op jit(solution)/shard_map/pallas_call | solution.py:175
  2.7 2.8 %collective-permute-start = (s16[1040,128]{1,0:T(8,128)(2,1)S(1)}, s16[1040,128]{1,0:T(8,128)(2,1)S(1)}, u32[]{:S(2)}, u32[]{:S(2)}) collective-permute-start(s16[1040,128]{1,0:T(8,128)(2,1)S(1)} %get-tuple-element.14.after), channel_id=1, source_target_pairs={{0,2},{2,0},{1,3},{3,1},{4,6},{6,4},{5,7},{7,5},{8,10},{10,8},{9,1... | collective-permute-start | bytes 798728 | tf_op jit(solution)/shard_map/ppermute | solution.py:34
  5.5 1.1 %shard_map.74.after = s16[1040,128]{1,0:T(8,128)(2,1)S(1)} custom-call(s32[12,32]{1,0:T(8,128)S(1)} %get-tuple-element.11.table_from.table_ref.refs_0_, bf16[32,4,128,128]{3,2,1,0:T(8,128)(2,1)S(1)} %get-tuple-element.12.projector_ref.refs_1_, bf16[6,128,128]{2,1,0:T(8,128)(2,1)S(1)} %get-tuple-element.13.volume_ref.rest_1_, ...), custom_call_target="tpu_custom_call" | custom-call | flops 1 | bytes 1 | tf_op jit(solution)/shard_map/pallas_call | solution.py:233
  6.6 2.5 %collective-permute-start.1 = (s16[1040,128]{1,0:T(8,128)(2,1)S(1)}, s16[1040,128]{1,0:T(8,128)(2,1)S(1)}, u32[]{:S(2)}, u32[]{:S(2)}) collective-permute-start(s16[1040,128]{1,0:T(8,128)(2,1)S(1)} %shard_map.74.after), channel_id=1, source_target_pairs={{0,4},{4,0},{8,12},{12,8},{1,5},{5,1},{9,13},{13,9},{2,6},{6,2},{1... | collective-permute-start | bytes 798728 | tf_op jit(solution)/shard_map/ppermute | solution.py:34
  9.2 2.1 %shard_map.75 = (s16[1040,128]{1,0:T(8,128)(2,1)S(1)}, f32[17,128,128]{2,1,0:T(8,128)S(1)}) custom-call(s32[12,32]{1,0:T(8,128)S(1)} %get-tuple-element.11.table_from.table_ref.refs_0_, bf16[32,4,128,128]{3,2,1,0:T(8,128)(2,1)S(1)} %get-tuple-element.12.projector_ref.refs_1_, bf16[6,128,128]{2,1,0:T(8,128)(2,1)S(1)} %get-tuple-element.13.volume_ref.rest_1_, ...), custom_call_target="tpu_custom_call" | custom-call | flops 1 | bytes 1 | tf_op jit(solution)/shard_map/pallas_call | solution.py:233
  11.2 0.6 %collective-permute-done.refs_0_ = s16[1040,128]{1,0:T(8,128)(2,1)S(1)} collective-permute-done((s16[1040,128]{1,0:T(8,128)(2,1)S(1)}, s16[1040,128]{1,0:T(8,128)(2,1)S(1)}, u32[]{:S(2)}, u32[]{:S(2)}) %collective-permute-start) | collective-permute-done | bytes 266272 | tf_op jit(solution)/shard_map/ppermute | solution.py:34
  11.9 0.2 shard_map.77.after.refs_1_
  12.1 1.8 %collective-permute-start.3 = (s16[1040,128]{1,0:T(8,128)(2,1)S(1)}, s16[1040,128]{1,0:T(8,128)(2,1)S(1)}, u32[]{:S(2)}, u32[]{:S(2)}) collective-permute-start(s16[1040,128]{1,0:T(8,128)(2,1)S(1)} %shard_map.80), channel_id=1, source_target_pairs={{0,2},{2,0},{1,3},{3,1},{4,6},{6,4},{5,7},{7,5},{8,10},{10,8},{9,1... | collective-permute-start | bytes 798728 | tf_op jit(solution)/shard_map/ppermute | solution.py:34
  13.9 1.8 %collective-permute-start.2 = (s16[1040,128]{1,0:T(8,128)(2,1)S(1)}, s16[1040,128]{1,0:T(8,128)(2,1)S(1)}, u32[]{:S(2)}, u32[]{:S(2)}) collective-permute-start(s16[1040,128]{1,0:T(8,128)(2,1)S(1)} %shard_map.77.after.refs_1_), channel_id=1, source_target_pairs={{0,4},{4,0},{8,12},{12,8},{1,5},{5,1},{9,13},{13,9},{2,6},{6,2},{1... | collective-permute-start | bytes 798728 | tf_op jit(solution)/shard_map/ppermute | solution.py:34
  15.7 2.4 %shard_map.78.own_ref = f32[25,128,128]{2,1,0:T(8,128)S(1)} custom-call(s32[12,32]{1,0:T(8,128)S(1)} %get-tuple-element.11.table_from.table_ref.refs_0_, bf16[32,4,128,128]{3,2,1,0:T(8,128)(2,1)S(1)} %get-tuple-element.12.projector_ref.refs_1_, bf16[6,128,128]{2,1,0:T(8,128)(2,1)S(1)} %get-tuple-element.13.volume_ref.rest_1_, ...), custom_call_target="tpu_custom_call" | custom-call | flops 1 | bytes 1 | tf_op jit(solution)/shard_map/pallas_call | solution.py:233
  18.0 0.0 copy-start.2
  18.1 0.0 collective-permute-done.1.rest_0_
  18.1 0.2 shard_map.79.after
  18.2 1.5 %collective-permute-done.3.rest_1_ = s16[1040,128]{1,0:T(8,128)(2,1)S(1)} collective-permute-done((s16[1040,128]{1,0:T(8,128)(2,1)S(1)}, s16[1040,128]{1,0:T(8,128)(2,1)S(1)}, u32[]{:S(2)}, u32[]{:S(2)}) %collective-permute-start.3) | collective-permute-done | bytes 266272 | tf_op jit(solution)/shard_map/ppermute | solution.py:34
  19.7 1.3 %collective-permute-done.2.rest_0_ = s16[1040,128]{1,0:T(8,128)(2,1)S(1)} collective-permute-done((s16[1040,128]{1,0:T(8,128)(2,1)S(1)}, s16[1040,128]{1,0:T(8,128)(2,1)S(1)}, u32[]{:S(2)}, u32[]{:S(2)}) %collective-permute-start.2) | collective-permute-done | bytes 266272 | tf_op jit(solution)/shard_map/ppermute | solution.py:34
  21.0 0.2 shard_map.81.after
  21.2 0.0 copy-start.1
  21.2 0.1 shard_map.83.after
  21.3 1.8 %collective-permute-start.5 = (s16[1040,128]{1,0:T(8,128)(2,1)S(1)}, s16[1040,128]{1,0:T(8,128)(2,1)S(1)}, u32[]{:S(2)}, u32[]{:S(2)}) collective-permute-start(s16[1040,128]{1,0:T(8,128)(2,1)S(1)} %shard_map.83.after), channel_id=1, source_target_pairs={{0,4},{4,0},{8,12},{12,8},{1,5},{5,1},{9,13},{13,9},{2,6},{6,2},{1... | collective-permute-start | bytes 798728 | tf_op jit(solution)/shard_map/ppermute | solution.py:34
  23.2 2.8 %collective-permute-start.4 = (s16[1040,128]{1,0:T(8,128)(2,1)S(1)}, s16[1040,128]{1,0:T(8,128)(2,1)S(1)}, u32[]{:S(2)}, u32[]{:S(2)}) collective-permute-start(s16[1040,128]{1,0:T(8,128)(2,1)S(1)} %shard_map.81.after), channel_id=1, source_target_pairs={{0,8},{4,12},{8,0},{12,4},{1,9},{5,13},{9,1},{13,5},{2,10},{6,14},... | collective-permute-start | bytes 798728 | tf_op jit(solution)/shard_map/ppermute | solution.py:34
  26.0 0.4 collective-permute-start.6
  26.3 0.0 copy-done.2
  26.3 0.0 copy-start
  26.3 1.8 %shard_map.86.after.rest_2_ = f32[6,1,128]{2,1,0:T(1,128)S(1)} custom-call(s32[12,32]{1,0:T(8,128)S(1)} %get-tuple-element.11.table_from.table_ref.refs_0_, bf16[32,4,128,128]{3,2,1,0:T(8,128)(2,1)S(1)} %get-tuple-element.12.projector_ref.refs_1_, s16[1040,128]{1,0:T(8,128)(2,1)S(1)} %shard_map.83.after), custom_call_target="tpu_custom_call" | custom-call | flops 1 | bytes 1 | tf_op jit(solution)/shard_map/pallas_call | solution.py:343
  28.1 5.0 %collective-permute-done.5.refs_0_ = s16[1040,128]{1,0:T(8,128)(2,1)S(1)} collective-permute-done((s16[1040,128]{1,0:T(8,128)(2,1)S(1)}, s16[1040,128]{1,0:T(8,128)(2,1)S(1)}, u32[]{:S(2)}, u32[]{:S(2)}) %collective-permute-start.5) | collective-permute-done | bytes 266272 | tf_op jit(solution)/shard_map/ppermute | solution.py:34
  33.1 2.8 %collective-permute-done.4.refs_0_ = s16[1040,128]{1,0:T(8,128)(2,1)S(1)} collective-permute-done((s16[1040,128]{1,0:T(8,128)(2,1)S(1)}, s16[1040,128]{1,0:T(8,128)(2,1)S(1)}, u32[]{:S(2)}, u32[]{:S(2)}) %collective-permute-start.4) | collective-permute-done | bytes 266272 | tf_op jit(solution)/shard_map/ppermute | solution.py:34
  35.9 0.0 copy-done.1
  35.9 0.7 %shard_map.87.weight_ref = bf16[8,128,128]{2,1,0:T(8,128)(2,1)S(1)} custom-call(f32[16]{0:T(128)S(1)} %convert_element_type.3.table_ref, s32[8,128]{1,0:T(8,128)S(1)} %copy-done.1, f32[6,1,128]{2,1,0:T(1,128)S(1)} %shard_map.86.after.rest_2_), custom_call_target="tpu_custom_call" | custom-call | flops 1 | bytes 1 | tf_op jit(solution)/shard_map/pallas_call | solution.py:297
  36.6 0.1 shard_map.85.sum_ref
  36.7 0.0 collective-permute-done.6.rest_0_
  36.7 0.0 copy-done
  36.7 0.2 shard_map.88.refs_2_
  36.9 0.1 collective-permute-start.8
  37.0 5.9 %collective-permute-start.7 = (bf16[8,128,128]{2,1,0:T(8,128)(2,1)S(1)}, bf16[8,128,128]{2,1,0:T(8,128)(2,1)S(1)}, u32[]{:S(2)}, u32[]{:S(2)}) collective-permute-start(bf16[8,128,128]{2,1,0:T(8,128)(2,1)S(1)} %shard_map.88.refs_2_), channel_id=1, source_target_pairs={{0,4},{4,0},{8,12},{12,8},{1,5},{5,1},{9,13},{13,9},{2,6},{6,2},{1... | collective-permute-start | bytes 786440 | tf_op jit(solution)/shard_map/ppermute | solution.py:34
  42.9 0.0 collective-permute-start.9
  42.9 4.3 %collective-permute-done.8.refs_4_ = bf16[8,128,128]{2,1,0:T(8,128)(2,1)S(1)} collective-permute-done((bf16[8,128,128]{2,1,0:T(8,128)(2,1)S(1)}, bf16[8,128,128]{2,1,0:T(8,128)(2,1)S(1)}, u32[]{:S(2)}, u32[]{:S(2)}) %collective-permute-start.8) | collective-permute-done | bytes 262176 | tf_op jit(solution)/shard_map/ppermute | solution.py:34
  47.2 0.2 collective-permute-start.10
  47.3 1.1 %collective-permute-start.11 = (bf16[8,128,128]{2,1,0:T(8,128)(2,1)S(1)}, bf16[8,128,128]{2,1,0:T(8,128)(2,1)S(1)}, u32[]{:S(2)}, u32[]{:S(2)}) collective-permute-start(bf16[8,128,128]{2,1,0:T(8,128)(2,1)S(1)} %collective-permute-done.8.refs_4_), channel_id=1, source_target_pairs={{0,2},{2,0},{1,3},{3,1},{4,6},{6,4},{5,7},{7,5},{8,10},{10,8},{9,1... | collective-permute-start | bytes 786440 | tf_op jit(solution)/shard_map/ppermute | solution.py:34
  48.4 1.5 %collective-permute-done.7.refs_0_ = bf16[8,128,128]{2,1,0:T(8,128)(2,1)S(1)} collective-permute-done((bf16[8,128,128]{2,1,0:T(8,128)(2,1)S(1)}, bf16[8,128,128]{2,1,0:T(8,128)(2,1)S(1)}, u32[]{:S(2)}, u32[]{:S(2)}) %collective-permute-start.7) | collective-permute-done | bytes 262176 | tf_op jit(solution)/shard_map/ppermute | solution.py:34
  49.9 0.8 %collective-permute-done.9.refs_5_.refs_0_ = bf16[8,128,128]{2,1,0:T(8,128)(2,1)S(1)} collective-permute-done((bf16[8,128,128]{2,1,0:T(8,128)(2,1)S(1)}, bf16[8,128,128]{2,1,0:T(8,128)(2,1)S(1)}, u32[]{:S(2)}, u32[]{:S(2)}) %collective-permute-start.9) | collective-permute-done | bytes 262176 | tf_op jit(solution)/shard_map/ppermute | solution.py:34
  50.7 3.0 %shard_map.90.refs_1_.refs_2_ = f32[7,128,128]{2,1,0:T(8,128)S(1)} custom-call(s32[12,32]{1,0:T(8,128)S(1)} %get-tuple-element.11.table_from.table_ref.refs_0_, bf16[32,4,128,128]{3,2,1,0:T(8,128)(2,1)S(1)} %get-tuple-element.12.projector_ref.refs_1_, bf16[8,128,128]{2,1,0:T(8,128)(2,1)S(1)} %shard_map.88.refs_2_, ...), custom_call_target="tpu_custom_call" | custom-call | flops 1 | bytes 1 | tf_op jit(solution)/shard_map/pallas_call | solution.py:417
  53.7 1.0 %collective-permute-done.10.refs_0_ = bf16[8,128,128]{2,1,0:T(8,128)(2,1)S(1)} collective-permute-done((bf16[8,128,128]{2,1,0:T(8,128)(2,1)S(1)}, bf16[8,128,128]{2,1,0:T(8,128)(2,1)S(1)}, u32[]{:S(2)}, u32[]{:S(2)}) %collective-permute-start.10) | collective-permute-done | bytes 262176 | tf_op jit(solution)/shard_map/ppermute | solution.py:34
  54.7 0.0 collective-permute-start.13
  54.7 0.7 %collective-permute-start.12 = (bf16[8,128,128]{2,1,0:T(8,128)(2,1)S(1)}, bf16[8,128,128]{2,1,0:T(8,128)(2,1)S(1)}, u32[]{:S(2)}, u32[]{:S(2)}) collective-permute-start(bf16[8,128,128]{2,1,0:T(8,128)(2,1)S(1)} %shard_map.91.refs_3_.refs_1_), channel_id=1, source_target_pairs={{0,2},{2,0},{1,3},{3,1},{4,6},{6,4},{5,7},{7,5},{8,10},{10,8},{9,1... | collective-permute-start | bytes 786440 | tf_op jit(solution)/shard_map/ppermute | solution.py:34
  55.4 0.5 collective-permute-done.11.refs_4_
  55.8 1.5 %shard_map.92.rest_0_ = f32[7,128,128]{2,1,0:T(8,128)S(1)} custom-call(s32[12,32]{1,0:T(8,128)S(1)} %get-tuple-element.11.table_from.table_ref.refs_0_, bf16[32,4,128,128]{3,2,1,0:T(8,128)(2,1)S(1)} %get-tuple-element.12.projector_ref.refs_1_, f32[7,128,128]{2,1,0:T(8,128)S(1)} %shard_map.90.refs_1_.refs_2_, ...), custom_call_target="tpu_custom_call" | custom-call | flops 1 | bytes 1 | tf_op jit(solution)/shard_map/pallas_call | solution.py:417
  57.4 3.7 %collective-permute-done.13.rest_4_ = bf16[8,128,128]{2,1,0:T(8,128)(2,1)S(1)} collective-permute-done((bf16[8,128,128]{2,1,0:T(8,128)(2,1)S(1)}, bf16[8,128,128]{2,1,0:T(8,128)(2,1)S(1)}, u32[]{:S(2)}, u32[]{:S(2)}) %collective-permute-start.13) | collective-permute-done | bytes 262176 | tf_op jit(solution)/shard_map/ppermute | solution.py:34
  61.1 0.0 collective-permute-done.12.rest_3_
  61.1 2.4 %shard_map.94 = f32[6,128,128]{2,1,0:T(8,128)} custom-call(s32[12,32]{1,0:T(8,128)S(1)} %get-tuple-element.11.table_from.table_ref.refs_0_, bf16[32,4,128,128]{3,2,1,0:T(8,128)(2,1)S(1)} %get-tuple-element.12.projector_ref.refs_1_, f32[7,128,128]{2,1,0:T(8,128)S(1)} %shard_map.92.rest_0_, bf16[6,128,128]{2,1,0:T(8,128)(2,1)S(1)} %get-tuple-element.13.volume_ref.rest_1_, ...), custom_call_target="tpu_custom_call" | custom-call | flops 1 | bytes 1 | tf_op jit(solution)/shard_map/pallas_call | solution.py:417
  (8 shorter events, 0.0 us)
Async XLA Ops:
  2.7 9.2 %collective-permute-start = (s16[1040,128]{1,0:T(8,128)(2,1)S(1)}, s16[1040,128]{1,0:T(8,128)(2,1)S(1)}, u32[]{:S(2)}, u32[]{:S(2)}) collective-permute-start(s16[1040,128]{1,0:T(8,128)(2,1)S(1)} %get-tuple-element.14.after), channel_id=1, source_target_pairs={{0,2},{2,0},{1,3},{3,1},{4,6},{6,4},{5,7},{7,5},{8,10},{10,8},{9,1... | collective-permute-start | bytes 798728 | tf_op jit(solution)/shard_map/ppermute | solution.py:34
  6.6 11.4 %collective-permute-start.1 = (s16[1040,128]{1,0:T(8,128)(2,1)S(1)}, s16[1040,128]{1,0:T(8,128)(2,1)S(1)}, u32[]{:S(2)}, u32[]{:S(2)}) collective-permute-start(s16[1040,128]{1,0:T(8,128)(2,1)S(1)} %shard_map.74.after), channel_id=1, source_target_pairs={{0,4},{4,0},{8,12},{12,8},{1,5},{5,1},{9,13},{13,9},{2,6},{6,2},{1... | collective-permute-start | bytes 798728 | tf_op jit(solution)/shard_map/ppermute | solution.py:34
  12.1 7.6 %collective-permute-start.3 = (s16[1040,128]{1,0:T(8,128)(2,1)S(1)}, s16[1040,128]{1,0:T(8,128)(2,1)S(1)}, u32[]{:S(2)}, u32[]{:S(2)}) collective-permute-start(s16[1040,128]{1,0:T(8,128)(2,1)S(1)} %shard_map.80), channel_id=1, source_target_pairs={{0,2},{2,0},{1,3},{3,1},{4,6},{6,4},{5,7},{7,5},{8,10},{10,8},{9,1... | collective-permute-start | bytes 798728 | tf_op jit(solution)/shard_map/ppermute | solution.py:34
  13.9 7.1 %collective-permute-start.2 = (s16[1040,128]{1,0:T(8,128)(2,1)S(1)}, s16[1040,128]{1,0:T(8,128)(2,1)S(1)}, u32[]{:S(2)}, u32[]{:S(2)}) collective-permute-start(s16[1040,128]{1,0:T(8,128)(2,1)S(1)} %shard_map.77.after.refs_1_), channel_id=1, source_target_pairs={{0,4},{4,0},{8,12},{12,8},{1,5},{5,1},{9,13},{13,9},{2,6},{6,2},{1... | collective-permute-start | bytes 798728 | tf_op jit(solution)/shard_map/ppermute | solution.py:34
  18.0 8.3 %copy-start.2 = (bf16[16]{0:T(256)(128)(2,1)S(1)}, bf16[16]{0:T(256)(128)(2,1)}, u32[]{:S(2)}) copy-start(bf16[16]{0:T(256)(128)(2,1)} %param.13) | copy-start | bytes 100
  21.2 14.7 %copy-start.1 = (s32[8,128]{1,0:T(8,128)S(1)}, s32[8,128]{1,0:T(8,128)}, u32[]{:S(2)}) copy-start(s32[8,128]{1,0:T(8,128)} %index_ref.1) | copy-start | bytes 12292
  21.3 11.8 %collective-permute-start.5 = (s16[1040,128]{1,0:T(8,128)(2,1)S(1)}, s16[1040,128]{1,0:T(8,128)(2,1)S(1)}, u32[]{:S(2)}, u32[]{:S(2)}) collective-permute-start(s16[1040,128]{1,0:T(8,128)(2,1)S(1)} %shard_map.83.after), channel_id=1, source_target_pairs={{0,4},{4,0},{8,12},{12,8},{1,5},{5,1},{9,13},{13,9},{2,6},{6,2},{1... | collective-permute-start | bytes 798728 | tf_op jit(solution)/shard_map/ppermute | solution.py:34
  23.2 12.7 %collective-permute-start.4 = (s16[1040,128]{1,0:T(8,128)(2,1)S(1)}, s16[1040,128]{1,0:T(8,128)(2,1)S(1)}, u32[]{:S(2)}, u32[]{:S(2)}) collective-permute-start(s16[1040,128]{1,0:T(8,128)(2,1)S(1)} %shard_map.81.after), channel_id=1, source_target_pairs={{0,8},{4,12},{8,0},{12,4},{1,9},{5,13},{9,1},{13,5},{2,10},{6,14},... | collective-permute-start | bytes 798728 | tf_op jit(solution)/shard_map/ppermute | solution.py:34
  26.0 10.8 %collective-permute-start.6 = (s16[1040,128]{1,0:T(8,128)(2,1)S(1)}, s16[1040,128]{1,0:T(8,128)(2,1)S(1)}, u32[]{:S(2)}, u32[]{:S(2)}) collective-permute-start(s16[1040,128]{1,0:T(8,128)(2,1)S(1)} %shard_map.79.after), channel_id=1, source_target_pairs={{0,2},{2,0},{1,3},{3,1},{4,6},{6,4},{5,7},{7,5},{8,10},{10,8},{9,1... | collective-permute-start | bytes 798728 | tf_op jit(solution)/shard_map/ppermute | solution.py:34
  26.3 10.4 %copy-start = (bf16[8,128,128]{2,1,0:T(8,128)(2,1)S(1)}, bf16[8,128,128]{2,1,0:T(8,128)(2,1)}, u32[]{:S(2)}) copy-start(bf16[8,128,128]{2,1,0:T(8,128)(2,1)} %sinogram_ref.1) | copy-start | bytes 786436
  36.9 10.2 %collective-permute-start.8 = (bf16[8,128,128]{2,1,0:T(8,128)(2,1)S(1)}, bf16[8,128,128]{2,1,0:T(8,128)(2,1)S(1)}, u32[]{:S(2)}, u32[]{:S(2)}) collective-permute-start(bf16[8,128,128]{2,1,0:T(8,128)(2,1)S(1)} %shard_map.88.refs_2_), channel_id=1, source_target_pairs={{0,8},{4,12},{8,0},{12,4},{1,9},{5,13},{9,1},{13,5},{2,10},{6,14},... | collective-permute-start | bytes 786440 | tf_op jit(solution)/shard_map/ppermute | solution.py:34
  37.0 12.9 %collective-permute-start.7 = (bf16[8,128,128]{2,1,0:T(8,128)(2,1)S(1)}, bf16[8,128,128]{2,1,0:T(8,128)(2,1)S(1)}, u32[]{:S(2)}, u32[]{:S(2)}) collective-permute-start(bf16[8,128,128]{2,1,0:T(8,128)(2,1)S(1)} %shard_map.88.refs_2_), channel_id=1, source_target_pairs={{0,4},{4,0},{8,12},{12,8},{1,5},{5,1},{9,13},{13,9},{2,6},{6,2},{1... | collective-permute-start | bytes 786440 | tf_op jit(solution)/shard_map/ppermute | solution.py:34
  42.9 7.8 %collective-permute-start.9 = (bf16[8,128,128]{2,1,0:T(8,128)(2,1)S(1)}, bf16[8,128,128]{2,1,0:T(8,128)(2,1)S(1)}, u32[]{:S(2)}, u32[]{:S(2)}) collective-permute-start(bf16[8,128,128]{2,1,0:T(8,128)(2,1)S(1)} %shard_map.88.refs_2_), channel_id=1, source_target_pairs={{0,2},{2,0},{1,3},{3,1},{4,6},{6,4},{5,7},{7,5},{8,10},{10,8},{9,1... | collective-permute-start | bytes 786440 | tf_op jit(solution)/shard_map/ppermute | solution.py:34
  47.2 7.5 %collective-permute-start.10 = (bf16[8,128,128]{2,1,0:T(8,128)(2,1)S(1)}, bf16[8,128,128]{2,1,0:T(8,128)(2,1)S(1)}, u32[]{:S(2)}, u32[]{:S(2)}) collective-permute-start(bf16[8,128,128]{2,1,0:T(8,128)(2,1)S(1)} %collective-permute-done.8.refs_4_), channel_id=1, source_target_pairs={{0,4},{4,0},{8,12},{12,8},{1,5},{5,1},{9,13},{13,9},{2,6},{6,2},{1... | collective-permute-start | bytes 786440 | tf_op jit(solution)/shard_map/ppermute | solution.py:34
  47.3 8.5 %collective-permute-start.11 = (bf16[8,128,128]{2,1,0:T(8,128)(2,1)S(1)}, bf16[8,128,128]{2,1,0:T(8,128)(2,1)S(1)}, u32[]{:S(2)}, u32[]{:S(2)}) collective-permute-start(bf16[8,128,128]{2,1,0:T(8,128)(2,1)S(1)} %collective-permute-done.8.refs_4_), channel_id=1, source_target_pairs={{0,2},{2,0},{1,3},{3,1},{4,6},{6,4},{5,7},{7,5},{8,10},{10,8},{9,1... | collective-permute-start | bytes 786440 | tf_op jit(solution)/shard_map/ppermute | solution.py:34
  54.7 6.4 %collective-permute-start.13 = (bf16[8,128,128]{2,1,0:T(8,128)(2,1)S(1)}, bf16[8,128,128]{2,1,0:T(8,128)(2,1)S(1)}, u32[]{:S(2)}, u32[]{:S(2)}) collective-permute-start(bf16[8,128,128]{2,1,0:T(8,128)(2,1)S(1)} %shard_map.93), channel_id=1, source_target_pairs={{0,4},{4,0},{8,12},{12,8},{1,5},{5,1},{9,13},{13,9},{2,6},{6,2},{1... | collective-permute-start | bytes 786440 | tf_op jit(solution)/shard_map/ppermute | solution.py:34
  54.7 6.4 %collective-permute-start.12 = (bf16[8,128,128]{2,1,0:T(8,128)(2,1)S(1)}, bf16[8,128,128]{2,1,0:T(8,128)(2,1)S(1)}, u32[]{:S(2)}, u32[]{:S(2)}) collective-permute-start(bf16[8,128,128]{2,1,0:T(8,128)(2,1)S(1)} %shard_map.91.refs_3_.refs_1_), channel_id=1, source_target_pairs={{0,2},{2,0},{1,3},{3,1},{4,6},{6,4},{5,7},{7,5},{8,10},{10,8},{9,1... | collective-permute-start | bytes 786440 | tf_op jit(solution)/shard_map/ppermute | solution.py:34
